TPU v7x, 32 devices: a whole 2x2x4 slice. The times are simulated.
32 devices in a mesh: dp: 8 (over z, y), tensor: 4 (over x, core).
Axes of the slice: x: 2, y: 2, z: 4, core: 2. Of those that a mesh axis runs over, the one named last changes fastest.
Arguments:
- tokens: bfloat16 [20480, 1024], P('dp'), may hold values from -6 to 6
- cotangent: bfloat16 [20480, 1024], P('dp'), may hold values from -6 to 6
- seq_extra: int32 [4], replicated, may hold values from 1 to 112, 256 in all
- deal: int32 [320], replicated, may hold values from 0 to 319, as said below
- proj_in: bfloat16 [1024, 4, 768], P('dp', 'tensor'), may hold values from -0.1875 to 0.1875
- decay_down: bfloat16 [1024, 16], P('dp'), may hold values from -0.1875 to 0.1875
- decay_up: bfloat16 [16, 4, 128], P(None, 'tensor'), may hold values from -1.5 to 1.5
- decay_bias: float32 [4, 128], P('tensor'), may hold values from 0.5 to 9
- head_gain: float32 [256], replicated, may hold values from 0.5 to 1.5
- proj_out: bfloat16 [4, 256, 1024], P('tensor', None, 'dp'), may hold values from -0.1875 to 0.1875
- block_gains: float32 [2, 1024], replicated, may hold values from 0.5 to 1.5
- ffn_in: bfloat16 [1024, 2, 2816], P('dp', None, 'tensor'), may hold values from -0.1875 to 0.1875
- ffn_out: bfloat16 [2816, 1024], P('tensor', 'dp'), may hold values from -0.109375 to 0.109375
- first_proj_in: float32 [1024, 4, 768], P('dp', 'tensor'), may hold values from -0.078125 to 0.078125
- second_proj_in: float32 [1024, 4, 768], P('dp', 'tensor'), may hold values from 0.00013 to 0.00053
- first_decay_down: float32 [1024, 16], P('dp'), may hold values from -0.078125 to 0.078125
- second_decay_down: float32 [1024, 16], P('dp'), may hold values from 0.00013 to 0.00053
- first_decay_up: float32 [16, 4, 128], P(None, 'tensor'), may hold values from -0.078125 to 0.078125
- second_decay_up: float32 [16, 4, 128], P(None, 'tensor'), may hold values from 1.5e-05 to 6e-05
- first_decay_bias: float32 [4, 128], P('tensor'), may hold values from -0.078125 to 0.078125
- second_decay_bias: float32 [4, 128], P('tensor'), may hold values from 0.00013 to 0.00053
- first_head_gain: float32 [256], replicated, may hold values from -0.078125 to 0.078125
- second_head_gain: float32 [256], replicated, may hold values from 0.00013 to 0.00053
- first_proj_out: float32 [4, 256, 1024], P('tensor', None, 'dp'), may hold values from -0.078125 to 0.078125
- second_proj_out: float32 [4, 256, 1024], P('tensor', None, 'dp'), may hold values from 0.00013 to 0.00053
- first_block_gains: float32 [2, 1024], replicated, may hold values from -0.078125 to 0.078125
- second_block_gains: float32 [2, 1024], replicated, may hold values from 0.00013 to 0.00053
- first_ffn_in: float32 [1024, 2, 2816], P('dp', None, 'tensor'), may hold values from -0.078125 to 0.078125
- second_ffn_in: float32 [1024, 2, 2816], P('dp', None, 'tensor'), may hold values from 0.00013 to 0.00053
- first_ffn_out: float32 [2816, 1024], P('tensor', 'dp'), may hold values from -0.078125 to 0.078125
- second_ffn_out: float32 [2816, 1024], P('tensor', 'dp'), may hold values from 0.00013 to 0.00053
Outputs:
- block_out: float32 [20480, 1024], P('dp', 'tensor')
- token_grad: float32 [20480, 1024], P('dp')
- grad_norm: float32 [], replicated
- grad_proj_in: float32 [1024, 4, 768], P('dp', 'tensor')
- first_new_proj_in: float32 [1024, 4, 768], P('dp', 'tensor')
- second_new_proj_in: float32 [1024, 4, 768], P('dp', 'tensor')
- step_proj_in: float32 [1024, 4, 768], P('dp', 'tensor')
- grad_decay_down: float32 [1024, 16], P('dp')
- first_new_decay_down: float32 [1024, 16], P('dp')
- second_new_decay_down: float32 [1024, 16], P('dp')
- step_decay_down: float32 [1024, 16], P('dp')
- grad_decay_up: float32 [16, 4, 128], P(None, 'tensor')
- first_new_decay_up: float32 [16, 4, 128], P(None, 'tensor')
- second_new_decay_up: float32 [16, 4, 128], P(None, 'tensor')
- step_decay_up: float32 [16, 4, 128], P(None, 'tensor')
- grad_decay_bias: float32 [4, 128], P('tensor')
- first_new_decay_bias: float32 [4, 128], P('tensor')
- second_new_decay_bias: float32 [4, 128], P('tensor')
- step_decay_bias: float32 [4, 128], P('tensor')
- grad_head_gain: float32 [256], replicated
- first_new_head_gain: float32 [256], replicated
- second_new_head_gain: float32 [256], replicated
- step_head_gain: float32 [256], replicated
- grad_proj_out: float32 [4, 256, 1024], P('tensor', None, 'dp')
- first_new_proj_out: float32 [4, 256, 1024], P('tensor', None, 'dp')
- second_new_proj_out: float32 [4, 256, 1024], P('tensor', None, 'dp')
- step_proj_out: float32 [4, 256, 1024], P('tensor', None, 'dp')
- grad_block_gains: float32 [2, 1024], replicated
- first_new_block_gains: float32 [2, 1024], replicated
- second_new_block_gains: float32 [2, 1024], replicated
- step_block_gains: float32 [2, 1024], replicated
- grad_ffn_in: float32 [1024, 2, 2816], P('dp', None, 'tensor')
- first_new_ffn_in: float32 [1024, 2, 2816], P('dp', None, 'tensor')
- second_new_ffn_in: float32 [1024, 2, 2816], P('dp', None, 'tensor')
- step_ffn_in: float32 [1024, 2, 2816], P('dp', None, 'tensor')
- grad_ffn_out: float32 [2816, 1024], P('tensor', 'dp')
- first_new_ffn_out: float32 [2816, 1024], P('tensor', 'dp')
- second_new_ffn_out: float32 [2816, 1024], P('tensor', 'dp')
- step_ffn_out: float32 [2816, 1024], P('tensor', 'dp')
Inputs may be any that keep to these rules, and one draw needn't show every extreme that they name: Sequence i of the dealt layout holds (16 + seq_extra[i]) * 64 tokens; the sequences lie one after another and together fill all 20480 tokens; some sequence has seq_extra equal to 112. deal names every one of the 320 spans once. Span p of the dealt layout lies with index p // 40 of dp, input span deal[p] with index deal[p] // 40. Every index of dp takes exactly 5 spans from each index.
All inputs are finite; a program needn't handle non-finite values.
Results may differ from a plain program's by a relative error of at most 0.02.
Values may be sent and summed in bfloat16 or wider, within the bound.
A program may use at most 256 MiB of HBM per device.

v0:
```python
import math

import jax
import jax.numpy as jnp
from jax import lax
from jax.sharding import PartitionSpec as P

DK = 128
DV = 256
SPAN = 64
MIN_SPANS = 16
PARAMS = 12872448


norm_eps = 1e-06
highest_precision = lax.Precision.HIGHEST
learn_rate = 0.05
beta_one = 0.9
beta_two = 0.95
adam_eps = 1e-08
weight_decay = 0.1
clip_scale = 0.05
adam_step = 10
decay_scale = 16.0


def carried_in(value, axis, join, neutral):
    place = lax.axis_index(axis)
    gathered = jax.tree.map(
        lambda a, kind: lax.all_gather(a.astype(kind), axis), value, (jnp.bfloat16, jnp.bfloat16)
    )
    state = jax.tree.map(lambda a, e: jnp.zeros_like(a) + jnp.asarray(e, a.dtype), value, neutral)

    def one(step, state):
        return join(
            state,
            jax.tree.map(
                lambda a, own: lax.dynamic_index_in_dim(a, step, 0, False).astype(own.dtype),
                gathered,
                value,
            ),
        )

    return lax.fori_loop(0, place, one, state)


def carried_in_2(value, axis, join, neutral):
    count = lax.axis_size(axis)
    place = lax.axis_index(axis)
    ahead = count - 1 - place
    gathered = jax.tree.map(
        lambda a, kind: lax.all_gather(a.astype(kind), axis),
        value,
        jax.tree.map(lambda a: jnp.bfloat16 if a.dtype == jnp.float32 else a.dtype, value),
    )
    state = jax.tree.map(lambda a, e: jnp.zeros_like(a) + jnp.asarray(e, a.dtype), value, neutral)

    def one(step, state):
        source = count - 1 - step
        return join(
            state,
            jax.tree.map(
                lambda a, own: lax.dynamic_index_in_dim(a, source, 0, False).astype(own.dtype),
                gathered,
                value,
            ),
        )

    return lax.fori_loop(0, ahead, one, state)


def combine_states(earlier, later):
    return (later[0] * earlier[0], later[0][..., None] * earlier[1] + later[1])


def span_starts(seq_extra, span_ids):
    seq_spans = seq_extra + MIN_SPANS
    bounds = jnp.cumsum(seq_spans) - seq_spans
    return jnp.any(bounds[None, :] == span_ids[:, None], axis=1).astype(jnp.float32)


def deal_tables(deal, n_data, per_dev, capacity, my_index):
    table_grid = deal.reshape(n_data, per_dev)
    src_dev = table_grid // per_dev
    src_local = table_grid % per_dev
    my_source = lax.dynamic_index_in_dim(src_dev, my_index, 0, keepdims=False)
    earlier = jnp.tril(jnp.ones((per_dev, per_dev), jnp.int32), -1)
    same_source = (my_source[:, None] == my_source[None, :]).astype(jnp.int32)
    my_rank = jnp.sum(same_source * earlier, axis=1)
    recv_slot = my_source * capacity + my_rank
    owned_here = (src_dev == my_index).astype(jnp.int32)
    send_rank = jnp.cumsum(owned_here, axis=1) - owned_here
    slot_ids = jnp.arange(capacity, dtype=jnp.int32)
    send_hit = owned_here[:, :, None] * (send_rank[:, :, None] == slot_ids[None, None, :]).astype(
        jnp.int32
    )
    send_local = jnp.sum(send_hit * src_local[:, :, None], axis=1)
    peer_ids = jnp.arange(n_data, dtype=jnp.int32)
    local_ids = jnp.arange(per_dev, dtype=jnp.int32)
    back_hit = (
        (my_source[None, None, :] == peer_ids[:, None, None])
        & (my_rank[None, None, :] == slot_ids[None, :, None])
    ).astype(jnp.int32)
    back_local = jnp.sum(back_hit * local_ids[None, None, :], axis=2)
    home_hit = owned_here[:, :, None] * (src_local[:, :, None] == local_ids[None, None, :]).astype(
        jnp.int32
    )
    home_slot = jnp.sum(
        home_hit * (peer_ids[:, None, None] * capacity + send_rank[:, :, None]), axis=(0, 1)
    )
    return (recv_slot, send_local, back_local, home_slot)


def deal_send(rows, picks, per_dev):
    spans = rows.reshape((per_dev, SPAN) + rows.shape[1:])
    picked = spans[picks.reshape(-1)]
    return picked.reshape((-1,) + rows.shape[1:])


def deal_pick(received, slot_index, per_dev):
    spans = received.reshape((-1, SPAN) + received.shape[1:])
    return spans[slot_index].reshape((per_dev * SPAN,) + received.shape[1:])


def causal_mask():
    return jnp.tril(jnp.ones((SPAN, SPAN), jnp.float32))


def decay_table(running_decay):
    causal = causal_mask()[None, :, :, None, None]
    return jnp.exp(jnp.minimum(running_decay[:, :, None] - running_decay[:, None, :], 0.0)) * causal


def span_forward(inputs):
    query_rows, key_rows, value_rows, running_decay, previous_state = inputs
    decays = decay_table(running_decay)
    scores = jnp.einsum(
        "nthk,nshk,ntshk->nhts", query_rows, key_rows, decays, precision=highest_precision
    )
    within = jnp.einsum("nhts,nshv->nthv", scores, value_rows, precision=highest_precision)
    across_spans = jnp.einsum(
        "nthk,nhkv->nthv",
        query_rows * jnp.exp(running_decay),
        previous_state,
        precision=highest_precision,
    )
    return (within + across_spans,)


def span_backward(inputs):
    query_rows, key_rows, value_rows, running_decay, previous_state, grad_mix, grad_state = inputs
    decays = decay_table(running_decay)
    causal = causal_mask()
    scores = jnp.einsum(
        "nthk,nshk,ntshk->nhts", query_rows, key_rows, decays, precision=highest_precision
    )
    grad_scores = (
        jnp.einsum("nthv,nshv->nhts", grad_mix, value_rows, precision=highest_precision) * causal
    )
    final_span_state = running_decay[:, -1:]
    towards = jnp.exp(final_span_state - running_decay)
    decayed_state = key_rows * towards
    through = jnp.einsum("nshv,nhkv->nshk", value_rows, grad_state, precision=highest_precision)
    grad_query = jnp.einsum(
        "nhts,nshk,ntshk->nthk", grad_scores, key_rows, decays, precision=highest_precision
    ) + jnp.exp(running_decay) * jnp.einsum(
        "nthv,nhkv->nthk", grad_mix, previous_state, precision=highest_precision
    )
    grad_key = (
        jnp.einsum(
            "nhts,nthk,ntshk->nshk", grad_scores, query_rows, decays, precision=highest_precision
        )
        + towards * through
    )
    grad_value = jnp.einsum(
        "nhts,nthv->nshv", scores, grad_mix, precision=highest_precision
    ) + jnp.einsum("nshk,nhkv->nshv", decayed_state, grad_state, precision=highest_precision)
    grad_last = jnp.sum(decayed_state * through, axis=1) + jnp.exp(
        final_span_state[:, 0]
    ) * jnp.sum(previous_state * grad_state, axis=-1)
    grad_cumul = query_rows * grad_query - key_rows * grad_key
    grad_cumul = grad_cumul.at[:, -1].add(grad_last)
    grad_log = jnp.flip(jnp.cumsum(jnp.flip(grad_cumul, 1), axis=1), 1)
    return (grad_query, grad_key, grad_value, grad_log)


def grouped(function, arrays, number):
    group_size = math.gcd(number, 8)
    shaped = tuple(
        (array.reshape((number // group_size, group_size) + array.shape[1:]) for array in arrays)
    )
    results = lax.map(function, shaped)
    return tuple((result.reshape((number,) + result.shape[2:]) for result in results))


def rms_back(grad_normed, source, inv_rms, gain):
    scaled = grad_normed * gain
    return inv_rms * (
        scaled - source * inv_rms * inv_rms * jnp.mean(scaled * source, axis=-1, keepdims=True)
    )


def square_sum(array):
    return jnp.sum(array * array)


def adam_update(weight, grad, first, second, factor, decay_rate):
    clipped = grad * factor
    first_new = beta_one * first + (1.0 - beta_one) * clipped
    second_new = beta_two * second + (1.0 - beta_two) * clipped * clipped
    first_hat = first_new / (1.0 - beta_one**adam_step)
    second_hat = second_new / (1.0 - beta_two**adam_step)
    master = weight.astype(jnp.float32)
    change = -learn_rate * (first_hat / (jnp.sqrt(second_hat) + adam_eps) + decay_rate * master)
    return (grad, first_new, second_new, change)


def on_device(
    tokens,
    cotangent,
    seq_extra,
    deal,
    proj_in,
    decay_down,
    decay_up,
    decay_bias,
    head_gain,
    proj_out,
    block_gains,
    ffn_in,
    ffn_out,
    first_proj_in,
    second_proj_in,
    first_decay_down,
    second_decay_down,
    first_decay_up,
    second_decay_up,
    first_decay_bias,
    second_decay_bias,
    first_head_gain,
    second_head_gain,
    first_proj_out,
    second_proj_out,
    first_block_gains,
    second_block_gains,
    first_ffn_in,
    second_ffn_in,
    first_ffn_out,
    second_ffn_out,
):
    tok_rows = tokens.shape[0]
    model_width = tokens.shape[1]
    n_spans = tok_rows // SPAN
    heads_dev = decay_bias.shape[0]
    n_tensor = lax.axis_size("tensor")
    n_data = lax.axis_size("dp")
    capacity = -(-n_spans // n_data)

    def by_span(array):
        return array.reshape((n_spans, SPAN) + array.shape[1:])

    recv_slot, send_local, back_local, home_slot = deal_tables(
        deal, n_data, n_spans, capacity, lax.axis_index("dp")
    )
    arrived_tok, arrived_cot = (
        lax.all_to_all(
            deal_send(tokens, send_local, n_spans), "dp", split_axis=0, concat_axis=0, tiled=True
        ),
        lax.all_to_all(
            deal_send(cotangent, send_local, n_spans), "dp", split_axis=0, concat_axis=0, tiled=True
        ),
    )
    dealt_tokens = deal_pick(arrived_tok, recv_slot, n_spans)
    dealt_cotangent = deal_pick(arrived_cot, recv_slot, n_spans)
    full_in, full_down, full_ffn_in, full_out, full_ffn_out = (
        lax.all_gather(proj_in, "dp", axis=0, tiled=True),
        lax.all_gather(decay_down, "dp", axis=0, tiled=True),
        lax.all_gather(ffn_in, "dp", axis=0, tiled=True),
        lax.all_gather(proj_out, "dp", axis=2, tiled=True),
        lax.all_gather(ffn_out, "dp", axis=1, tiled=True),
    )
    source = dealt_tokens.astype(jnp.float32)
    inv_first = lax.rsqrt(jnp.mean(source * source, axis=-1, keepdims=True) + norm_eps)
    normed_first = (source * inv_first * block_gains[0]).astype(jnp.bfloat16)
    project = jnp.einsum("td,dhc->thc", normed_first, full_in, preferred_element_type=jnp.float32)
    rank_in = jnp.dot(normed_first, full_down, preferred_element_type=jnp.float32).astype(
        jnp.bfloat16
    )
    logits = (
        jnp.einsum("tr,rhk->thk", rank_in, decay_up, preferred_element_type=jnp.float32)
        + decay_bias
    )
    log_decay = jax.nn.log_sigmoid(logits) / decay_scale
    scaling = DK ** (-0.5)
    query_rows = by_span(project[..., :DK] * scaling)
    key_rows = by_span(project[..., DK : 2 * DK])
    value_rows = by_span(project[..., 2 * DK : 2 * DK + DV])
    gate_raw = project[..., 2 * DK + DV :]
    running_decay = jnp.cumsum(by_span(log_decay), axis=1)
    span_ids = lax.axis_index("dp") * n_spans + jnp.arange(n_spans, dtype=jnp.int32)
    keep_state = 1.0 - span_starts(seq_extra, span_ids)
    final_span_state = running_decay[:, -1]
    decayed_state = key_rows * jnp.exp(final_span_state[:, None] - running_decay)
    span_state = jnp.einsum(
        "nchk,nchv->nhkv", decayed_state, value_rows, precision=highest_precision
    )
    factors = keep_state[:, None, None] * jnp.exp(final_span_state)
    inclusive = lax.associative_scan(combine_states, (factors, span_state), axis=0)
    identity = (jnp.ones_like(factors[0]), jnp.zeros_like(span_state[0]))
    entering = carried_in((inclusive[0][-1], inclusive[1][-1]), "dp", combine_states, identity)[1]
    before_factor = jnp.concatenate([identity[0][None], inclusive[0][:-1]], axis=0)
    before_state = jnp.concatenate([identity[1][None], inclusive[1][:-1]], axis=0)
    previous_state = keep_state[:, None, None, None] * (
        before_factor[..., None] * entering[None] + before_state
    )
    mixed = grouped(
        span_forward, (query_rows, key_rows, value_rows, running_decay, previous_state), n_spans
    )[0]
    mixed = mixed.reshape(tok_rows, heads_dev, DV)
    inv_head = lax.rsqrt(jnp.mean(mixed * mixed, axis=-1, keepdims=True) + norm_eps)
    normed_head = mixed * inv_head
    gate_sig = jax.nn.sigmoid(gate_raw)
    swish = gate_raw * gate_sig
    gated = (normed_head * head_gain * swish).astype(jnp.bfloat16).reshape(tok_rows, heads_dev * DV)
    attn_part = jnp.dot(
        gated, full_out.reshape(heads_dev * DV, model_width), preferred_element_type=jnp.float32
    )
    share_cols = model_width // n_tensor
    start_col = lax.axis_index("tensor") * share_cols
    own_cols = lax.dynamic_slice_in_dim(source, start_col, share_cols, 1)
    hidden_share = own_cols + lax.psum_scatter(
        attn_part.astype(jnp.bfloat16), "tensor", scatter_dimension=1, tiled=True
    ).astype(jnp.float32)
    hidden = lax.all_gather(hidden_share.astype(jnp.bfloat16), "tensor", axis=1, tiled=True).astype(
        hidden_share.dtype
    )
    inv_second = lax.rsqrt(jnp.mean(hidden * hidden, axis=-1, keepdims=True) + norm_eps)
    normed_second = (hidden * inv_second * block_gains[1]).astype(jnp.bfloat16)
    gate_up = jnp.einsum(
        "td,dgf->tgf", normed_second, full_ffn_in, preferred_element_type=jnp.float32
    )
    ffn_gate = gate_up[:, 0]
    ffn_upper = gate_up[:, 1]
    ffn_sig = jax.nn.sigmoid(ffn_gate)
    activated = (ffn_gate * ffn_sig * ffn_upper).astype(jnp.bfloat16)
    ffn_part = jnp.dot(activated, full_ffn_out, preferred_element_type=jnp.float32)
    ffn_share = lax.psum_scatter(
        ffn_part.astype(jnp.bfloat16), "tensor", scatter_dimension=1, tiled=True
    ).astype(jnp.float32)
    dealt_out = hidden_share + ffn_share
    grad_output = dealt_cotangent.astype(jnp.float32)
    grad_act = jnp.dot(dealt_cotangent, full_ffn_out.T, preferred_element_type=jnp.float32)
    grad_ffn_out = jnp.dot(activated.T, dealt_cotangent, preferred_element_type=jnp.float32)
    grad_gate = grad_act * ffn_upper * ffn_sig * (1.0 + ffn_gate * (1.0 - ffn_sig))
    grad_upper = grad_act * ffn_gate * ffn_sig
    grad_gate_up = jnp.stack([grad_gate, grad_upper], axis=1).astype(jnp.bfloat16)
    grad_ffn_in = jnp.einsum(
        "td,tgf->dgf", normed_second, grad_gate_up, preferred_element_type=jnp.float32
    )
    grad_second = lax.psum(
        jnp.einsum(
            "tgf,dgf->td", grad_gate_up, full_ffn_in, preferred_element_type=jnp.float32
        ).astype(jnp.bfloat16),
        "tensor",
    ).astype(jnp.float32)
    gain_second = jnp.sum(grad_second * hidden * inv_second, axis=0)
    grad_hidden = grad_output + rms_back(grad_second, hidden, inv_second, block_gains[1])
    hidden_low = grad_hidden.astype(jnp.bfloat16)
    out_flat = full_out.reshape(heads_dev * DV, model_width)
    grad_gated = jnp.dot(hidden_low, out_flat.T, preferred_element_type=jnp.float32).reshape(
        tok_rows, heads_dev, DV
    )
    grad_proj_out = jnp.dot(gated.T, hidden_low, preferred_element_type=jnp.float32).reshape(
        heads_dev, DV, model_width
    )
    grad_normed = grad_gated * head_gain * swish
    head_part = jnp.sum(grad_gated * normed_head * swish, axis=(0, 1))
    grad_gate_raw = (
        grad_gated * normed_head * head_gain * gate_sig * (1.0 + gate_raw * (1.0 - gate_sig))
    )
    grad_mixed = inv_head * (
        grad_normed - normed_head * jnp.mean(grad_normed * normed_head, axis=-1, keepdims=True)
    )
    grad_spans = by_span(grad_mixed)
    collect = jnp.einsum(
        "nchk,nchv->nhkv",
        query_rows * jnp.exp(running_decay),
        grad_spans,
        precision=highest_precision,
    )
    suffix = lax.associative_scan(
        combine_states,
        (jnp.flip(factors, 0), jnp.flip(keep_state[:, None, None, None] * collect, 0)),
        axis=0,
    )
    suffix_factor = jnp.flip(suffix[0], 0)
    suffix_grad = jnp.flip(suffix[1], 0)
    leaving = carried_in_2((suffix_factor[0], suffix_grad[0]), "dp", combine_states, identity)[1]
    reach = suffix_grad + suffix_factor[..., None] * leaving[None]
    grad_state = jnp.concatenate([reach[1:], leaving[None]], axis=0)
    grad_query, grad_key, grad_value, grad_log = grouped(
        span_backward,
        (query_rows, key_rows, value_rows, running_decay, previous_state, grad_spans, grad_state),
        n_spans,
    )
    grad_logits = (
        grad_log.reshape(tok_rows, heads_dev, DK) / decay_scale * jax.nn.sigmoid(-logits)
    ).astype(jnp.bfloat16)
    grad_decay_up = jnp.einsum(
        "tr,thk->rhk", rank_in, grad_logits, preferred_element_type=jnp.float32
    )
    grad_decay_bias = jnp.sum(grad_logits.astype(jnp.float32), axis=0)
    rank_part = jnp.einsum("thk,rhk->tr", grad_logits, decay_up, preferred_element_type=jnp.float32)
    grad_project = jnp.concatenate(
        [
            grad_query.reshape(tok_rows, heads_dev, DK) * scaling,
            grad_key.reshape(tok_rows, heads_dev, DK),
            grad_value.reshape(tok_rows, heads_dev, DV),
            grad_gate_raw,
        ],
        axis=-1,
    ).astype(jnp.bfloat16)
    grad_proj_in = jnp.einsum(
        "td,thc->dhc", normed_first, grad_project, preferred_element_type=jnp.float32
    )
    grad_first = lax.psum(
        jnp.einsum("thc,dhc->td", grad_project, full_in, preferred_element_type=jnp.float32).astype(
            jnp.bfloat16
        ),
        "tensor",
    ).astype(jnp.float32)
    rank_sum, head_sum = (
        lax.psum(rank_part.astype(jnp.bfloat16), "tensor").astype(jnp.float32),
        lax.psum(head_part.astype(jnp.bfloat16), "tensor").astype(jnp.float32),
    )
    rank_low = rank_sum.astype(jnp.bfloat16)
    grad_decay_down = jnp.dot(normed_first.T, rank_low, preferred_element_type=jnp.float32)
    grad_first = grad_first + jnp.dot(rank_low, full_down.T, preferred_element_type=jnp.float32)
    gain_first = jnp.sum(grad_first * source * inv_first, axis=0)
    dealt_grad = grad_hidden + rms_back(grad_first, source, inv_first, block_gains[0])
    grad_gains = jnp.stack([gain_first, gain_second], axis=0)
    back_out, back_grad = (
        lax.all_to_all(
            deal_send(dealt_out, back_local, n_spans).astype(jnp.bfloat16),
            "dp",
            split_axis=0,
            concat_axis=0,
            tiled=True,
        ).astype(jnp.float32),
        lax.all_to_all(
            deal_send(dealt_grad, back_local, n_spans).astype(jnp.bfloat16),
            "dp",
            split_axis=0,
            concat_axis=0,
            tiled=True,
        ).astype(jnp.float32),
    )
    block_out = deal_pick(back_out, home_slot, n_spans)
    token_grad = deal_pick(back_grad, home_slot, n_spans)
    shard_in, shard_down, shard_ffn_in, shard_out, shard_ffn_out = (
        lax.psum_scatter(grad_proj_in, "dp", scatter_dimension=0, tiled=True),
        lax.psum_scatter(grad_decay_down, "dp", scatter_dimension=0, tiled=True),
        lax.psum_scatter(grad_ffn_in, "dp", scatter_dimension=0, tiled=True),
        lax.psum_scatter(grad_proj_out, "dp", scatter_dimension=2, tiled=True),
        lax.psum_scatter(grad_ffn_out, "dp", scatter_dimension=1, tiled=True),
    )
    large_sq = (
        square_sum(shard_in)
        + square_sum(shard_ffn_in)
        + square_sum(shard_out)
        + square_sum(shard_ffn_out)
        + square_sum(shard_down) / n_tensor
    )
    slot_mask = (jnp.arange(n_tensor, dtype=jnp.int32) == lax.axis_index("tensor")).astype(
        jnp.float32
    )
    merged = lax.psum(
        (
            head_sum / n_tensor,
            grad_gains / n_tensor,
            slot_mask[:, None, None, None] * grad_decay_up[None],
            slot_mask[:, None, None] * grad_decay_bias[None],
            large_sq,
        ),
        ("dp", "tensor"),
    )
    head_total = merged[0]
    gains_total = merged[1]
    up_total = lax.dynamic_index_in_dim(merged[2], lax.axis_index("tensor"), 0, keepdims=False)
    bias_total = lax.dynamic_index_in_dim(merged[3], lax.axis_index("tensor"), 0, keepdims=False)
    grad_norm = jnp.sqrt(
        merged[4]
        + square_sum(head_total)
        + square_sum(gains_total)
        + square_sum(merged[2])
        + square_sum(merged[3])
    )
    clip_norm = clip_scale * math.sqrt(PARAMS)
    factor = jnp.minimum(1.0, clip_norm / (grad_norm + 1e-06))
    update_in = adam_update(proj_in, shard_in, first_proj_in, second_proj_in, factor, weight_decay)
    update_down = adam_update(
        decay_down, shard_down, first_decay_down, second_decay_down, factor, weight_decay
    )
    update_up = adam_update(
        decay_up, up_total, first_decay_up, second_decay_up, factor, weight_decay
    )
    update_bias = adam_update(
        decay_bias, bias_total, first_decay_bias, second_decay_bias, factor, 0.0
    )
    update_head = adam_update(head_gain, head_total, first_head_gain, second_head_gain, factor, 0.0)
    update_out = adam_update(
        proj_out, shard_out, first_proj_out, second_proj_out, factor, weight_decay
    )
    update_gains = adam_update(
        block_gains, gains_total, first_block_gains, second_block_gains, factor, 0.0
    )
    update_ffn_in = adam_update(
        ffn_in, shard_ffn_in, first_ffn_in, second_ffn_in, factor, weight_decay
    )
    update_ffn_out = adam_update(
        ffn_out, shard_ffn_out, first_ffn_out, second_ffn_out, factor, weight_decay
    )
    return (
        block_out,
        token_grad,
        grad_norm,
        update_in[0],
        update_in[1],
        update_in[2],
        update_in[3],
        update_down[0],
        update_down[1],
        update_down[2],
        update_down[3],
        update_up[0],
        update_up[1],
        update_up[2],
        update_up[3],
        update_bias[0],
        update_bias[1],
        update_bias[2],
        update_bias[3],
        update_head[0],
        update_head[1],
        update_head[2],
        update_head[3],
        update_out[0],
        update_out[1],
        update_out[2],
        update_out[3],
        update_gains[0],
        update_gains[1],
        update_gains[2],
        update_gains[3],
        update_ffn_in[0],
        update_ffn_in[1],
        update_ffn_in[2],
        update_ffn_in[3],
        update_ffn_out[0],
        update_ffn_out[1],
        update_ffn_out[2],
        update_ffn_out[3],
    )


def solution(mesh):
    placed = (
        P("dp", None),
        P("dp", None),
        P(),
        P(),
        P("dp", "tensor", None),
        P("dp", None),
        P(None, "tensor", None),
        P("tensor", None),
        P(),
        P("tensor", None, "dp"),
        P(),
        P("dp", None, "tensor"),
        P("tensor", "dp"),
        P("dp", "tensor", None),
        P("dp", "tensor", None),
        P("dp", None),
        P("dp", None),
        P(None, "tensor", None),
        P(None, "tensor", None),
        P("tensor", None),
        P("tensor", None),
        P(),
        P(),
        P("tensor", None, "dp"),
        P("tensor", None, "dp"),
        P(),
        P(),
        P("dp", None, "tensor"),
        P("dp", None, "tensor"),
        P("tensor", "dp"),
        P("tensor", "dp"),
    )
    return jax.shard_map(
        on_device,
        mesh=mesh,
        in_specs=placed,
        out_specs=(
            P("dp", "tensor"),
            P("dp", None),
            P(),
            P("dp", "tensor", None),
            P("dp", "tensor", None),
            P("dp", "tensor", None),
            P("dp", "tensor", None),
            P("dp", None),
            P("dp", None),
            P("dp", None),
            P("dp", None),
            P(None, "tensor", None),
            P(None, "tensor", None),
            P(None, "tensor", None),
            P(None, "tensor", None),
            P("tensor", None),
            P("tensor", None),
            P("tensor", None),
            P("tensor", None),
            P(),
            P(),
            P(),
            P(),
            P("tensor", None, "dp"),
            P("tensor", None, "dp"),
            P("tensor", None, "dp"),
            P("tensor", None, "dp"),
            P(),
            P(),
            P(),
            P(),
            P("dp", None, "tensor"),
            P("dp", None, "tensor"),
            P("dp", None, "tensor"),
            P("dp", None, "tensor"),
            P("tensor", "dp"),
            P("tensor", "dp"),
            P("tensor", "dp"),
            P("tensor", "dp"),
        ),
        check_vma=False,
    )
```

profile of v0, /device:TPU:0, one launch (start us, length us, event | category | flops | bytes accessed | tf_op | source)
XLA Modules:
  0.0 2088.6 jit_solution(12280268460282041667)
XLA Ops:
  26.4 152.1 %all_gather.35 = bf16[1024,16]{0,1:T(8,128)(2,1)S(1)} all-gather(bf16[128,16]{0,1:T(8,128)(2,1)S(1)} %copy-done.90), channel_id=1, replica_groups=mesh['dp'=8,'tensor'=4] {'dp'}, dimensions={0}, use_global_device_ids=true | all-gather | bytes 36864 | tf_op jit(solution)/shard_map/all_gather | solution.py:277
  178.9 29.5 %all_gather.38 = bf16[1,256,1024]{2,1,0:T(8,128)(2,1)} all-gather(bf16[1,256,128]{2,1,0:T(8,128)(2,1)S(1)} %copy-done.45), channel_id=1, replica_groups=mesh['dp'=8,'tensor'=4] {'dp'}, dimensions={2}, use_global_device_ids=true | all-gather | bytes 589824 | tf_op jit(solution)/shard_map/all_gather | solution.py:279
  244.9 17.1 all_gather.36
  373.0 31.5 %all_gather.37 = bf16[8,1,128,256]{3,2,1,0:T(8,128)(2,1)S(1)} all-gather(bf16[1,1,128,256]{3,2,1,0:T(8,128)(2,1)S(1)} %fusion.123), channel_id=1, replica_groups=mesh['dp'=8,'tensor'=4] {'dp'}, dimensions={0}, use_global_device_ids=true | all-gather | bytes 589824 | tf_op jit(solution)/shard_map/all_gather | solution.py:30
  409.3 113.3 %while.60 = (s32[]{:T(128)}, f32[5,8,64,1,256]{4,2,1,3,0:T(8,128)}, f32[5,8,64,1,256]{4,2,1,3,0:T(8,128)S(1)}, f32[5,8,64,1,128]{4,2,1,3,0:T(8,128)}, f32[5,8,64...) while((s32[]{:T(128)}, f32[5,8,64,1,256]{4,2,1,3,0:T(8,128)}, ...), condition=%wide.region_10.11_spmd.clone, body=%wide.region_9.10_spmd.sunk.clone | while | flops 327327744 | bytes 40011360 | solution.py:192
  414.4 14.1 fusion.245
  459.8 14.1 fusion.245
  540.9 47.3 %reduce-scatter.8.cloned.1.call-done = bf16[2560,256]{1,0:T(8,128)(2,1)} async-done(((bf16[2560,1024]{1,0:T(8,128)(2,1)}), bf16[2560,256]{1,0:T(8,128)(2,1)}) %reduce-scatter.8.cloned.1.call-update) | async-done | bytes 1310736 | tf_op jit(solution)/shard_map/reduce_scatter | solution.py:331
  605.8 149.5 %all-to-all-done.2 = bf16[8,320,1024]{2,1,0:T(8,128)(2,1)} async-done(((bf16[8,320,1024]{2,1,0:T(8,128)(2,1)}), bf16[8,320,1024]{2,1,0:T(8,128)(2,1)}, u32[]{:S(2)}, u32[]{:S(2)}) %all-to-all-start.2) | async-done | bytes 5242912 | tf_op jit(solution)/shard_map/all_to_all | solution.py:269
  780.1 14.4 all-gather.11.cloned.1.call-done
  822.1 18.3 all_gather.42
  840.4 80.0 %all-reduce.47.cloned.1.call-done = bf16[2560,1024]{1,0:T(8,128)(2,1)} async-done(((bf16[2560,1024]{1,0:T(8,128)(2,1)}), bf16[2560,1024]{1,0:T(8,128)(2,1)}) %all-reduce.47.cloned.1.call-update) | async-done | bytes 5242896 | tf_op jit(solution)/shard_map/psum | solution.py:360
  1042.8 31.5 %all_gather.43 = bf16[8,1,128,256]{3,2,1,0:T(8,128)(2,1)S(1)} all-gather(bf16[1,1,128,256]{3,2,1,0:T(8,128)(2,1)S(1)} %fusion.124), channel_id=1, replica_groups=mesh['dp'=8,'tensor'=4] {'dp'}, dimensions={0}, use_global_device_ids=true | all-gather | bytes 589824 | tf_op jit(solution)/shard_map/all_gather | solution.py:52
  1085.4 268.2 %while.62 = (s32[]{:T(128)}, f32[5,8,64,1,128]{4,2,1,3,0:T(8,128)}, bf16[5,8,64,1,128]{4,2,1,3,0:T(8,128)(2,1)}, bf16[5,8,64,1,256]{4,2,1,3,0:T(8,128)(2,1)}, f3...) while((s32[]{:T(128)}, f32[5,8,64,1,128]{4,2,1,3,0:T(8,128)}, ...), condition=%wide.region_26.27_spmd.clone, body=%wide.region_22.26_spmd.sunk.clone | while | flops 873800704 | bytes 88221352 | solution.py:192
  1156.4 14.1 fusion.259
  1385.4 79.7 %all-reduce.49.cloned.1.call-done = (bf16[2560,1024]{1,0:T(8,128)(2,1)}, bf16[2560,16]{0,1:T(8,128)(2,1)}) async-done(((bf16[2560,1024]{1,0:T(8,128)(2,1)}, bf16[2560,16]{0,1:T(8,128)(2,1)}), (bf16[2560,1024]{1,0:T(8,128)(2,1)}, bf16[2560,16]{0,1:T(8,128)(2,1)})) %all-reduce.49.cloned.1.call-update) | async-done | bytes 5324816 | tf_op jit(solution)/shard_map/psum | solution.py:426
  1469.3 14.1 fusion.74
  1549.7 19.2 all-to-all-done.1
  1581.4 87.7 %reduce-scatter.16.cloned.1.call-done = f32[1,256,128]{2,1,0:T(8,128)} async-done(((f32[1,256,1024]{2,1,0:T(8,128)}), f32[1,256,128]{2,1,0:T(8,128)}) %reduce-scatter.16.cloned.1.call-update) | async-done | bytes 131088 | tf_op jit(solution)/shard_map/reduce_scatter | solution.py:464
  1670.6 53.1 %reduce-scatter.20.cloned.1.call-done = f32[128,16]{0,1:T(8,128)} async-done(((f32[1024,16]{0,1:T(8,128)}), f32[128,16]{0,1:T(8,128)}) %reduce-scatter.20.cloned.1.call-update) | async-done | bytes 8208 | tf_op jit(solution)/shard_map/reduce_scatter | solution.py:462
  1725.8 73.9 %reduce-scatter.18.cloned.1.call-done = f32[704,128]{1,0:T(8,128)} async-done(((f32[704,1024]{1,0:T(8,128)}), f32[704,128]{1,0:T(8,128)}) %reduce-scatter.18.cloned.1.call-update) | async-done | bytes 360464 | tf_op jit(solution)/shard_map/reduce_scatter | solution.py:465
  1801.5 75.7 %reduce-scatter.12.cloned.1.call-done = f32[128,1,768]{2,0,1:T(8,128)} async-done(((f32[1024,1,768]{2,0,1:T(8,128)}), f32[128,1,768]{2,0,1:T(8,128)}) %reduce-scatter.12.cloned.1.call-update) | async-done | bytes 393232 | tf_op jit(solution)/shard_map/reduce_scatter | solution.py:461
  1878.9 112.5 %reduce-scatter.14.cloned.1.call-done = f32[128,2,704]{0,2,1:T(8,128)} async-done(((f32[1024,2,704]{0,2,1:T(8,128)}), f32[128,2,704]{0,2,1:T(8,128)}) %reduce-scatter.14.cloned.1.call-update) | async-done | bytes 720912 | tf_op jit(solution)/shard_map/reduce_scatter | solution.py:463
  1998.1 41.3 %all-reduce.42 = (f32[]{:T(128)}, f32[256]{0:T(256)S(1)}, f32[2,1024]{1,0:T(2,128)S(1)}, f32[4,16,1,128]{3,1,2,0:T(8,128)S(1)}, f32[4,1,128]{2,1,0:T(1,128)S(1)}) all-reduce(f32[]{:T(128)S(6)} %add.778, f32[256]{0:T(256)S(1)} %convert_multiply_fusion.5, ...), channel_id=1, replica_groups=mesh['dp'=8,'tensor'=4] {'dp','tensor'}, use_global_device_ids=true, to_apply=%region_40.41 | all-reduce | flops 11009 | bytes 88072 | tf_op jit(solution)/shard_map/psum | solution.py:477
  (754 shorter events, 897.5 us)
Async XLA Ops:
  17.9 190.5 %all-to-all-start = ((bf16[8,320,1024]{2,1,0:T(8,128)(2,1)}), bf16[8,320,1024]{2,1,0:T(8,128)(2,1)}, u32[]{:S(2)}, u32[]{:S(2)}) async-start(bf16[8,320,1024]{2,1,0:T(8,128)(2,1)} %bitcast.600), calls=%async_computation | async-start | bytes 10485760 | tf_op jit(solution)/shard_map/all_to_all | solution.py:266
  25.3 200.0 %all-gather.5.cloned.1.call-start = ((), (), s32[]{:S(2)}) async-start(), calls=%async_computation.11 | async-start | bytes 1769472 | tf_op jit(solution)/shard_map/all_gather | solution.py:276
  26.1 562.2 %reduce-scatter.8.cloned.1.call-start = ((), (), s32[]{:S(2)}) async-start(), calls=%async_computation.12 | async-start | bytes 6553600 | tf_op jit(solution)/shard_map/reduce_scatter | solution.py:331
  178.9 750.4 %copy-start.72 = (f32[1,1024]{1,0:T(1,128)}, f32[1,1024]{1,0:T(1,128)S(1)}, u32[]{:S(2)}) copy-start(f32[1,1024]{1,0:T(1,128)S(1)} %get-tuple-element.943) | copy-start | bytes 12292
  533.0 229.7 %all-gather.7.cloned.1.call-start = ((), (), s32[]{:S(2)}) async-start(), calls=%async_computation.13 | async-start | bytes 6553600 | tf_op jit(solution)/shard_map/all_gather | solution.py:334
  599.1 156.2 %all-to-all-start.2 = ((bf16[8,320,1024]{2,1,0:T(8,128)(2,1)}), bf16[8,320,1024]{2,1,0:T(8,128)(2,1)}, u32[]{:S(2)}, u32[]{:S(2)}) async-start(bf16[8,320,1024]{2,1,0:T(8,128)(2,1)} %bitcast.601), calls=%async_computation.4 | async-start | bytes 10485760 | tf_op jit(solution)/shard_map/all_to_all | solution.py:269
  604.6 161.7 %all-gather.9.cloned.1.call-start = ((), (), s32[]{:S(2)}) async-start(), calls=%async_computation.14 | async-start | bytes 3244032 | tf_op jit(solution)/shard_map/all_gather | solution.py:278
  605.2 189.4 %all-gather.11.cloned.1.call-start = ((), (), s32[]{:S(2)}) async-start(), calls=%async_computation.15 | async-start | bytes 1622016 | tf_op jit(solution)/shard_map/all_gather | solution.py:280
  605.8 314.6 %all-reduce.47.cloned.1.call-start = ((), (), s32[]{:S(2)}) async-start(), calls=%async_computation.17 | async-start | bytes 10485760 | tf_op jit(solution)/shard_map/psum | solution.py:360
  819.3 645.7 %all-reduce.49.cloned.1.call-start = ((), (), s32[]{:S(2)}) async-start(), calls=%async_computation.23 | async-start | bytes 10649600 | tf_op jit(solution)/shard_map/psum | solution.py:426
  1364.0 155.2 %reduce-scatter.10.cloned.1.call-start = ((), (), s32[]{:S(2)}) async-start(), calls=%async_computation.16 | async-start | bytes 6553600 | tf_op jit(solution)/shard_map/reduce_scatter | solution.py:347
  1377.4 291.7 %reduce-scatter.16.cloned.1.call-start = ((), (), s32[]{:S(2)}) async-start(), calls=%async_computation.20 | async-start | bytes 1179648 | tf_op jit(solution)/shard_map/reduce_scatter | solution.py:464
  1385.3 338.4 %reduce-scatter.20.cloned.1.call-start = ((), (), s32[]{:S(2)}) async-start(), calls=%async_computation.22 | async-start | bytes 73728 | tf_op jit(solution)/shard_map/reduce_scatter | solution.py:462
  1469.0 330.7 %reduce-scatter.18.cloned.1.call-start = ((), (), s32[]{:S(2)}) async-start(), calls=%async_computation.21 | async-start | bytes 3244032 | tf_op jit(solution)/shard_map/reduce_scatter | solution.py:465
  1483.5 393.7 %reduce-scatter.12.cloned.1.call-start = ((), (), s32[]{:S(2)}) async-start(), calls=%async_computation.18 | async-start | bytes 3538944 | tf_op jit(solution)/shard_map/reduce_scatter | solution.py:461
  1492.5 498.9 %reduce-scatter.14.cloned.1.call-start = ((), (), s32[]{:S(2)}) async-start(), calls=%async_computation.19 | async-start | bytes 6488064 | tf_op jit(solution)/shard_map/reduce_scatter | solution.py:463
  1523.6 45.3 %all-to-all-start.1 = ((bf16[8,320,256]{2,1,0:T(8,128)(2,1)}), bf16[8,320,256]{2,1,0:T(8,128)(2,1)S(1)}, u32[]{:S(2)}, u32[]{:S(2)}) async-start(bf16[8,320,256]{2,1,0:T(8,128)(2,1)} %bitcast.117), calls=%async_computation.3 | async-start | bytes 2621440 | tf_op jit(solution)/shard_map/all_to_all | solution.py:443
  1568.9 476.3 %copy-start.36 = (bf16[128,1,768]{2,0,1:T(8,128)(2,1)S(1)}, bf16[128,1,768]{2,0,1:T(8,128)(2,1)}, u32[]{:S(2)}) copy-start(bf16[128,1,768]{2,0,1:T(8,128)(2,1)} %param.45) | copy-start | bytes 589828
  1569.9 491.6 %all-to-all-start.3 = ((bf16[8,320,1024]{2,1,0:T(8,128)(2,1)}), bf16[8,320,1024]{2,1,0:T(8,128)(2,1)}, u32[]{:S(2)}, u32[]{:S(2)}) async-start(bf16[8,320,1024]{2,1,0:T(8,128)(2,1)} %bitcast.599), calls=%async_computation.5 | async-start | bytes 10485760 | tf_op jit(solution)/shard_map/all_to_all | solution.py:450
  1725.7 325.9 %copy-start.86 = (f32[256]{0:T(256)S(1)}, f32[256]{0:T(256)}, u32[]{:S(2)}) copy-start(f32[256]{0:T(256)} %param.49) | copy-start | bytes 3076
  1725.7 326.5 %copy-start.79 = (f32[128,16]{0,1:T(8,128)S(1)}, f32[128,16]{0,1:T(8,128)}, u32[]{:S(2)}) copy-start(f32[128,16]{0,1:T(8,128)} %reduce-scatter.20.cloned.1.call-done) | copy-start | bytes 24580
  1725.8 326.5 %copy-start.91 = (bf16[128,16]{0,1:T(8,128)(2,1)S(1)}, bf16[128,16]{0,1:T(8,128)(2,1)}, u32[]{:S(2)}) copy-start(bf16[128,16]{0,1:T(8,128)(2,1)} %param.46) | copy-start | bytes 12292
  1725.8 326.5 %copy-start.94 = (f32[128,16]{0,1:T(8,128)S(1)}, f32[128,16]{0,1:T(8,128)}, u32[]{:S(2)}) copy-start(f32[128,16]{0,1:T(8,128)} %param.57) | copy-start | bytes 24580
  1725.8 326.5 %copy-start.95 = (f32[128,16]{0,1:T(8,128)S(1)}, f32[128,16]{0,1:T(8,128)}, u32[]{:S(2)}) copy-start(f32[128,16]{0,1:T(8,128)} %param.56) | copy-start | bytes 24580
  (131 other events, 5565.8 us)
Sparse Core Ops, SparseCore 0:
  28.4 111.4 all-gather.4
  533.1 55.0 reduce-scatter.7
  591.9 41.1 all-gather.6
  635.2 114.5 all-gather.8
  751.8 42.6 all-gather.10
  819.4 100.9 all-reduce.46
  1364.2 100.8 all-reduce.48
  1467.7 51.4 reduce-scatter.9
  1523.2 145.8 reduce-scatter.15
  1673.5 50.1 reduce-scatter.19
  1728.3 71.3 reduce-scatter.17
  1803.6 73.5 reduce-scatter.11
  1881.9 109.5 reduce-scatter.13
where the time goes:
time: 2100 us; the launch traced here: 2090 us
  waiting for transfers between devices  807 us (38%)
  other arithmetic  447 us (21%)
  blocking collectives  327 us (16%)
  local copies, waits for them, and re-layouts  244 us (12%)
  matrix products  213 us (10%)
  starting transfers between devices  24.5 us (1%)
  between operations  24.3 us (1%)
    all_gather x1, blocking collectives, on_device(): lax.all_gather(decay_down, 'dp', axis=0, tiled=True)  152 us
    all_to_all x1, waiting for transfers between devices, on_device(): lax.all_to_all(deal_send(cotangent, send_local, n_spans), 'dp', split_axi...  150 us
    reduce_scatter x1, waiting for transfers between devices, on_device(): lax.psum_scatter(grad_ffn_in, 'dp', scatter_dimension=0, tiled=True)  113 us
    reduce_scatter x1, waiting for transfers between devices, on_device(): lax.psum_scatter(grad_proj_out, 'dp', scatter_dimension=2, tiled=True)  87.7 us
    psum x1, waiting for transfers between devices, on_device(): lax.psum(jnp.einsum('tgf,dgf->td', grad_gate_up, full_ffn_in, preferred_e...  80 us
    psum x1, waiting for transfers between devices, on_device(): lax.psum(jnp.einsum('thc,dhc->td', grad_project, full_in, preferred_eleme...  79.7 us
    reduce_scatter x1, waiting for transfers between devices, on_device(): lax.psum_scatter(grad_proj_in, 'dp', scatter_dimension=0, tiled=True)  75.7 us
    reduce_scatter x1, waiting for transfers between devices, on_device(): lax.psum_scatter(grad_ffn_out, 'dp', scatter_dimension=1, tiled=True)  73.9 us
  transfers between devices with their start and end apart: 17, of which 12 were waited for; matrix products, arithmetic and copies ran while one was open for 8% of the time, Pallas kernels for 0%

commit v1 on v0

v1 whole, which is shorter than its diff:
```python
import functools
import math

import jax
import jax.numpy as jnp
from jax import lax
from jax.experimental import pallas as pl
from jax.experimental.pallas import tpu as pltpu
from jax.sharding import Mesh
from jax.sharding import PartitionSpec as P

DK = 128
DV = 256
SPAN = 64
MIN_SPANS = 16
MAX_SPANS = 128
PARAMS = 12872448
TILE = 256
LEVELS = 6
HEAD = 2 * DK + 2 * DV
VMEM_LIMIT = 60 * 1024 * 1024
BF = jnp.bfloat16
F32 = jnp.float32

norm_eps = 1e-06
learn_rate = 0.05
beta_one = 0.9
beta_two = 0.95
adam_eps = 1e-08
weight_decay = 0.1
clip_scale = 0.05
adam_step = 10
decay_scale = 16.0
scaling = DK ** (-0.5)
ANY = pl.BlockSpec(memory_space=pl.ANY)
SMEM = pl.BlockSpec(memory_space=pltpu.SMEM)
VMEM = pl.BlockSpec(memory_space=pltpu.VMEM)


def dot(a, b, ca=1, cb=0):
    return lax.dot_general(a, b, (((ca,), (cb,)), ((), ())), preferred_element_type=F32)


def run(kernel, grid, in_specs, out_specs, out_shape, scratch, name, flops, moved):
    return pl.pallas_call(
        kernel,
        grid=grid,
        in_specs=in_specs,
        out_specs=out_specs,
        out_shape=out_shape,
        scratch_shapes=scratch,
        name=name,
        compiler_params=pltpu.CompilerParams(vmem_limit_bytes=VMEM_LIMIT),
        cost_estimate=pl.CostEstimate(
            flops=int(flops), bytes_accessed=int(moved), transcendentals=0
        ),
    )


def sds(*shape, dtype=F32):
    return jax.ShapeDtypeStruct(shape, dtype)


def rows_spec(cols, order=None):
    if order is None:
        return pl.BlockSpec((TILE, cols), lambda i: (i, 0))
    return pl.BlockSpec((TILE, cols), lambda i: (order - 1 - i, 0))


def whole_spec(*shape):
    zeros = (0,) * len(shape)
    return pl.BlockSpec(shape, lambda i: zeros, pipeline_mode=pl.Buffered(1))


def span_starts(seq_extra, span_ids):
    seq_spans = seq_extra + MIN_SPANS
    n = seq_extra.shape[0]
    earlier = jnp.tril(jnp.ones((n, n), jnp.int32), -1)
    bounds = jnp.sum(earlier * seq_spans[None, :], axis=1)
    return jnp.any(bounds[None, :] == span_ids[:, None], axis=1).astype(jnp.int32)


def deal_tables(deal, n_data, per_dev, capacity, my_index):
    table_grid = deal.reshape(n_data, per_dev)
    src_dev = table_grid // per_dev
    src_local = table_grid % per_dev
    my_source = lax.dynamic_index_in_dim(src_dev, my_index, 0, keepdims=False)
    earlier = jnp.tril(jnp.ones((per_dev, per_dev), jnp.int32), -1)
    same_source = (my_source[:, None] == my_source[None, :]).astype(jnp.int32)
    my_rank = jnp.sum(same_source * earlier, axis=1)
    recv_slot = my_source * capacity + my_rank
    owned_here = (src_dev == my_index).astype(jnp.int32)
    send_rank = jnp.sum(owned_here[:, None, :] * earlier[None], axis=2)
    slot_ids = jnp.arange(capacity, dtype=jnp.int32)
    send_hit = owned_here[:, :, None] * (
        send_rank[:, :, None] == slot_ids[None, None, :]
    ).astype(jnp.int32)
    send_local = jnp.sum(send_hit * src_local[:, :, None], axis=1)
    peer_ids = jnp.arange(n_data, dtype=jnp.int32)
    local_ids = jnp.arange(per_dev, dtype=jnp.int32)
    back_hit = (
        (my_source[None, None, :] == peer_ids[:, None, None])
        & (my_rank[None, None, :] == slot_ids[None, :, None])
    ).astype(jnp.int32)
    back_local = jnp.sum(back_hit * local_ids[None, None, :], axis=2)
    home_hit = owned_here[:, :, None] * (
        src_local[:, :, None] == local_ids[None, None, :]
    ).astype(jnp.int32)
    home_slot = jnp.sum(
        home_hit * (peer_ids[:, None, None] * capacity + send_rank[:, :, None]), axis=(0, 1)
    )
    return recv_slot, send_local.reshape(-1), back_local.reshape(-1), home_slot


def level_matrices():
    t = jnp.arange(TILE, dtype=jnp.int32)[:, None]
    u = jnp.arange(TILE, dtype=jnp.int32)[None, :]
    ups = []
    level = jnp.full((TILE, TILE), LEVELS + 1, jnp.int32)
    for l in range(LEVELS):
        block = SPAN >> l
        half = block // 2
        same = (t // block) == (u // block)
        mid = (t // block) * block + half
        right = (t >= mid) & (u >= mid) & (u <= t)
        left = (t < mid) & (u > t) & (u < mid)
        ups.append(same & (right | left))
        hit = same & (t % block >= half) & (u % block < half)
        level = jnp.where(hit, l, level)
    level = jnp.where(t == u, LEVELS, level)
    same = (t // SPAN) == (u // SPAN)
    ups.append(same & (u <= t))
    ups.append(same & (u > t))
    ups = jnp.stack(ups).astype(BF)
    return ups, jnp.swapaxes(ups, 1, 2), level, level.T


def send_pick_kernel(count, width, table, src, out, sems):
    col = pl.multiple_of(table[count], 128)

    def copy(i):
        return pltpu.make_async_copy(
            src.at[pl.ds(pl.multiple_of(table[i] * SPAN, SPAN), SPAN), pl.ds(col, width)],
            out.at[pl.ds(pl.multiple_of(i * SPAN, SPAN), SPAN), :],
            sems.at[i],
        )

    for i in range(count):
        copy(i).start()
    for i in range(count):
        copy(i).wait()


def send_pick(rows, table, col, width, name):
    count = table.shape[0]
    return pl.pallas_call(
        functools.partial(send_pick_kernel, count, width),
        in_specs=[SMEM, ANY],
        out_specs=VMEM,
        out_shape=sds(count * SPAN, width, dtype=rows.dtype),
        scratch_shapes=[pltpu.SemaphoreType.DMA((count,))],
        name=name,
        cost_estimate=pl.CostEstimate(
            flops=0, bytes_accessed=count * SPAN * width * 4, transcendentals=0
        ),
    )(jnp.concatenate([table, col.reshape(1)]), rows)


def split_pick_kernel(half, table, src, own, other):
    def body(i, _):
        to = pl.multiple_of(i * SPAN, SPAN)
        for out, at in ((own, i), (other, i + half)):
            out[pl.ds(to, SPAN), :] = src[pl.ds(pl.multiple_of(table[at] * SPAN, SPAN), SPAN), :]
        return 0

    lax.fori_loop(0, half, body, 0)


def split_pick(rows, table, name):
    half = table.shape[0] // 2
    out = sds(half * SPAN, rows.shape[1], dtype=rows.dtype)
    return pl.pallas_call(
        functools.partial(split_pick_kernel, half),
        in_specs=[SMEM, VMEM],
        out_specs=[VMEM, VMEM],
        out_shape=[out, out],
        name=name,
        cost_estimate=pl.CostEstimate(
            flops=0, bytes_accessed=rows.size * 4, transcendentals=0
        ),
    )(table, rows)


def join_pick_kernel(count, half, table, own, other, out):
    x = table[count]

    def body(i, _):
        local = table[i]
        low = pl.multiple_of(lax.rem(local, half) * SPAN, SPAN)
        here = (local >= half).astype(jnp.int32) == x
        to = pl.ds(pl.multiple_of(i * SPAN, SPAN), SPAN)

        @pl.when(here)
        def _():
            out[to, :] = own[pl.ds(low, SPAN), :]

        @pl.when(jnp.logical_not(here))
        def _():
            out[to, :] = other[pl.ds(low, SPAN), :]

        return 0

    lax.fori_loop(0, count, body, 0)


def join_pick(own, other, table, x, name):
    count = table.shape[0]
    half = own.shape[0] // SPAN
    return pl.pallas_call(
        functools.partial(join_pick_kernel, count, half),
        in_specs=[SMEM, VMEM, VMEM],
        out_specs=VMEM,
        out_shape=sds(count * SPAN, own.shape[1], dtype=own.dtype),
        name=name,
        cost_estimate=pl.CostEstimate(
            flops=0, bytes_accessed=count * SPAN * own.shape[1] * 4, transcendentals=0
        ),
    )(jnp.concatenate([table, x.reshape(1)]), own, other)


def home_kernel(count, table, *refs):
    srcs, out = refs[:-1], refs[-1]
    width = srcs[0].shape[1]

    def body(i, _):
        row = pl.multiple_of(table[i] * SPAN, SPAN)
        to = pl.multiple_of(i * SPAN, SPAN)
        for k, src in enumerate(srcs):
            col = pl.multiple_of(table[count + k], 128)
            out[pl.ds(to, SPAN), pl.ds(col, width)] = src[pl.ds(row, SPAN), :].astype(F32)
        return 0

    lax.fori_loop(0, count, body, 0)


def home(pieces, table, cols, name):
    count = table.shape[0]
    width = pieces[0].shape[1]
    total = width * len(pieces)
    return pl.pallas_call(
        functools.partial(home_kernel, count),
        in_specs=[SMEM] + [VMEM] * len(pieces),
        out_specs=VMEM,
        out_shape=sds(count * SPAN, total),
        name=name,
        compiler_params=pltpu.CompilerParams(vmem_limit_bytes=VMEM_LIMIT),
        cost_estimate=pl.CostEstimate(
            flops=0, bytes_accessed=count * SPAN * total * 6, transcendentals=0
        ),
    )(jnp.concatenate([table, jnp.stack(cols)]), *pieces)


def rms_scale(x):
    return lax.rsqrt(jnp.mean(x * x, axis=-1, keepdims=True) + norm_eps)


def distances(ups, log_decay):
    high = log_decay.astype(BF)
    lower = (log_decay - high.astype(F32)).astype(BF)
    return dot(ups, high) + dot(ups, lower)


def head_cols(h, part):
    start = h * HEAD + (0, DK, 2 * DK, 2 * DK + DV)[part]
    return slice(start, start + (DK, DK, DV, DV)[part])


def log_sigmoid(v):
    return jnp.minimum(v, 0.0) - jnp.log(1.0 + jnp.exp(-jnp.abs(v)))


def project_kernel(
    spans, n, ints, q0, q1, q2, q3, gain, w_in, w_down, up, bias, ups,
    src, normed, qkvg, log_decay, rank, packet, state, factor,
):
    step = pl.program_id(0)
    quarter = src.shape[1] // 4
    for k, piece in enumerate((q0, q1, q2, q3)):
        src[:, pl.ds(pl.multiple_of(ints[spans + k] * quarter, 128), quarter)] = piece[...]

    @pl.when(step == 0)
    def _():
        state[...] = jnp.zeros_like(state)
        factor[...] = jnp.ones_like(factor)

    x = src[...].astype(F32)
    nf = (x * rms_scale(x) * gain[...]).astype(BF)
    normed[...] = nf
    low = dot(nf, w_down[...], 1, 1).astype(BF)
    rank[...] = low
    logits = dot(low, up[...]) + bias[...]
    ld = log_sigmoid(logits) * (1.0 / decay_scale)
    log_decay[...] = ld
    proj = dot(nf, w_in[...], 1, 1)
    towards = jnp.exp(distances(ups[LEVELS + 1], ld))
    per_tile = TILE // SPAN
    for h in range(2):
        qkvg[:, head_cols(h, 0)] = (proj[:, head_cols(h, 0)] * scaling).astype(BF)
        qkvg[:, h * HEAD + DK : (h + 1) * HEAD] = proj[:, h * HEAD + DK : (h + 1) * HEAD].astype(BF)
    for j in range(per_tile):
        rows = slice(j * SPAN, (j + 1) * SPAN)
        keep = ints[step * per_tile + j].astype(F32)
        total = jnp.exp(jnp.sum(ld[rows], axis=0, keepdims=True)) * keep
        factor[0:1, :] = factor[0:1, :] * total
        for h in range(2):
            lanes = slice(h * DK, (h + 1) * DK)
            kd = (qkvg[rows, head_cols(h, 1)].astype(F32) * towards[rows, lanes]).astype(BF)
            state[h] = state[h] * total[:, lanes] + dot(qkvg[rows, head_cols(h, 2)], kd, 0, 0)

    @pl.when(step == n - 1)
    def _():
        packet[0:DV] = state[0]
        packet[DV : 2 * DV] = state[1]
        packet[2 * DV :] = jnp.zeros((16, DK), F32)
        packet[2 * DV : 2 * DV + 1] = factor[0:1, 0:DK]
        packet[2 * DV + 1 : 2 * DV + 2] = factor[0:1, DK : 2 * DK]


def within_kernel(qkvg, log_decay, ups, level, within):
    ld = log_decay[...]
    high = ld.astype(BF)
    lower = (ld - high.astype(F32)).astype(BF)
    lev = level[...]
    scores = [None, None]
    for l in range(LEVELS + 1):
        if l < LEVELS:
            x = jnp.exp(dot(ups[l], high) + dot(ups[l], lower))
        for h in range(2):
            q, k = qkvg[:, head_cols(h, 0)], qkvg[:, head_cols(h, 1)]
            if l < LEVELS:
                xh = x[:, h * DK : (h + 1) * DK]
                q = (q.astype(F32) * xh).astype(BF)
                k = (k.astype(F32) * xh).astype(BF)
            s = dot(q, k, 1, 1)
            scores[h] = jnp.where(lev == l, s, 0.0 if l == 0 else scores[h])
    for h in range(2):
        within[:, h * DV : (h + 1) * DV] = dot(scores[h].astype(BF), qkvg[:, head_cols(h, 2)])


def mix_kernel(
    spans, ints, qkvg, log_decay, within, entering, ups, head_gain, w_out,
    mixed, gated, attn, before, state,
):
    step = pl.program_id(0)
    per_tile = TILE // SPAN

    @pl.when(step == 0)
    def _():
        state[0] = entering[0:DV]
        state[1] = entering[DV : 2 * DV]

    ld = log_decay[...]
    since = jnp.exp(distances(ups[LEVELS], ld))
    towards = jnp.exp(distances(ups[LEVELS + 1], ld))
    for j in range(per_tile):
        rows = slice(j * SPAN, (j + 1) * SPAN)
        keep = ints[step * per_tile + j].astype(F32)
        for h in range(2):
            lanes = slice(h * DK, (h + 1) * DK)
            values = slice(h * DV, (h + 1) * DV)
            prev = state[h] * keep
            prev_low = prev.astype(BF)
            before[j, h] = prev_low
            qd = (qkvg[rows, head_cols(h, 0)].astype(F32) * since[rows, lanes]).astype(BF)
            kd = (qkvg[rows, head_cols(h, 1)].astype(F32) * towards[rows, lanes]).astype(BF)
            mixed[rows, values] = within[rows, values] + dot(qd, prev_low, 1, 1)
            last = since[j * SPAN + SPAN - 1 : j * SPAN + SPAN, lanes]
            state[h] = prev * last + dot(qkvg[rows, head_cols(h, 2)], kd, 0, 0)
    for h in range(2):
        values = slice(h * DV, (h + 1) * DV)
        m = mixed[:, values]
        g = qkvg[:, head_cols(h, 3)].astype(F32)
        y = m * rms_scale(m) * head_gain[...] * g * jax.nn.sigmoid(g)
        gated[:, values] = y.astype(BF)
    attn[...] = dot(gated[...], w_out[...]).astype(BF)


def ffn_kernel(
    ints, src, attn_a, attn_b, c0, c1, c2, c3, gain, w_gate, w_up, w_out,
    hidden, normed, act, grad_gu, cot, keep_out, send_out, grad_second,
    part,
):
    quarter = cot.shape[1] // 4
    for k, piece in enumerate((c0, c1, c2, c3)):
        cot[:, pl.ds(pl.multiple_of(ints[k] * quarter, 128), quarter)] = piece[...]
    hid = src[...].astype(F32) + (attn_a[...].astype(F32) + attn_b[...].astype(F32))
    hidden[...] = hid
    ns = (hid * rms_scale(hid) * gain[...]).astype(BF)
    normed[...] = ns
    gate = dot(ns, w_gate[...], 1, 1)
    upper = dot(ns, w_up[...], 1, 1)
    sig = jax.nn.sigmoid(gate)
    swish = gate * sig
    low = (swish * upper).astype(BF)
    act[...] = low
    part[...] = dot(low, w_out[...]).astype(BF)
    core = ints[4]
    for h in range(2):
        mine = pl.multiple_of((2 * h + core) * quarter, 128)
        theirs = pl.multiple_of((2 * h + 1 - core) * quarter, 128)
        keep_out[:, h * quarter : (h + 1) * quarter] = part[:, pl.ds(mine, quarter)]
        send_out[:, h * quarter : (h + 1) * quarter] = part[:, pl.ds(theirs, quarter)]
    ga = dot(cot[...], w_out[...], 1, 1)
    f = gate.shape[1]
    gg = (ga * upper * sig * (1.0 + gate * (1.0 - sig))).astype(BF)
    gu = (ga * swish).astype(BF)
    grad_gu[:, :f] = gg
    grad_gu[:, f:] = gu
    grad_second[...] = (dot(gg, w_gate[...]) + dot(gu, w_up[...])).astype(BF)


def ring_dp(p, n):
    p = lax.rem(p + 2 * n, n)
    return jnp.where(p < n // 2, 2 * p, 2 * (n - 1 - p) + 1)


def weight_grad_into(acc, lhs, rhs, chunk):
    def body(i, _):
        at = pl.multiple_of(i * chunk, chunk)
        acc[pl.ds(at, chunk), :] = dot(lhs[:, pl.ds(at, chunk)], rhs[...], 0, 0).astype(BF)
        return 0

    lax.fori_loop(0, acc.shape[0] // chunk, body, 0)


def grad_pair_kernel(n, f, ints, grad_gu, normed, own, *rest):
    others, (acc,) = rest[:n], rest[n:]
    r, x = ints[5], ints[6]
    w = own.shape[2]
    for m in range(2):
        weight_grad_into(acc, grad_gu.at[:, pl.ds(m * 2 * f, 2 * f)], normed, 128)
        for s in range(1, n + 1):
            col = pl.multiple_of(ring_dp(r - s if m == 0 else r + s, n) * w, 128)
            mine = pl.multiple_of(x * f, 16)
            theirs = pl.multiple_of((1 - x) * f, 16)
            own[s - 1, m * f : (m + 1) * f, :] = acc[pl.ds(mine, f), pl.ds(col, w)]
            others[s - 1][m * f : (m + 1) * f, :] = acc[pl.ds(theirs, f), pl.ds(col, w)]


def to_blocks(n, ints, acc, out, f):
    r = ints[5]
    w = out.shape[3]
    for s in range(1, n + 1):
        for h in range(2):
            col = pl.multiple_of(ring_dp(r - s if h == 0 else r + s, n) * w, 128)
            out[s - 1, h] = acc[h * f : (h + 1) * f, pl.ds(col, w)]


def grad_blocks_kernel(n, f, ints, lhs, rhs, out, acc):
    weight_grad_into(acc, lhs, rhs, 128)
    to_blocks(n, ints, acc, out, f)


def grad_plain_kernel(f, ints, lhs, rhs, out):
    weight_grad_into(out, lhs, rhs, 128)


def out_back_kernel(
    spans, n, nd, ints, hidden, cot, gs_a, gs_b, gain, w_out, gated, mixed, qkvg, log_decay, head_gain, ups,
    grad_hidden, grad_mixed, grad_gate, w_grad, gain_grad, head_grad, packet,
    acc, state, gain_sum, head_sum,
):
    step = pl.program_id(0)
    tile = n - 1 - step
    per_tile = TILE // SPAN

    @pl.when(step == 0)
    def _():
        acc[...] = jnp.zeros_like(acc)
        state[...] = jnp.zeros_like(state)
        gain_sum[...] = jnp.zeros_like(gain_sum)
        head_sum[...] = jnp.zeros_like(head_sum)

    gs = gs_a[...].astype(F32) + gs_b[...].astype(F32)
    hid = hidden[...]
    inv = rms_scale(hid)
    normal = hid * inv
    gain_sum[0:1, :] += jnp.sum(gs * normal, axis=0, keepdims=True)
    e = gs * gain[...]
    gh = cot[...].astype(F32) + inv * (e - normal * jnp.mean(e * normal, axis=-1, keepdims=True))
    grad_hidden[...] = gh
    low = gh.astype(BF)
    acc[...] += dot(gated[...], low, 0, 0)
    gg = dot(low, w_out[...], 1, 1)
    for h in range(2):
        values = slice(h * DV, (h + 1) * DV)
        m = mixed[:, values]
        inv_head = rms_scale(m)
        nh = m * inv_head
        g = qkvg[:, head_cols(h, 3)].astype(F32)
        sig = jax.nn.sigmoid(g)
        w = g * sig
        gd = gg[:, values]
        head_sum[0:1, :] += jnp.sum(gd * nh * w, axis=0, keepdims=True)
        gn = gd * head_gain[...]
        grad_gate[:, values] = (gn * nh * sig * (1.0 + g * (1.0 - sig))).astype(BF)
        gn = gn * w
        gm = inv_head * (gn - nh * jnp.mean(gn * nh, axis=-1, keepdims=True))
        grad_mixed[:, values] = gm.astype(BF)
    since = jnp.exp(distances(ups[LEVELS], log_decay[...]))
    for j in reversed(range(per_tile)):
        rows = slice(j * SPAN, (j + 1) * SPAN)
        keep = ints[7 + tile * per_tile + j].astype(F32)
        for h in range(2):
            lanes = slice(h * DK, (h + 1) * DK)
            values = slice(h * DV, (h + 1) * DV)
            qd = (qkvg[rows, head_cols(h, 0)].astype(F32) * since[rows, lanes]).astype(BF)
            last = since[j * SPAN + SPAN - 1 : j * SPAN + SPAN, lanes]
            state[h] = keep * (state[h] * last + dot(grad_mixed[rows, values], qd, 0, 0))

    @pl.when(step == n - 1)
    def _():
        packet[0:DV] = state[0]
        packet[DV : 2 * DV] = state[1]
        gain_grad[...] = gain_sum[...]
        head_grad[...] = head_sum[...]
        low_acc = acc[...].astype(BF)
        if nd is None:
            w_grad[...] = low_acc
        else:
            r = ints[5]
            width = w_grad.shape[3]
            acc[...] = low_acc.astype(F32)
            for s in range(1, nd + 1):
                for h in range(2):
                    col = pl.multiple_of(ring_dp(r - s if h == 0 else r + s, nd) * width, 128)
                    w_grad[s - 1, h] = acc[h * DV : (h + 1) * DV, pl.ds(col, width)].astype(BF)


def within_back_kernel(qkvg, log_decay, grad_mixed, ups, downs, level, level_t, grad_qk, grad_v, grad_ld):
    ld = log_decay[...]
    high = ld.astype(BF)
    lower = (ld - high.astype(F32)).astype(BF)
    lev, lev_t = level[...], level_t[...]
    gd, gd_t = [], []
    for h in range(2):
        v, gm = qkvg[:, head_cols(h, 2)], grad_mixed[:, h * DV : (h + 1) * DV]
        gd.append(dot(gm, v, 1, 1))
        gd_t.append(dot(v, gm, 1, 1))
    scores_t = [None, None]
    grad_q, grad_k = [None, None], [None, None]
    for l in range(LEVELS + 1):
        if l < LEVELS:
            x = jnp.exp(dot(ups[l], high) + dot(ups[l], lower))
        parts = []
        for h in range(2):
            q, k = qkvg[:, head_cols(h, 0)], qkvg[:, head_cols(h, 1)]
            if l < LEVELS:
                xh = x[:, h * DK : (h + 1) * DK]
                qf, kf = q.astype(F32) * xh, k.astype(F32) * xh
                q, k = qf.astype(BF), kf.astype(BF)
            s = dot(k, q, 1, 1)
            scores_t[h] = jnp.where(lev_t == l, s, 0.0 if l == 0 else scores_t[h])
            here = jnp.where(lev == l, gd[h], 0.0).astype(BF)
            here_t = jnp.where(lev_t == l, gd_t[h], 0.0).astype(BF)
            dq, dk = dot(here, k), dot(here_t, q)
            if l < LEVELS:
                parts.append(qf * dq + kf * dk)
                dq, dk = dq * xh, dk * xh
            grad_q[h] = dq if l == 0 else grad_q[h] + dq
            grad_k[h] = dk if l == 0 else grad_k[h] + dk
        if l < LEVELS:
            both = dot(downs[l], jnp.concatenate(parts, axis=1).astype(BF))
            total = both if l == 0 else total + both
    grad_ld[...] = total
    for h in range(2):
        grad_qk[:, 2 * h * DK : (2 * h + 1) * DK] = grad_q[h]
        grad_qk[:, (2 * h + 1) * DK : (2 * h + 2) * DK] = grad_k[h]
        grad_v[:, h * DV : (h + 1) * DV] = dot(
            scores_t[h].astype(BF), grad_mixed[:, h * DV : (h + 1) * DV]
        )


def project_back_kernel(
    n, ints, qkvg, log_decay, grad_mixed, before, leaving, grad_qk, grad_v, grad_ld, grad_gate, rank, up, bias,
    ups, downs, w_in,
    grad_project, grad_first, rank_part, up_grad, bias_grad,
    state, up_sum, bias_sum, d_since, d_towards, ld_sum,
):
    step = pl.program_id(0)
    tile = n - 1 - step
    per_tile = TILE // SPAN

    @pl.when(step == 0)
    def _():
        state[0] = leaving[0:DV]
        state[1] = leaving[DV : 2 * DV]
        up_sum[...] = jnp.zeros_like(up_sum)
        bias_sum[...] = jnp.zeros_like(bias_sum)

    ld = log_decay[...]
    since = jnp.exp(distances(ups[LEVELS], ld))
    towards = jnp.exp(distances(ups[LEVELS + 1], ld))
    for j in reversed(range(per_tile)):
        rows = slice(j * SPAN, (j + 1) * SPAN)
        keep = ints[7 + tile * per_tile + j].astype(F32)
        for h in range(2):
            lanes = slice(h * DK, (h + 1) * DK)
            values = slice(h * DV, (h + 1) * DV)
            gm = grad_mixed[rows, values]
            v = qkvg[rows, head_cols(h, 2)]
            qd = qkvg[rows, head_cols(h, 0)].astype(F32) * since[rows, lanes]
            kd = qkvg[rows, head_cols(h, 1)].astype(F32) * towards[rows, lanes]
            prev = before[j, h]
            after = state[h]
            after_low = after.astype(BF)
            dq = dot(gm, prev)
            dk = dot(v, after_low)
            d_since[rows, lanes] = (qd * dq).astype(BF)
            d_towards[rows, lanes] = (kd * dk).astype(BF)
            dq = grad_qk[rows, 2 * h * DK : (2 * h + 1) * DK] + dq * since[rows, lanes]
            dk = grad_qk[rows, (2 * h + 1) * DK : (2 * h + 2) * DK] + dk * towards[rows, lanes]
            dv = grad_v[rows, values] + dot(kd.astype(BF), after_low, 1, 1)
            grad_project[rows, head_cols(h, 0)] = (dq * scaling).astype(BF)
            grad_project[rows, head_cols(h, 1)] = dk.astype(BF)
            grad_project[rows, head_cols(h, 2)] = dv.astype(BF)
            grad_project[rows, head_cols(h, 3)] = grad_gate[rows, values]
            last = since[j * SPAN + SPAN - 1 : j * SPAN + SPAN, lanes]
            d_last = last * jnp.sum(prev.astype(F32) * after, axis=0, keepdims=True)
            ld_sum[rows, lanes] = grad_ld[rows, lanes] + d_last
            state[h] = keep * (after * last + dot(gm, qd.astype(BF), 0, 0))
    d_log = ld_sum[...] + dot(downs[LEVELS], d_since[...]) + dot(downs[LEVELS + 1], d_towards[...])
    logits = dot(rank[...], up[...]) + bias[...]
    gl = (d_log * (1.0 / decay_scale) * jax.nn.sigmoid(-logits)).astype(BF)
    up_sum[...] += dot(rank[...], gl, 0, 0)
    bias_sum[0:1, :] += jnp.sum(gl.astype(F32), axis=0, keepdims=True)
    rank_part[...] = dot(up[...], gl, 1, 1)
    grad_first[...] = dot(grad_project[...], w_in[...]).astype(BF)

    @pl.when(step == n - 1)
    def _():
        up_grad[...] = up_sum[...]
        bias_grad[...] = bias_sum[...]


def source_back_kernel(
    n, ints, src, normed, gf_a, gf_b, rank_a, rank_b, w_down, gain, grad_hidden,
    own, other, down_grad, gain_grad,
    dealt, down_sum, gain_sum,
):
    step = pl.program_id(0)

    @pl.when(step == 0)
    def _():
        down_sum[...] = jnp.zeros_like(down_sum)
        gain_sum[...] = jnp.zeros_like(gain_sum)

    low = (rank_a[...] + rank_b[...]).astype(BF)
    gf = gf_a[...].astype(F32) + gf_b[...].astype(F32) + dot(low, w_down[...], 0, 0)
    x = src[...].astype(F32)
    inv = rms_scale(x)
    normal = x * inv
    gain_sum[0:1, :] += jnp.sum(gf * normal, axis=0, keepdims=True)
    e = gf * gain[...]
    dealt[...] = (
        grad_hidden[...] + inv * (e - normal * jnp.mean(e * normal, axis=-1, keepdims=True))
    ).astype(BF)
    down_sum[...] += dot(low, normed[...])
    quarter = own.shape[1]
    own[...] = dealt[:, pl.ds(pl.multiple_of(ints[0] * quarter, 128), quarter)]
    other[...] = dealt[:, pl.ds(pl.multiple_of(ints[1] * quarter, 128), quarter)]

    @pl.when(step == n - 1)
    def _():
        down_grad[...] = down_sum[...]
        gain_grad[...] = gain_sum[...]


def block_out_kernel(ints, hidden, keep_out, recv_out, own, other):
    x, core = ints[6], ints[4]
    quarter = own.shape[1]
    for target, half in ((own, x), (other, 1 - x)):
        at = pl.multiple_of((2 * half + core) * quarter, 128)
        pair = pl.multiple_of(half * quarter, 128)
        share = keep_out[:, pl.ds(pair, quarter)].astype(F32) + recv_out[:, pl.ds(pair, quarter)].astype(F32)
        target[...] = (hidden[:, pl.ds(at, quarter)] + share).astype(BF)


def ring_perms(n):
    order = [2 * p for p in range(n // 2)] + [2 * (n - 1 - p) + 1 for p in range(n // 2, n)]
    forward = [(order[p], order[(p + 1) % n]) for p in range(n)]
    return forward, [(b, a) for a, b in forward]


def place_kernel(count, moves, ints, *refs):
    pieces, outs, sems = refs[:count], refs[count:-1], refs[-1]
    copies = []
    for k, (piece, low, rows, out, row_at, col_at) in enumerate(moves):
        w = pieces[piece].shape[1]
        copies.append(
            pltpu.make_async_copy(
                pieces[piece].at[pl.ds(low, rows), :],
                outs[out].at[
                    pl.ds(pl.multiple_of(ints[row_at], 16), rows),
                    pl.ds(pl.multiple_of(ints[col_at], 128), w),
                ],
                sems.at[k],
            )
        )
    for c in copies:
        c.start()
    for c in copies:
        c.wait()


def place(pieces, moves, ints, outs, name):
    return pl.pallas_call(
        functools.partial(place_kernel, len(pieces), moves),
        in_specs=[SMEM] + [ANY] * len(pieces),
        out_specs=[VMEM] * len(outs),
        out_shape=outs,
        scratch_shapes=[pltpu.SemaphoreType.DMA((len(moves),))],
        name=name,
        compiler_params=pltpu.CompilerParams(vmem_limit_bytes=VMEM_LIMIT),
        cost_estimate=pl.CostEstimate(
            flops=0, bytes_accessed=4 * sum(o.size for o in outs), transcendentals=0
        ),
    )(ints, *pieces)


def ring_gather(forward_piece, backward_piece, n):
    forward, backward = ring_perms(n)
    ahead, behind = [forward_piece], [backward_piece]
    for _ in range(n - 1):
        ahead.append(lax.ppermute(ahead[-1], "dp", forward))
        behind.append(lax.ppermute(behind[-1], "dp", backward))
    return ahead, behind


def ring_sum(first, second, n):
    forward, backward = ring_perms(n)
    a, b = first(1).astype(BF), second(1).astype(BF)
    for s in range(1, n):
        a = lax.ppermute(a, "dp", forward).astype(F32) + first(s + 1).astype(F32)
        b = lax.ppermute(b, "dp", backward).astype(F32) + second(s + 1).astype(F32)
        if s < n - 1:
            a, b = a.astype(BF), b.astype(BF)
    return a, b


def combine(earlier, later):
    fe, fl = earlier[2 * DV : 2 * DV + 2], later[2 * DV : 2 * DV + 2]
    se, sl = (a[: 2 * DV].reshape(2, DV, DK) for a in (earlier, later))
    s = fl[:, None, :] * se + sl
    return jnp.concatenate(
        [s.reshape(2 * DV, DK), fl * fe, jnp.zeros((14, DK), F32)], axis=0
    )


def carried(packet, count, reach, ahead):
    def shifted(value, k):
        if ahead:
            perm = [(i, i + k) for i in range(count - k)]
        else:
            perm = [(i + k, i) for i in range(count - k)]
        return lax.ppermute(value.astype(BF), ("dp", "x"), perm).astype(F32)

    width = 1
    while 2 * width < reach:
        packet = combine(shifted(packet, width), packet)
        width *= 2
    return combine(shifted(packet, 1 + width), shifted(packet, 1))


def all_sum(value, axes, sizes):
    for axis, size in zip(axes, sizes):
        bit = 1
        while bit < size:
            value = value + lax.ppermute(value, axis, [(i, i ^ bit) for i in range(size)])
            bit *= 2
    return value


def square_sum(array):
    return jnp.sum(array * array)


def adam_update(weight, grad, first, second, factor, decay_rate):
    clipped = grad * factor
    first_new = beta_one * first + (1.0 - beta_one) * clipped
    second_new = beta_two * second + (1.0 - beta_two) * clipped * clipped
    first_hat = first_new / (1.0 - beta_one**adam_step)
    second_hat = second_new / (1.0 - beta_two**adam_step)
    master = weight.astype(F32)
    change = -learn_rate * (first_hat / (jnp.sqrt(second_hat) + adam_eps) + decay_rate * master)
    return (grad, first_new, second_new, change)


def swap(value, axis):
    return lax.ppermute(value, axis, [(0, 1), (1, 0)])


def on_device(
    tokens, cotangent, seq_extra, deal, proj_in, decay_down, decay_up, decay_bias, head_gain, proj_out, block_gains,
    ffn_in, ffn_out, first_proj_in, second_proj_in, first_decay_down, second_decay_down, first_decay_up,
    second_decay_up, first_decay_bias, second_decay_bias, first_head_gain, second_head_gain, first_proj_out,
    second_proj_out, first_block_gains, second_block_gains, first_ffn_in, second_ffn_in, first_ffn_out, second_ffn_out,
):
    d = tokens.shape[1]
    nd = lax.axis_size("dp")
    dp, x, core = lax.axis_index("dp"), lax.axis_index("x"), lax.axis_index("core")
    tensor = 2 * x + core
    per_dev = tokens.shape[0] // SPAN
    spans = per_dev // 2
    rows = spans * SPAN
    tiles = rows // TILE
    capacity = -(-per_dev // nd)
    quarter = d // 4
    f = ffn_out.shape[0]
    w = d // nd
    ring = w % 128 == 0
    place_in_ring = jnp.where(dp % 2 == 0, dp // 2, nd - 1 - dp // 2)

    recv_slot, send_local, back_local, home_slot = deal_tables(deal, nd, per_dev, capacity, dp)
    mine = lax.dynamic_slice_in_dim(recv_slot, x * spans, spans)
    theirs = lax.dynamic_slice_in_dim(recv_slot, (1 - x) * spans, spans)
    split_table = jnp.concatenate([mine, theirs])
    span_ids = (dp * 2 + x) * spans + jnp.arange(spans, dtype=jnp.int32)
    keep = 1 - span_starts(seq_extra, span_ids)
    other_quarter = 2 * (1 - x) + core
    quarters = jnp.stack([tensor, other_quarter, 2 * x + 1 - core, 2 * (1 - x) + 1 - core])
    ints = jnp.concatenate([quarters, jnp.stack([core, place_in_ring, x]), keep])
    ints = ints.astype(jnp.int32)
    span_ints = jnp.concatenate([keep, quarters]).astype(jnp.int32)
    ups, downs, level, level_t = level_matrices()

    def dealt(array, name):
        picked = send_pick(array, send_local, tensor * quarter, quarter, name + "_send")
        arrived = lax.all_to_all(picked, "dp", split_axis=0, concat_axis=0, tiled=True)
        own, other = split_pick(arrived, split_table, name + "_split")
        across = swap(other, "x")
        return own, across, swap(own, "core"), swap(across, "core")

    down_t = decay_down.T
    shard_p = jnp.concatenate([proj_in.reshape(w, HEAD).T, proj_out.reshape(DV, w), down_t], axis=0)
    shard_f = jnp.concatenate([ffn_in.reshape(w, 2 * f).T, ffn_out], axis=0)

    pieces_t = dealt(tokens, "tokens")
    shard_p_other = swap(shard_p, "x")
    if ring:
        own_p, other_p = ring_gather(shard_p, shard_p_other, nd)
        moves, table = [], [jnp.int32(0), x * HEAD, (1 - x) * HEAD, x * DV, (1 - x) * DV]
        for j in range(nd):
            table.append(ring_dp(place_in_ring - j, nd) * w)
            table.append(ring_dp(place_in_ring + j, nd) * w)
            moves.append((j, 0, HEAD, 0, 1, 5 + 2 * j))
            moves.append((j, HEAD, DV, 1, 3, 5 + 2 * j))
            moves.append((j, HEAD + DV, 16, 2, 0, 5 + 2 * j))
            moves.append((nd + j, 0, HEAD, 0, 2, 6 + 2 * j))
            moves.append((nd + j, HEAD, DV, 1, 4, 6 + 2 * j))
        w_in, w_out, w_down = place(
            own_p + other_p,
            moves,
            jnp.stack(table).astype(jnp.int32),
            [sds(2 * HEAD, d, dtype=BF), sds(2 * DV, d, dtype=BF), sds(16, d, dtype=BF)],
            "place_proj",
        )
        half = (3 * f) // 2
        a, b = ring_gather(shard_f[:half], shard_f[half:], nd)
        ax, bx = [swap(p, "x") for p in a], [swap(p, "x") for p in b]
        moves, table = [], [x * f, (1 - x) * f, x * f + f // 2, (1 - x) * f + f // 2]
        for j in range(nd):
            table.append(ring_dp(place_in_ring - j, nd) * w)
            table.append(ring_dp(place_in_ring + j, nd) * w)
            for side in range(2):
                moves.append((side * 2 * nd + j, 0, f, 0, side, 4 + 2 * j))
                moves.append((side * 2 * nd + j, f, f // 2, 1, side, 4 + 2 * j))
                moves.append((side * 2 * nd + nd + j, 0, f // 2, 1, 2 + side, 5 + 2 * j))
                moves.append((side * 2 * nd + nd + j, f // 2, f, 2, side, 5 + 2 * j))
        f_gate, f_up, f_out = place(
            a + b + ax + bx,
            moves,
            jnp.stack(table).astype(jnp.int32),
            [sds(2 * f, d, dtype=BF)] * 3,
            "place_ffn",
        )
    else:

        def gathered(shard):
            return jnp.swapaxes(lax.all_gather(shard, "dp", axis=0), 0, 1).reshape(shard.shape[0], d)

        own_p, other_p = gathered(shard_p), gathered(shard_p_other)
        low = jnp.where(x == 0, own_p, other_p)
        high = jnp.where(x == 0, other_p, own_p)
        w_in = jnp.concatenate([low[:HEAD], high[:HEAD]])
        w_out = jnp.concatenate([low[HEAD : HEAD + DV], high[HEAD : HEAD + DV]])
        w_down = own_p[HEAD + DV :]
        own_f, other_f = gathered(shard_f), gathered(swap(shard_f, "x"))
        low = jnp.where(x == 0, own_f, other_f)
        high = jnp.where(x == 0, other_f, own_f)
        f_gate, f_up, f_out = (
            jnp.concatenate([low[k * f : (k + 1) * f], high[k * f : (k + 1) * f]]) for k in range(3)
        )

    up_own = decay_up.reshape(16, DK)
    up_other = swap(up_own, "x")
    bias_own = decay_bias.reshape(1, DK)
    bias_other = swap(bias_own, "x")

    def both(own, other):
        return jnp.where(
            x == 0, jnp.concatenate([own, other], axis=1), jnp.concatenate([other, own], axis=1)
        )

    up = both(up_own, up_other)
    bias = both(bias_own, bias_other)
    gain_one, gain_two = block_gains[0:1], block_gains[1:2]
    head_row = head_gain.reshape(1, DV)

    def tall(cols, dtype=BF):
        return sds(rows, cols, dtype=dtype)

    nlev = LEVELS + 2
    src, normed_first, qkvg, log_decay, rank, packet = run(
        functools.partial(project_kernel, spans, tiles),
        (tiles,),
        [SMEM] + [rows_spec(quarter)] * 4
        + [whole_spec(1, d), whole_spec(2 * HEAD, d), whole_spec(16, d), whole_spec(16, 2 * DK),
           whole_spec(1, 2 * DK), whole_spec(nlev, TILE, TILE)],
        [rows_spec(d), rows_spec(d), rows_spec(2 * HEAD), rows_spec(2 * DK), rows_spec(16),
         whole_spec(2 * DV + 16, DK)],
        [tall(d), tall(d), tall(2 * HEAD), tall(2 * DK, F32), tall(16), sds(2 * DV + 16, DK)],
        [pltpu.VMEM((2, DV, DK), F32), pltpu.VMEM((8, 2 * DK), F32)],
        "project", 2 * rows * d * 2 * HEAD, rows * d * 10,
    )(span_ints, *pieces_t, gain_one, w_in, w_down, up, bias, ups)

    sequence = nd * 2
    reach = -(-(MAX_SPANS - 1) // spans)
    entering = carried(packet, sequence, reach, True)

    within = run(
        within_kernel, (tiles,),
        [rows_spec(2 * HEAD), rows_spec(2 * DK), whole_spec(nlev, TILE, TILE), whole_spec(TILE, TILE)],
        rows_spec(2 * DV), tall(2 * DV, F32), [],
        "within", rows * 2 * 8 * 256 * 256, rows * 2 * HEAD * 4,
    )(qkvg, log_decay, ups, level)

    mixed, gated, attn, before = run(
        functools.partial(mix_kernel, spans), (tiles,),
        [SMEM, rows_spec(2 * HEAD), rows_spec(2 * DK), rows_spec(2 * DV), whole_spec(2 * DV + 16, DK),
         whole_spec(nlev, TILE, TILE), whole_spec(1, DV), whole_spec(2 * DV, d)],
        [rows_spec(2 * DV), rows_spec(2 * DV), rows_spec(d),
         pl.BlockSpec((TILE // SPAN, 2, DV, DK), lambda i: (i, 0, 0, 0))],
        [tall(2 * DV, F32), tall(2 * DV), tall(d), sds(spans, 2, DV, DK, dtype=BF)],
        [pltpu.VMEM((2, DV, DK), F32)],
        "mix", 2 * rows * d * 2 * DV, rows * d * 10,
    )(span_ints, qkvg, log_decay, within, entering, ups, head_row, w_out)

    pieces_c = dealt(cotangent, "cotangent")
    attn_other = swap(attn, "core")
    ff = 2 * f
    hidden, normed_second, act, grad_gu, cot, keep_out, send_out, grad_second = run(
        ffn_kernel, (tiles,),
        [SMEM] + [rows_spec(d)] * 3 + [rows_spec(quarter)] * 4
        + [whole_spec(1, d), whole_spec(ff, d), whole_spec(ff, d), whole_spec(ff, d)],
        [rows_spec(d), rows_spec(d), rows_spec(ff), rows_spec(2 * ff), rows_spec(d), rows_spec(2 * quarter),
         rows_spec(2 * quarter), rows_spec(d)],
        [tall(d, F32), tall(d), tall(ff), tall(2 * ff), tall(d), tall(2 * quarter), tall(2 * quarter), tall(d)],
        [pltpu.VMEM((TILE, d), BF)],
        "ffn", 2 * rows * d * ff * 6, rows * d * 20 + 6 * ff * d,
    )(ints, src, attn, attn_other, *pieces_c, gain_two, f_gate, f_up, f_out)

    gs_other = swap(grad_second, "core")
    recv_out = swap(send_out, "core")

    if ring:
        own_gu, *other_gu = pl.pallas_call(
            functools.partial(grad_pair_kernel, nd, f),
            in_specs=[SMEM, VMEM, VMEM],
            out_specs=[VMEM] * (nd + 1),
            out_shape=[sds(nd, ff, w, dtype=BF)] + [sds(ff, w, dtype=BF)] * nd,
            scratch_shapes=[pltpu.VMEM((ff, d), BF)],
            name="grad_ffn_in",
            compiler_params=pltpu.CompilerParams(vmem_limit_bytes=VMEM_LIMIT),
            cost_estimate=pl.CostEstimate(
                flops=2 * rows * d * ff * 2, bytes_accessed=30000000, transcendentals=0
            ),
        )(ints, grad_gu, normed_second)
        across_gu = [swap(o, "x") for o in other_gu]

        def gu_term(m, s):
            at = slice(m * f, (m + 1) * f)
            return own_gu[s - 1, at].astype(F32) + across_gu[s - 1][at].astype(F32)

        shard_gate, shard_up = ring_sum(
            functools.partial(gu_term, 0), functools.partial(gu_term, 1), nd
        )

    def blocks(lhs, rhs, f_rows, name):
        n_out = 2 * f_rows
        flops = 2 * rows * d * n_out
        if ring:
            return pl.pallas_call(
                functools.partial(grad_blocks_kernel, nd, f_rows),
                in_specs=[SMEM, VMEM, VMEM],
                out_specs=VMEM,
                out_shape=sds(nd, 2, f_rows, w, dtype=BF),
                scratch_shapes=[pltpu.VMEM((n_out, d), BF)],
                name=name,
                compiler_params=pltpu.CompilerParams(vmem_limit_bytes=VMEM_LIMIT),
                cost_estimate=pl.CostEstimate(
                    flops=flops, bytes_accessed=15000000, transcendentals=0
                ),
            )(ints, lhs, rhs)
        return pl.pallas_call(
            functools.partial(grad_plain_kernel, f_rows),
            in_specs=[SMEM, VMEM, VMEM],
            out_specs=VMEM,
            out_shape=sds(n_out, d, dtype=BF),
            name=name,
            compiler_params=pltpu.CompilerParams(vmem_limit_bytes=VMEM_LIMIT),
            cost_estimate=pl.CostEstimate(flops=flops, bytes_accessed=15000000, transcendentals=0),
        )(ints, lhs, rhs)

    blocks_o = blocks(act, cot, f, "grad_ffn_out")

    def plain_shard(full, f_rows):
        full = jnp.swapaxes(full.reshape(2 * f_rows, nd, w), 0, 1)
        total = lax.psum_scatter(full, "dp", scatter_dimension=0, tiled=True)[0].astype(F32)
        keep_rows = lax.dynamic_slice_in_dim(total, x * f_rows, f_rows)
        give_rows = lax.dynamic_slice_in_dim(total, (1 - x) * f_rows, f_rows)
        return keep_rows + swap(give_rows, "x")

    def ring_shard(first, second):
        a, b = ring_sum(first, second, nd)
        give = jnp.where(x == 0, b, a).astype(BF)
        return jnp.where(x == 0, a, b) + swap(give, "x").astype(F32)

    if ring:
        shard_fo = ring_shard(lambda s: blocks_o[s - 1, 0], lambda s: blocks_o[s - 1, 1])
    else:
        shard_fo = plain_shard(blocks_o, f)
        shard_gate = plain_shard(blocks(grad_gu[:, :ff], normed_second, f, "grad_gate"), f)
        shard_up = plain_shard(blocks(grad_gu[:, ff:], normed_second, f, "grad_up"), f)

    w_out_shape = sds(nd, 2, DV, w, dtype=BF) if ring else sds(2 * DV, d, dtype=BF)
    grad_hidden, grad_mixed, grad_gate, blocks_po, gain_second, head_part, packet_back = run(
        functools.partial(out_back_kernel, spans, tiles, nd if ring else None), (tiles,),
        [SMEM] + [rows_spec(d, tiles)] * 4
        + [whole_spec(1, d), whole_spec(2 * DV, d), rows_spec(2 * DV, tiles), rows_spec(2 * DV, tiles),
           rows_spec(2 * HEAD, tiles), rows_spec(2 * DK, tiles), whole_spec(1, DV), whole_spec(nlev, TILE, TILE)],
        [rows_spec(d, tiles), rows_spec(2 * DV, tiles), rows_spec(2 * DV, tiles), whole_spec(*w_out_shape.shape),
         whole_spec(8, d), whole_spec(8, DV), whole_spec(2 * DV, DK)],
        [tall(d, F32), tall(2 * DV), tall(2 * DV), w_out_shape, sds(8, d), sds(8, DV), sds(2 * DV, DK)],
        [pltpu.VMEM((2 * DV, d), F32), pltpu.VMEM((2, DV, DK), F32), pltpu.VMEM((8, d), F32), pltpu.VMEM((8, DV), F32)],
        "out_back", 2 * rows * d * 2 * DV * 2, rows * d * 24,
    )(ints, hidden, cot, grad_second, gs_other, gain_two, w_out, gated, mixed, qkvg, log_decay, head_row, ups)

    packet_back = jnp.concatenate([packet_back, packet[2 * DV :]], axis=0)
    leaving = carried(packet_back, sequence, reach, False)

    grad_qk, grad_v, grad_ld = run(
        within_back_kernel, (tiles,),
        [rows_spec(2 * HEAD), rows_spec(2 * DK), rows_spec(2 * DV), whole_spec(nlev, TILE, TILE),
         whole_spec(nlev, TILE, TILE), whole_spec(TILE, TILE), whole_spec(TILE, TILE)],
        [rows_spec(4 * DK), rows_spec(2 * DV), rows_spec(2 * DK)],
        [tall(4 * DK, F32), tall(2 * DV, F32), tall(2 * DK, F32)], [],
        "within_back", rows * 2 * 30 * 256 * 256, rows * 2 * HEAD * 6,
    )(qkvg, log_decay, grad_mixed, ups, downs, level, level_t)

    grad_project, grad_first, rank_part, up_grad, bias_grad = run(
        functools.partial(project_back_kernel, tiles), (tiles,),
        [SMEM, rows_spec(2 * HEAD, tiles), rows_spec(2 * DK, tiles), rows_spec(2 * DV, tiles),
         pl.BlockSpec((TILE // SPAN, 2, DV, DK), lambda i: (tiles - 1 - i, 0, 0, 0)), whole_spec(2 * DV + 16, DK),
         rows_spec(4 * DK, tiles), rows_spec(2 * DV, tiles), rows_spec(2 * DK, tiles), rows_spec(2 * DV, tiles),
         rows_spec(16, tiles), whole_spec(16, 2 * DK), whole_spec(1, 2 * DK), whole_spec(nlev, TILE, TILE),
         whole_spec(nlev, TILE, TILE), whole_spec(2 * HEAD, d)],
        [rows_spec(2 * HEAD, tiles), rows_spec(d, tiles), pl.BlockSpec((16, TILE), lambda i: (0, tiles - 1 - i)),
         whole_spec(16, 2 * DK), whole_spec(8, 2 * DK)],
        [tall(2 * HEAD), tall(d), sds(16, rows), sds(16, 2 * DK), sds(8, 2 * DK)],
        [pltpu.VMEM((2, DV, DK), F32), pltpu.VMEM((16, 2 * DK), F32), pltpu.VMEM((8, 2 * DK), F32),
         pltpu.VMEM((TILE, 2 * DK), BF), pltpu.VMEM((TILE, 2 * DK), BF), pltpu.VMEM((TILE, 2 * DK), F32)],
        "project_back", 2 * rows * d * 2 * HEAD, rows * d * 20,
    )(ints, qkvg, log_decay, grad_mixed, before, leaving, grad_qk, grad_v, grad_ld, grad_gate, rank, up, bias,
      ups, downs, w_in)

    gf_other = swap(grad_first, "core")
    rank_other = swap(rank_part, "core")
    blocks_pi = blocks(grad_project, normed_first, HEAD, "grad_proj_in")
    if ring:

        def p_term(h, s):
            return jnp.concatenate([blocks_pi[s - 1, h], blocks_po[s - 1, h]], axis=0)

        shard_pg = ring_shard(functools.partial(p_term, 0), functools.partial(p_term, 1))
        shard_pi, shard_po = shard_pg[:HEAD], shard_pg[HEAD:]
    else:
        shard_pi = plain_shard(blocks_pi, HEAD)
        shard_po = plain_shard(blocks_po, DV)

    grad_own, grad_cross, down_grad, gain_first = run(
        functools.partial(source_back_kernel, tiles), (tiles,),
        [SMEM] + [rows_spec(d)] * 4 + [pl.BlockSpec((16, TILE), lambda i: (0, i))] * 2
        + [whole_spec(16, d), whole_spec(1, d), rows_spec(d)],
        [rows_spec(quarter), rows_spec(quarter), whole_spec(16, d), whole_spec(8, d)],
        [tall(quarter), tall(quarter), sds(16, d), sds(8, d)],
        [pltpu.VMEM((TILE, d), BF), pltpu.VMEM((16, d), F32), pltpu.VMEM((8, d), F32)],
        "source_back", 2 * rows * d * 64, rows * d * 16,
    )(ints, src, normed_first, grad_first, gf_other, rank_part, rank_other, w_down, gain_one, grad_hidden)

    out_own, out_cross = run(
        block_out_kernel, (tiles,),
        [SMEM, rows_spec(d), rows_spec(2 * quarter), rows_spec(2 * quarter)],
        [rows_spec(quarter)] * 2, [tall(quarter)] * 2, [],
        "block_out", 0, rows * d * 8,
    )(ints, hidden, keep_out, recv_out)

    def undealt(own, cross, name):
        joined = join_pick(own, swap(cross, "x"), back_local, x, name + "_join")
        return lax.all_to_all(joined, "dp", split_axis=0, concat_axis=0, tiled=True)

    back_out = undealt(out_own, out_cross, "block_out")
    block_out = home([back_out], home_slot, [jnp.int32(0)], "block_out_home")
    back_grad = undealt(grad_own, grad_cross, "token_grad")
    back_x = swap(back_grad, "x")
    token_grad = home(
        [back_grad, back_x, swap(back_grad, "core"), swap(back_x, "core")],
        home_slot,
        [quarters[k] * quarter for k in range(4)],
        "token_grad_home",
    )

    small = jnp.concatenate(
        [
            gain_first[0].reshape(-1, 128),
            gain_second[0].reshape(-1, 128),
            down_grad.reshape(-1, 128),
            up_grad.reshape(-1, 128),
            bias_grad[0].reshape(-1, 128),
            head_part[0].reshape(-1, 128),
        ],
        axis=0,
    )
    small = all_sum(small, ("x", "dp"), (2, nd))
    rows_d = d // 128
    cuts = [rows_d, rows_d, 16 * rows_d, 32, 2, 2]
    starts = [sum(cuts[:k]) for k in range(len(cuts) + 1)]
    gain_first, gain_second, down_total, up_total, bias_total, head_total = (
        small[starts[k] : starts[k + 1]].reshape(-1) for k in range(len(cuts))
    )
    head_total = head_total + swap(head_total, "core")
    gains_total = jnp.stack([gain_first, gain_second])
    down_total = down_total.reshape(16, d)
    shard_down = lax.dynamic_slice_in_dim(down_total, dp * w, w, 1).T
    up_total = up_total.reshape(16, 2, DK)
    up_total = jnp.where(x == 0, up_total[:, 0:1], up_total[:, 1:2])
    bias_total = bias_total.reshape(2, DK)
    bias_total = jnp.where(x == 0, bias_total[0:1], bias_total[1:2])

    shard_in = shard_pi.T.reshape(proj_in.shape)
    shard_out = shard_po.reshape(proj_out.shape)
    shard_ffn_in = jnp.stack([shard_gate.T, shard_up.T], axis=1)
    shard_ffn_out = shard_fo
    n_dev = 4 * nd
    local_sq = (
        square_sum(shard_pi)
        + square_sum(shard_po)
        + square_sum(shard_gate)
        + square_sum(shard_up)
        + square_sum(shard_fo)
        + square_sum(shard_down) / 4
        + (square_sum(up_total) + square_sum(bias_total)) / nd
        + (square_sum(head_total) + square_sum(gains_total)) / n_dev
    )
    norm_sq = all_sum(jnp.broadcast_to(local_sq, (8, 128)), ("core", "x", "dp"), (2, 2, nd))
    grad_norm = jnp.sqrt(norm_sq[0, 0])
    clip_norm = clip_scale * math.sqrt(PARAMS)
    factor = jnp.minimum(1.0, clip_norm / (grad_norm + 1e-06))
    update_in = adam_update(proj_in, shard_in, first_proj_in, second_proj_in, factor, weight_decay)
    update_down = adam_update(decay_down, shard_down, first_decay_down, second_decay_down, factor, weight_decay)
    update_up = adam_update(decay_up, up_total, first_decay_up, second_decay_up, factor, weight_decay)
    update_bias = adam_update(decay_bias, bias_total, first_decay_bias, second_decay_bias, factor, 0.0)
    update_head = adam_update(head_gain, head_total, first_head_gain, second_head_gain, factor, 0.0)
    update_out = adam_update(proj_out, shard_out, first_proj_out, second_proj_out, factor, weight_decay)
    update_gains = adam_update(block_gains, gains_total, first_block_gains, second_block_gains, factor, 0.0)
    update_ffn_in = adam_update(ffn_in, shard_ffn_in, first_ffn_in, second_ffn_in, factor, weight_decay)
    update_ffn_out = adam_update(ffn_out, shard_ffn_out, first_ffn_out, second_ffn_out, factor, weight_decay)
    return (
        block_out, token_grad, grad_norm, *update_in, *update_down, *update_up, *update_bias, *update_head,
        *update_out, *update_gains, *update_ffn_in, *update_ffn_out,
    )


def solution(mesh):
    nd, nt = mesh.shape["dp"], mesh.shape["tensor"]
    fine = Mesh(mesh.devices.reshape(nd, nt // 2, 2), ("dp", "x", "core"))
    t = ("x", "core")
    w_specs = {
        "proj_in": P("dp", t, None),
        "decay_down": P("dp", None),
        "decay_up": P(None, t, None),
        "decay_bias": P(t, None),
        "head_gain": P(),
        "proj_out": P(t, None, "dp"),
        "block_gains": P(),
        "ffn_in": P("dp", None, t),
        "ffn_out": P(t, "dp"),
    }
    specs = list(w_specs.values())
    placed = [P("dp", None), P("dp", None), P(), P()] + specs
    results = [P("dp", t), P("dp", None), P()]
    for spec in specs:
        placed += [spec] * 2
        results += [spec] * 4
    return jax.shard_map(
        on_device,
        mesh=fine,
        in_specs=tuple(placed),
        out_specs=tuple(results),
        check_vma=False,
    )
```

time: 2100 us -> 803 us (0.38)
  waiting for transfers between devices: 807 us -> 243 us
  other arithmetic: 447 us -> 83.8 us
  blocking collectives: 327 us -> 0 us
  Pallas kernels: 0 us -> 226 us
  matrix products: 213 us -> 0 us
  local copies, waits for them, and re-layouts: 244 us -> 39.9 us
  starting transfers between devices: 24.5 us -> 188 us
    reduce_scatter x7 -> x0, waiting for transfers between devices: 462 us -> none  [the longest x1 113 us: on_device(): lax.psum_scatter(grad_ffn_in, 'dp', scatter_dimension=0, tiled=True)]
    all_gather x6 -> x0, blocking collectives: 280 us -> none  [the longest x1 152 us: on_device(): lax.all_gather(decay_down, 'dp', axis=0, tiled=True)]
    ppermute x0 -> x133, waiting for transfers between devices: none -> 243 us  [the longest x46 99.2 us: swap(): return lax.ppermute(value, axis, [(0, 1), (1, 0)])]
    pallas_call x0 -> x22, Pallas kernels: none -> 226 us  [the longest x1 34.3 us: on_device(): run(ffn_kernel, (tiles,), [SMEM] + [rows_spec(d)] * 3 + [rows_spec(quarte...]
    dot_general x20 -> x0, other arithmetic: 224 us -> none  [the longest x5 70.3 us: span_forward(): jnp.einsum('nthk,nshk,ntshk->nhts', query_rows, key_rows, decays, precisi...]
    dot_general x55 -> x0, matrix products: 213 us -> none  [the longest x5 16.6 us: span_backward(): jnp.einsum('nthv,nhkv->nthk', grad_mix, previous_state, precision=highest...]
    all_to_all x4, waiting for transfers between devices: 169 us -> 0.01 us  [the longest x2 0.01 us: undealt(): return lax.all_to_all(joined, 'dp', split_axis=0, concat_axis=0, tiled=True)]
    ppermute x0 -> x133, starting transfers between devices: none -> 167 us  [the longest x21 33.9 us: ring_sum(): a = lax.ppermute(a, 'dp', forward).astype(F32) + first(s + 1).astype(F32)]
  transfers between devices with their start and end apart: 17 -> 137, of which waited for: 12 -> 54; matrix products, arithmetic and copies ran while one was open for 8% -> 14% of each run, Pallas kernels for 0% -> 23%
where the time goes in v1:
time: 803 us; the launch traced here: 792 us
  waiting for transfers between devices  243 us (30%)
  Pallas kernels  226 us (28%)
  starting transfers between devices  188 us (23%)
  other arithmetic  83.8 us (10%)
  local copies, waits for them, and re-layouts  39.9 us (5%)
  between operations  11.1 us (1%)
    ppermute x46, waiting for transfers between devices, swap(): return lax.ppermute(value, axis, [(0, 1), (1, 0)])  99.2 us
    pallas_call x1, Pallas kernels, on_device(): run(ffn_kernel, (tiles,), [SMEM] + [rows_spec(d)] * 3 + [rows_spec(quarte...  34.3 us
    ppermute x21, starting transfers between devices, ring_sum(): a = lax.ppermute(a, 'dp', forward).astype(F32) + first(s + 1).astype(F32)  33.9 us
    ppermute x21, waiting for transfers between devices, ring_sum(): a = lax.ppermute(a, 'dp', forward).astype(F32) + first(s + 1).astype(F32)  32.7 us
    ppermute x14, waiting for transfers between devices, ring_gather(): ahead.append(lax.ppermute(ahead[-1], 'dp', forward))  28.8 us
    ppermute x14, starting transfers between devices, ring_gather(): ahead.append(lax.ppermute(ahead[-1], 'dp', forward))  27.5 us
    ppermute x14, waiting for transfers between devices, ring_gather(): behind.append(lax.ppermute(behind[-1], 'dp', backward))  27.3 us
    ppermute x46, starting transfers between devices, swap(): return lax.ppermute(value, axis, [(0, 1), (1, 0)])  25 us
  transfers between devices with their start and end apart: 137, of which 54 were waited for; matrix products, arithmetic and copies ran while one was open for 14% of the time, Pallas kernels for 23%

profile of v1, /device:TPU:0, one launch (start us, length us, event | category | flops | bytes accessed | tf_op | source)
XLA Modules:
  0.0 791.7 jit_solution(10570573580684667213)
XLA Ops:
  24.6 17.9 %collective-permute-done.11.refs_9_ = bf16[1040,128]{1,0:T(8,128)(2,1)} collective-permute-done((bf16[1040,128]{1,0:T(8,128)(2,1)}, bf16[1040,128]{1,0:T(8,128)(2,1)}, u32[]{:S(2)}, u32[]{:S(2)}) %collective-permute-start.11) | collective-permute-done | bytes 266272 | tf_op jit(solution)/shard_map/ppermute | solution.py:736
  47.9 9.1 %collective-permute-start.5 = (bf16[1040,128]{1,0:T(8,128)(2,1)}, bf16[1040,128]{1,0:T(8,128)(2,1)}, u32[]{:S(2)}, u32[]{:S(2)}) collective-permute-start(bf16[1040,128]{1,0:T(8,128)(2,1)} %collective-permute-done.4.refs_2_), channel_id=1, source_target_pairs={{0,8},{8,16},{16,24},{24,28},{28,20},{20,12},{12,4},{4,0},{1,9},{9... | collective-permute-start | bytes 798728 | tf_op jit(solution)/shard_map/ppermute | solution.py:735
  78.1 20.1 %collective-permute-done.6.refs_4_ = bf16[1040,128]{1,0:T(8,128)(2,1)S(1)} collective-permute-done((bf16[1040,128]{1,0:T(8,128)(2,1)}, bf16[1040,128]{1,0:T(8,128)(2,1)S(1)}, u32[]{:S(2)}, u32[]{:S(2)}) %collective-permute-start.6) | collective-permute-done | bytes 266272 | tf_op jit(solution)/shard_map/ppermute | solution.py:735
  98.2 8.5 %collective-permute-start.7 = (bf16[1040,128]{1,0:T(8,128)(2,1)S(1)}, bf16[1040,128]{1,0:T(8,128)(2,1)S(1)}, u32[]{:S(2)}, u32[]{:S(2)}) collective-permute-start(bf16[1040,128]{1,0:T(8,128)(2,1)S(1)} %collective-permute-done.6.refs_4_), channel_id=1, source_target_pairs={{0,8},{8,16},{16,24},{24,28},{28,20},{20,12},{12,4},{4,0},{1,9},{9... | collective-permute-start | bytes 798728 | tf_op jit(solution)/shard_map/ppermute | solution.py:735
  136.1 14.3 %project.1 = (bf16[1280,1024]{1,0:T(8,128)(2,1)}, bf16[1280,1024]{1,0:T(8,128)(2,1)}, bf16[1280,1536]{1,0:T(8,128)(2,1)}, f32[1280,256]{1,0:T(8,128)}, bf16[1280,16]{1,0:T(8,128)(2,1)}, /*index=5*/f32[528,128]{1,0:T(8,128)}) custom-call(s32[24]{0:T(128)} %concatenate.139.ints, bf16[1280,256]{1,0:T(8,128)(2,1)} %get-tuple-element.97.q0, ...), custom_call_target="tpu_custom_call" | custom-call | flops 4026531840 | bytes 13107200 | tf_op jit(solution)/shard_map/project/pallas_call | solution.py:924
  178.7 9.7 %within.1 = f32[1280,512]{1,0:T(8,128)} custom-call(bf16[1280,1536]{1,0:T(8,128)(2,1)} %get-tuple-element.102.qkvg, f32[1280,256]{1,0:T(8,128)} %get-tuple-element.103.log_decay, bf16[8,256,256]{2,1,0:T(8,128)(2,1)} %copy.88.ups, s32[256,256]{1,0:T(8,128)} %get-tuple-element.355.level), custom_call_target="tpu_custom_call" | custom-call | flops 1342177280 | bytes 7864320 | tf_op jit(solution)/shard_map/within/pallas_call | solution.py:941
  189.4 10.0 %mix.1 = (f32[1280,512]{1,0:T(8,128)}, bf16[1280,512]{1,0:T(8,128)(2,1)}, bf16[1280,1024]{1,0:T(8,128)(2,1)}, bf16[20,2,256,128]{3,2,1,0:T(8,128)(2,1)}) custom-call(s32[24]{0:T(128)} %concatenate.139.ints, bf16[1280,1536]{1,0:T(8,128)(2,1)} %get-tuple-element.102.qkvg, f32[1280,256]{1,0:T(8,128)} %get-tuple-element.103.log_decay, f32[1280,512]{1,0:T(8,128)} %within.1, ...), custom_call_target="tpu_custom_call" | custom-call | flops 1342177280 | bytes 13107200 | tf_op jit(solution)/shard_map/mix/pallas_call | solution.py:948
  266.6 17.5 %collective-permute-done.47.refs_21_ = bf16[1056,128]{1,0:T(8,128)(2,1)S(1)} collective-permute-done((bf16[1056,128]{1,0:T(8,128)(2,1)}, bf16[1056,128]{1,0:T(8,128)(2,1)S(1)}, u32[]{:S(2)}, u32[]{:S(2)}) %collective-permute-start.47) | collective-permute-done | bytes 270368 | tf_op jit(solution)/shard_map/ppermute | solution.py:800
  291.7 6.9 collective-permute-done.48.refs_22_
  314.6 8.3 %place_ffn.1 = (bf16[1408,1024]{1,0:T(8,128)(2,1)}, bf16[1408,1024]{1,0:T(8,128)(2,1)}, bf16[1408,1024]{1,0:T(8,128)(2,1)}) custom-call(s32[20]{0:T(128)} %stack.176.ints, bf16[1056,128]{1,0:T(8,128)(2,1)} %get-tuple-element.350.refs_0_, bf16[1056,128]{1,0:T(8,128)(2,1)} %copy-done.33, bf16[1056,128]{1,0:T(8,128)(2,1)} %copy-done.37, ...), custom_call_target="tpu_custom_call" | custom-call | bytes 17301504 | tf_op jit(solution)/shard_map/place_ffn/pallas_call | solution.py:717
  322.9 34.3 %ffn.1 = (f32[1280,1024]{1,0:T(8,128)}, bf16[1280,1024]{1,0:T(8,128)(2,1)}, bf16[1280,1408]{1,0:T(8,128)(2,1)}, bf16[1280,2816]{1,0:T(8,128)(2,1)}, bf16[1280,10...) custom-call(s32[27]{0:T(128)} %concatenate.138.ints, ...), custom_call_target="tpu_custom_call" | custom-call | flops 22145925120 | bytes 34865152 | tf_op jit(solution)/shard_map/ffn/pallas_call | solution.py:962
  357.3 19.8 %grad_ffn_in.1 = (bf16[8,1408,128]{2,1,0:T(8,128)(2,1)}, bf16[1408,128]{1,0:T(8,128)(2,1)}, bf16[1408,128]{1,0:T(8,128)(2,1)}, bf16[1408,128]{1,0:T(8,128)(2,1)}...) custom-call(s32[27]{0:T(128)} %concatenate.138.ints, ...), custom_call_target="tpu_custom_call" | custom-call | flops 7381975040 | bytes 30000000 | tf_op jit(solution)/shard_map/grad_ffn_in/pallas_call | solution.py:977
  377.6 11.3 %grad_ffn_out.1 = bf16[8,2,704,128]{3,2,1,0:T(8,128)(2,1)} custom-call(s32[27]{0:T(128)} %concatenate.138.ints, bf16[1280,1408]{1,0:T(8,128)(2,1)} %get-tuple-element.148.lhs, bf16[1280,1024]{1,0:T(8,128)(2,1)} %get-tuple-element.118.cot.rhs), custom_call_target="tpu_custom_call" | custom-call | flops 3690987520 | bytes 15000000 | tf_op jit(solution)/shard_map/grad_ffn_out/pallas_call | solution.py:1003
  424.3 17.1 %out_back.1 = (f32[1280,1024]{1,0:T(8,128)}, bf16[1280,512]{1,0:T(8,128)(2,1)}, bf16[1280,512]{1,0:T(8,128)(2,1)}, bf16[8,2,256,128]{3,2,1,0:T(8,128)(2,1)}, f32...) custom-call(s32[27]{0:T(128)} %concatenate.138.ints, f32[1280,1024]{1,0:T(8,128)} %get-tuple-element.112.hidden, ...), custom_call_target="tpu_custom_call" | custom-call | flops 2684354560 | bytes 31457280 | tf_op jit(solution)/shard_map/out_back/pallas_call | solution.py:1047
  452.4 21.9 %within_back.1 = (f32[1280,512]{1,0:T(8,128)}, f32[1280,512]{1,0:T(8,128)}, f32[1280,256]{1,0:T(8,128)}) custom-call(bf16[1280,1536]{1,0:T(8,128)(2,1)} %get-tuple-element.102.qkvg, f32[1280,256]{1,0:T(8,128)} %get-tuple-element.103.log_decay, bf16[1280,512]{1,0:T(8,128)(2,1)} %get-tuple-element.122.grad_mixed, bf16[8,256,256]{2,1,0:T(8,128)(2,1)} %copy.88.ups, ...), custom_call_target="tpu_custom_call" | custom-call | flops 5033164800 | bytes 11796480 | tf_op jit(solution)/shard_map/within_back/pallas_call | solution.py:1062
  488.7 17.5 %project_back.1 = (bf16[1280,1536]{1,0:T(8,128)(2,1)}, bf16[1280,1024]{1,0:T(8,128)(2,1)}, f32[16,1280]{1,0:T(8,128)}, f32[16,256]{1,0:T(8,128)}, f32[8,256]{1,0:T(8,128)}) custom-call(s32[27]{0:T(128)} %concatenate.138.ints, bf16[1280,1536]{1,0:T(8,128)(2,1)} %get-tuple-element.102.qkvg, f32[1280,256]{1,0:T(8,128)} %get-tuple-element.103.log_decay, ...), custom_call_target="tpu_custom_call" | custom-call | flops 4026531840 | bytes 26214400 | tf_op jit(solution)/shard_map/project_back/pallas_call | solution.py:1071
  506.2 12.1 %grad_proj_in.1 = bf16[8,2,768,128]{3,2,1,0:T(8,128)(2,1)} custom-call(s32[27]{0:T(128)} %concatenate.138.ints, bf16[1280,1536]{1,0:T(8,128)(2,1)} %get-tuple-element.135.lhs, bf16[1280,1024]{1,0:T(8,128)(2,1)} %get-tuple-element.117.normed.rhs), custom_call_target="tpu_custom_call" | custom-call | flops 4026531840 | bytes 15000000 | tf_op jit(solution)/shard_map/grad_proj_in/pallas_call | solution.py:1003
  569.7 9.3 %source_back.1 = (bf16[1280,256]{1,0:T(8,128)(2,1)}, bf16[1280,256]{1,0:T(8,128)(2,1)}, f32[16,1024]{1,0:T(8,128)}, f32[8,1024]{1,0:T(8,128)}) custom-call(s32[27]{0:T(128)} %concatenate.138.ints, bf16[1280,1024]{1,0:T(8,128)(2,1)} %get-tuple-element.101.src, bf16[1280,1024]{1,0:T(8,128)(2,1)} %get-tuple-element.117.normed.rhs, ...), custom_call_target="tpu_custom_call" | custom-call | flops 167772160 | bytes 20971520 | tf_op jit(solution)/shard_map/source_back/pallas_call | solution.py:1101
  587.7 9.2 %collective-permute-done.67.other = bf16[1280,256]{1,0:T(8,128)(2,1)S(1)} collective-permute-done((bf16[1280,256]{1,0:T(8,128)(2,1)}, bf16[1280,256]{1,0:T(8,128)(2,1)S(1)}, u32[]{:S(2)}, u32[]{:S(2)}) %collective-permute-start.67) | collective-permute-done | bytes 655392 | tf_op jit(solution)/shard_map/ppermute | solution.py:800
  614.4 18.8 %collective-permute-done.76 = bf16[1024,128]{1,0:T(8,128)(2,1)S(1)} collective-permute-done((bf16[1024,128]{1,0:T(8,128)(2,1)S(1)}, bf16[1024,128]{1,0:T(8,128)(2,1)S(1)}, u32[]{:S(2)}, u32[]{:S(2)}) %collective-permute-start.76) | collective-permute-done | bytes 262176 | tf_op jit(solution)/shard_map/ppermute | solution.py:744
  635.1 7.2 collective-permute-start.97
  666.4 6.9 collective-permute-done.122
  713.4 11.6 %collective-permute-done.126 = f32[180,128]{1,0:T(8,128)} collective-permute-done((f32[180,128]{1,0:T(8,128)}, f32[180,128]{1,0:T(8,128)}, u32[]{:S(2)}, u32[]{:S(2)}) %collective-permute-start.126) | collective-permute-done | bytes 92192 | tf_op jit(solution)/shard_map/ppermute | solution.py:779
  782.5 7.7 token_grad_home.1
  (656 shorter events, 453.8 us)
Async XLA Ops:
  14.4 52.0 %all-to-all-start = ((bf16[8,320,256]{2,1,0:T(8,128)(2,1)}), bf16[8,320,256]{2,1,0:T(8,128)(2,1)S(1)}, u32[]{:S(2)}, u32[]{:S(2)}) async-start(bf16[8,320,256]{2,1,0:T(8,128)(2,1)} %bitcast.337), calls=%async_computation | async-start | bytes 2621440 | tf_op jit(solution)/shard_map/all_to_all | solution.py:839
  19.4 106.1 %collective-permute-start.19 = (f32[1,128]{1,0:T(1,128)S(1)}, f32[1,128]{1,0:T(1,128)S(1)}, u32[]{:S(2)}, u32[]{:S(2)}) collective-permute-start(f32[1,128]{1,0:T(1,128)S(1)} %copy-done.93), channel_id=1, source_target_pairs={{0,2},{2,0},{1,3},{3,1},{4,6},{6,4},{5,7},{7,5},{8,10},{10,8},{9,1... | collective-permute-start | bytes 1544 | tf_op jit(solution)/shard_map/ppermute | solution.py:800
  66.4 187.1 %all-to-all-start.1 = ((bf16[8,320,256]{2,1,0:T(8,128)(2,1)}), bf16[8,320,256]{2,1,0:T(8,128)(2,1)S(1)}, u32[]{:S(2)}, u32[]{:S(2)}) async-start(bf16[8,320,256]{2,1,0:T(8,128)(2,1)} %bitcast.336), calls=%async_computation.1 | async-start | bytes 2621440 | tf_op jit(solution)/shard_map/all_to_all | solution.py:839
  74.7 32.1 %collective-permute-start = (bf16[1280,256]{1,0:T(8,128)(2,1)}, bf16[1280,256]{1,0:T(8,128)(2,1)}, u32[]{:S(2)}, u32[]{:S(2)}) collective-permute-start(bf16[1280,256]{1,0:T(8,128)(2,1)} %get-tuple-element.98), channel_id=1, source_target_pairs={{0,2},{2,0},{1,3},{3,1},{4,6},{6,4},{5,7},{7,5},{8,10},{10,8},{9,1... | collective-permute-start | bytes 1966088 | tf_op jit(solution)/shard_map/ppermute | solution.py:800
  77.2 29.5 %collective-permute-start.14 = (bf16[1040,128]{1,0:T(8,128)(2,1)}, bf16[1040,128]{1,0:T(8,128)(2,1)S(1)}, u32[]{:S(2)}, u32[]{:S(2)}) collective-permute-start(bf16[1040,128]{1,0:T(8,128)(2,1)} %collective-permute-done.13.refs_11_), channel_id=1, source_target_pairs={{8,0},{16,8},{24,16},{28,24},{20,28},{12,20},{4,12},{0,4},{9,1},{1... | collective-permute-start | bytes 798728 | tf_op jit(solution)/shard_map/ppermute | solution.py:736
  106.7 29.3 %collective-permute-start.1 = (bf16[1280,256]{1,0:T(8,128)(2,1)}, bf16[1280,256]{1,0:T(8,128)(2,1)}, u32[]{:S(2)}, u32[]{:S(2)}) collective-permute-start(bf16[1280,256]{1,0:T(8,128)(2,1)} %get-tuple-element.97.q0), channel_id=1, source_target_pairs={{0,1},{1,0},{2,3},{3,2},{4,5},{5,4},{6,7},{7,6},{8,9},{9,8},{10,11... | collective-permute-start | bytes 1966088 | tf_op jit(solution)/shard_map/ppermute | solution.py:800
  129.1 75.8 %collective-permute-start.28 = (bf16[1056,128]{1,0:T(8,128)(2,1)}, bf16[1056,128]{1,0:T(8,128)(2,1)S(1)}, u32[]{:S(2)}, u32[]{:S(2)}) collective-permute-start(bf16[1056,128]{1,0:T(8,128)(2,1)} %get-tuple-element.350.refs_0_), channel_id=1, source_target_pairs={{0,8},{8,16},{16,24},{24,28},{28,20},{20,12},{12,4},{4,0},{1,9},{9... | collective-permute-start | bytes 811016 | tf_op jit(solution)/shard_map/ppermute | solution.py:735
  199.4 123.5 %collective-permute-start.24 = (bf16[1280,1024]{1,0:T(8,128)(2,1)}, bf16[1280,1024]{1,0:T(8,128)(2,1)}, u32[]{:S(2)}, u32[]{:S(2)}) collective-permute-start(bf16[1280,1024]{1,0:T(8,128)(2,1)} %get-tuple-element.106.attn_a), channel_id=1, source_target_pairs={{0,1},{1,0},{2,3},{3,2},{4,5},{5,4},{6,7},{7,6},{8,9},{9,8},{10,11... | collective-permute-start | bytes 7864328 | tf_op jit(solution)/shard_map/ppermute | solution.py:800
  257.1 34.1 %collective-permute-start.25 = (bf16[1280,256]{1,0:T(8,128)(2,1)}, bf16[1280,256]{1,0:T(8,128)(2,1)}, u32[]{:S(2)}, u32[]{:S(2)}) collective-permute-start(bf16[1280,256]{1,0:T(8,128)(2,1)} %get-tuple-element.108), channel_id=1, source_target_pairs={{0,2},{2,0},{1,3},{3,1},{4,6},{6,4},{5,7},{7,5},{8,10},{10,8},{9,1... | collective-permute-start | bytes 1966088 | tf_op jit(solution)/shard_map/ppermute | solution.py:800
  291.2 31.6 %collective-permute-start.26 = (bf16[1280,256]{1,0:T(8,128)(2,1)}, bf16[1280,256]{1,0:T(8,128)(2,1)}, u32[]{:S(2)}, u32[]{:S(2)}) collective-permute-start(bf16[1280,256]{1,0:T(8,128)(2,1)} %get-tuple-element.107.c0), channel_id=1, source_target_pairs={{0,1},{1,0},{2,3},{3,2},{4,5},{5,4},{6,7},{7,6},{8,9},{9,8},{10,11... | collective-permute-start | bytes 1966088 | tf_op jit(solution)/shard_map/ppermute | solution.py:800
  291.2 31.6 %collective-permute-start.27 = (bf16[1280,256]{1,0:T(8,128)(2,1)}, bf16[1280,256]{1,0:T(8,128)(2,1)}, u32[]{:S(2)}, u32[]{:S(2)}) collective-permute-start(bf16[1280,256]{1,0:T(8,128)(2,1)} %collective-permute-done.25.c1), channel_id=1, source_target_pairs={{0,1},{1,0},{2,3},{3,2},{4,5},{5,4},{6,7},{7,6},{8,9},{9,8},{10,11... | collective-permute-start | bytes 1966088 | tf_op jit(solution)/shard_map/ppermute | solution.py:800
  357.2 65.8 %collective-permute-start.60 = (bf16[1280,1024]{1,0:T(8,128)(2,1)}, bf16[1280,1024]{1,0:T(8,128)(2,1)}, u32[]{:S(2)}, u32[]{:S(2)}) collective-permute-start(bf16[1280,1024]{1,0:T(8,128)(2,1)} %get-tuple-element.119.gs_a), channel_id=1, source_target_pairs={{0,1},{1,0},{2,3},{3,2},{4,5},{5,4},{6,7},{7,6},{8,9},{9,8},{10,11... | collective-permute-start | bytes 7864328 | tf_op jit(solution)/shard_map/ppermute | solution.py:800
  398.0 44.5 %collective-permute-start.90 = (bf16[1408,128]{1,0:T(8,128)(2,1)}, bf16[1408,128]{1,0:T(8,128)(2,1)S(1)}, u32[]{:S(2)}, u32[]{:S(2)}) collective-permute-start(bf16[1408,128]{1,0:T(8,128)(2,1)} %get-tuple-element.142), channel_id=1, source_target_pairs={{0,2},{2,0},{1,3},{3,1},{4,6},{6,4},{5,7},{7,5},{8,10},{10,8},{9,1... | collective-permute-start | bytes 1081352 | tf_op jit(solution)/shard_map/ppermute | solution.py:800
  408.4 127.1 %collective-permute-start.92 = (bf16[1408,128]{1,0:T(8,128)(2,1)}, bf16[1408,128]{1,0:T(8,128)(2,1)}, u32[]{:S(2)}, u32[]{:S(2)}) collective-permute-start(bf16[1408,128]{1,0:T(8,128)(2,1)} %get-tuple-element.143), channel_id=1, source_target_pairs={{0,2},{2,0},{1,3},{3,1},{4,6},{6,4},{5,7},{7,5},{8,10},{10,8},{9,1... | collective-permute-start | bytes 1081352 | tf_op jit(solution)/shard_map/ppermute | solution.py:800
  423.0 100.7 %collective-permute-start.118 = (bf16[704,128]{1,0:T(8,128)(2,1)}, bf16[704,128]{1,0:T(8,128)(2,1)}, u32[]{:S(2)}, u32[]{:S(2)}) collective-permute-start(bf16[704,128]{1,0:T(8,128)(2,1)} %get-tuple-element.319), channel_id=1, source_target_pairs={{8,0},{16,8},{24,16},{28,24},{20,28},{12,20},{4,12},{0,4},{9,1},{1... | collective-permute-start | bytes 540680 | tf_op jit(solution)/shard_map/ppermute | solution.py:745
  442.5 81.3 %collective-permute-start.111 = (bf16[704,128]{1,0:T(8,128)(2,1)}, bf16[704,128]{1,0:T(8,128)(2,1)}, u32[]{:S(2)}, u32[]{:S(2)}) collective-permute-start(bf16[704,128]{1,0:T(8,128)(2,1)} %get-tuple-element.320), channel_id=1, source_target_pairs={{0,8},{8,16},{16,24},{24,28},{28,20},{20,12},{12,4},{4,0},{1,9},{9... | collective-permute-start | bytes 540680 | tf_op jit(solution)/shard_map/ppermute | solution.py:744
  487.0 50.1 %collective-permute-start.91 = (bf16[704,128]{1,0:T(8,128)(2,1)}, bf16[704,128]{1,0:T(8,128)(2,1)}, u32[]{:S(2)}, u32[]{:S(2)}) collective-permute-start(bf16[704,128]{1,0:T(8,128)(2,1)} %get-tuple-element.291), channel_id=1, source_target_pairs={{0,8},{8,16},{16,24},{24,28},{28,20},{20,12},{12,4},{4,0},{1,9},{9... | collective-permute-start | bytes 540680 | tf_op jit(solution)/shard_map/ppermute | solution.py:744
  523.7 43.2 %collective-permute-start.65 = (bf16[1280,1024]{1,0:T(8,128)(2,1)S(1)}, bf16[1280,1024]{1,0:T(8,128)(2,1)S(1)}, u32[]{:S(2)}, u32[]{:S(2)}) collective-permute-start(bf16[1280,1024]{1,0:T(8,128)(2,1)S(1)} %copy-done.6), channel_id=1, source_target_pairs={{0,1},{1,0},{2,3},{3,2},{4,5},{5,4},{6,7},{7,6},{8,9},{9,8},{10,11... | collective-permute-start | bytes 7864328 | tf_op jit(solution)/shard_map/ppermute | solution.py:800
  560.0 89.6 %collective-permute-start.58 = (bf16[1280,512]{1,0:T(8,128)(2,1)}, bf16[1280,512]{1,0:T(8,128)(2,1)}, u32[]{:S(2)}, u32[]{:S(2)}) collective-permute-start(bf16[1280,512]{1,0:T(8,128)(2,1)} %get-tuple-element.114), channel_id=1, source_target_pairs={{0,1},{1,0},{2,3},{3,2},{4,5},{5,4},{6,7},{7,6},{8,9},{9,8},{10,11... | collective-permute-start | bytes 3932168 | tf_op jit(solution)/shard_map/ppermute | solution.py:800
  601.1 96.9 %all-to-all-start.3 = ((bf16[8,320,256]{2,1,0:T(8,128)(2,1)}), bf16[8,320,256]{2,1,0:T(8,128)(2,1)S(1)}, u32[]{:S(2)}, u32[]{:S(2)}) async-start(bf16[8,320,256]{2,1,0:T(8,128)(2,1)} %bitcast.332), calls=%async_computation.3 | async-start | bytes 2621440 | tf_op jit(solution)/shard_map/all_to_all | solution.py:1120
  609.5 48.3 %collective-permute-start.98 = (bf16[1408,128]{1,0:T(8,128)(2,1)}, bf16[1408,128]{1,0:T(8,128)(2,1)S(1)}, u32[]{:S(2)}, u32[]{:S(2)}) collective-permute-start(bf16[1408,128]{1,0:T(8,128)(2,1)} %get-tuple-element.146), channel_id=1, source_target_pairs={{0,2},{2,0},{1,3},{3,1},{4,6},{6,4},{5,7},{7,5},{8,10},{10,8},{9,1... | collective-permute-start | bytes 1081352 | tf_op jit(solution)/shard_map/ppermute | solution.py:800
  610.3 32.9 %collective-permute-start.114 = (bf16[704,128]{1,0:T(8,128)(2,1)}, bf16[704,128]{1,0:T(8,128)(2,1)S(1)}, u32[]{:S(2)}, u32[]{:S(2)}) collective-permute-start(bf16[704,128]{1,0:T(8,128)(2,1)} %get-tuple-element.314), channel_id=1, source_target_pairs={{0,8},{8,16},{16,24},{24,28},{28,20},{20,12},{12,4},{4,0},{1,9},{9... | collective-permute-start | bytes 540680 | tf_op jit(solution)/shard_map/ppermute | solution.py:744
  698.0 59.5 %all-to-all-start.2 = ((bf16[8,320,256]{2,1,0:T(8,128)(2,1)}), bf16[8,320,256]{2,1,0:T(8,128)(2,1)S(1)}, u32[]{:S(2)}, u32[]{:S(2)}) async-start(bf16[8,320,256]{2,1,0:T(8,128)(2,1)} %bitcast.333), calls=%async_computation.2 | async-start | bytes 2621440 | tf_op jit(solution)/shard_map/all_to_all | solution.py:1120
  742.3 30.9 %collective-permute-start.68 = (bf16[2560,256]{1,0:T(8,128)(2,1)S(1)}, bf16[2560,256]{1,0:T(8,128)(2,1)}, u32[]{:S(2)}, u32[]{:S(2)}) collective-permute-start(bf16[2560,256]{1,0:T(8,128)(2,1)S(1)} %bitcast.328), channel_id=1, source_target_pairs={{0,2},{2,0},{1,3},{3,1},{4,6},{6,4},{5,7},{7,5},{8,10},{10,8},{9,1... | collective-permute-start | bytes 3932168 | tf_op jit(solution)/shard_map/ppermute | solution.py:800
  (211 other events, 3753.3 us)

commit v2 on v1

v2 whole, which is shorter than its diff:
```python
import functools
import math

import jax
import jax.numpy as jnp
from jax import lax
from jax.experimental import pallas as pl
from jax.experimental.pallas import tpu as pltpu
from jax.sharding import Mesh
from jax.sharding import PartitionSpec as P

DK = 128
DV = 256
SPAN = 64
MIN_SPANS = 16
MAX_SPANS = 128
PARAMS = 12872448
TILE = 256
LEVELS = 6
HEAD = 2 * DK + 2 * DV
VMEM_LIMIT = 60 * 1024 * 1024
BF = jnp.bfloat16
F32 = jnp.float32

norm_eps = 1e-06
learn_rate = 0.05
beta_one = 0.9
beta_two = 0.95
adam_eps = 1e-08
weight_decay = 0.1
clip_scale = 0.05
adam_step = 10
decay_scale = 16.0
scaling = DK ** (-0.5)
ANY = pl.BlockSpec(memory_space=pl.ANY)
SMEM = pl.BlockSpec(memory_space=pltpu.SMEM)
VMEM = pl.BlockSpec(memory_space=pltpu.VMEM)


def dot(a, b, ca=1, cb=0):
    return lax.dot_general(a, b, (((ca,), (cb,)), ((), ())), preferred_element_type=F32)


def cost(us):
    return pl.CostEstimate(flops=int(us * 1.0e9), bytes_accessed=int(us * 1.0e6), transcendentals=0)


def run(kernel, grid, in_specs, out_specs, out_shape, scratch, name, us):
    return pl.pallas_call(
        kernel,
        grid=grid,
        in_specs=in_specs,
        out_specs=out_specs,
        out_shape=out_shape,
        scratch_shapes=scratch,
        name=name,
        compiler_params=pltpu.CompilerParams(vmem_limit_bytes=VMEM_LIMIT),
        cost_estimate=cost(us),
    )


def sds(*shape, dtype=F32):
    return jax.ShapeDtypeStruct(shape, dtype)


def rows_spec(cols, order=None):
    if order is None:
        return pl.BlockSpec((TILE, cols), lambda i: (i, 0))
    return pl.BlockSpec((TILE, cols), lambda i: (order - 1 - i, 0))


def whole_spec(*shape):
    zeros = (0,) * len(shape)
    return pl.BlockSpec(shape, lambda i: zeros, pipeline_mode=pl.Buffered(1))


def span_starts(seq_extra, span_ids):
    seq_spans = seq_extra + MIN_SPANS
    n = seq_extra.shape[0]
    earlier = jnp.tril(jnp.ones((n, n), jnp.int32), -1)
    bounds = jnp.sum(earlier * seq_spans[None, :], axis=1)
    return jnp.any(bounds[None, :] == span_ids[:, None], axis=1).astype(jnp.int32)


def deal_tables(deal, n_data, per_dev, capacity, my_index):
    table_grid = deal.reshape(n_data, per_dev)
    src_dev = table_grid // per_dev
    src_local = table_grid % per_dev
    my_source = lax.dynamic_index_in_dim(src_dev, my_index, 0, keepdims=False)
    earlier = jnp.tril(jnp.ones((per_dev, per_dev), jnp.int32), -1)
    same_source = (my_source[:, None] == my_source[None, :]).astype(jnp.int32)
    my_rank = jnp.sum(same_source * earlier, axis=1)
    recv_slot = my_source * capacity + my_rank
    owned_here = (src_dev == my_index).astype(jnp.int32)
    send_rank = jnp.sum(owned_here[:, None, :] * earlier[None], axis=2)
    slot_ids = jnp.arange(capacity, dtype=jnp.int32)
    send_hit = owned_here[:, :, None] * (
        send_rank[:, :, None] == slot_ids[None, None, :]
    ).astype(jnp.int32)
    send_local = jnp.sum(send_hit * src_local[:, :, None], axis=1)
    peer_ids = jnp.arange(n_data, dtype=jnp.int32)
    local_ids = jnp.arange(per_dev, dtype=jnp.int32)
    back_hit = (
        (my_source[None, None, :] == peer_ids[:, None, None])
        & (my_rank[None, None, :] == slot_ids[None, :, None])
    ).astype(jnp.int32)
    back_local = jnp.sum(back_hit * local_ids[None, None, :], axis=2)
    home_hit = owned_here[:, :, None] * (
        src_local[:, :, None] == local_ids[None, None, :]
    ).astype(jnp.int32)
    home_slot = jnp.sum(
        home_hit * (peer_ids[:, None, None] * capacity + send_rank[:, :, None]), axis=(0, 1)
    )
    return recv_slot, send_local.reshape(-1), back_local.reshape(-1), home_slot


def level_matrices():
    t = jnp.arange(TILE, dtype=jnp.int32)[:, None]
    u = jnp.arange(TILE, dtype=jnp.int32)[None, :]
    ups = []
    level = jnp.full((TILE, TILE), LEVELS + 1, jnp.int32)
    for l in range(LEVELS):
        block = SPAN >> l
        half = block // 2
        same = (t // block) == (u // block)
        mid = (t // block) * block + half
        right = (t >= mid) & (u >= mid) & (u <= t)
        left = (t < mid) & (u > t) & (u < mid)
        ups.append(same & (right | left))
        hit = same & (t % block >= half) & (u % block < half)
        level = jnp.where(hit, l, level)
    level = jnp.where(t == u, LEVELS, level)
    same = (t // SPAN) == (u // SPAN)
    ups.append(same & (u <= t))
    ups.append(same & (u > t))
    ups = jnp.stack(ups).astype(BF)
    return ups, jnp.swapaxes(ups, 1, 2), level, level.T


def home_kernel(count, table, *refs):
    srcs, out = refs[:-1], refs[-1]
    width = srcs[0].shape[1]

    def body(i, _):
        row = pl.multiple_of(table[i] * SPAN, SPAN)
        to = pl.multiple_of(i * SPAN, SPAN)
        for k, src in enumerate(srcs):
            col = pl.multiple_of(table[count + k], 128)
            out[pl.ds(to, SPAN), pl.ds(col, width)] = src[pl.ds(row, SPAN), :].astype(F32)
        return 0

    lax.fori_loop(0, count, body, 0)


def home(pieces, table, cols, name):
    count = table.shape[0]
    width = pieces[0].shape[1]
    total = width * len(pieces)
    return pl.pallas_call(
        functools.partial(home_kernel, count),
        in_specs=[SMEM] + [VMEM] * len(pieces),
        out_specs=VMEM,
        out_shape=sds(count * SPAN, total),
        name=name,
        compiler_params=pltpu.CompilerParams(vmem_limit_bytes=VMEM_LIMIT),
        cost_estimate=cost(4),
    )(jnp.concatenate([table, jnp.stack(cols)]), *pieces)


def copy_to(src, dst, send_sem, recv_sem, target):
    return pltpu.make_async_remote_copy(
        src_ref=src,
        dst_ref=dst,
        send_sem=send_sem,
        recv_sem=recv_sem,
        device_id=target,
        device_id_type=pl.DeviceIdType.MESH,
    )


def enter(nd, shifts=()):
    dp, x, core = lax.axis_index("dp"), lax.axis_index("x"), lax.axis_index("core")
    peers = [{"dp": lax.rem(dp + k, nd)} for k in range(1, nd)] + [{"x": 1 - x}, {"core": 1 - core}]
    for k in shifts:
        peers += [along_sequence(nd, k), along_sequence(nd, -k)]
    barrier = pltpu.get_barrier_semaphore()
    for peer in peers:
        pl.semaphore_signal(barrier, inc=1, device_id=peer, device_id_type=pl.DeviceIdType.MESH)
    pl.semaphore_wait(barrier, len(peers))


def along_sequence(nd, k):
    q = lax.rem(lax.axis_index("dp") * 2 + lax.axis_index("x") + k + 2 * nd, 2 * nd)
    return {"dp": q // 2, "x": lax.rem(q, 2)}


def carry_widths(reach):
    widths = []
    width = 1
    while 2 * width < reach:
        widths.append(width)
        width *= 2
    return widths, width


class Carry:
    def __init__(self, nd, reach, sign, packet, sent, got, send_sems, recv_sems):
        self.nd, self.sign, self.packet, self.sent, self.got = nd, sign, packet, sent, got
        self.send_sems, self.recv_sems = send_sems, recv_sems
        self.widths, self.last = carry_widths(reach)
        self.q = lax.axis_index("dp") * 2 + lax.axis_index("x")

    def shifts(self):
        return self.widths + [1, 1 + self.last]

    def copy(self, index):
        source = min(index, len(self.widths))
        return copy_to(
            self.sent.at[source],
            self.got.at[index],
            self.send_sems.at[index],
            self.recv_sems.at[index],
            along_sequence(self.nd, self.sign * self.shifts()[index]),
        )

    def send(self, stage):
        self.sent[stage] = self.packet[...].astype(BF)
        self.copy(stage).start()
        if stage == len(self.widths):
            self.copy(stage + 1).start()

    def receive(self, index):
        self.copy(index).wait_recv()
        k = self.shifts()[index]
        there = self.q >= k if self.sign > 0 else self.q + k < 2 * self.nd
        return jnp.where(there, self.got[index].astype(F32), 0.0)

    def step(self, stage):
        if stage < len(self.widths):
            self.join(self.receive(stage), self.packet[...])
            self.send(stage + 1)
        else:
            near, far = self.receive(stage), self.receive(stage + 1)
            self.join(far, near)
            for index in range(stage + 2):
                self.copy(index).wait_send()

    def join(self, earlier, later):
        for h in range(2):
            states = slice(h * DV, (h + 1) * DV)
            f = slice(2 * DV + h, 2 * DV + h + 1)
            self.packet[states] = later[f] * earlier[states] + later[states]
            self.packet[f] = later[f] * earlier[f]

    def run(self):
        return len(self.widths) + 1


class Spread:
    def __init__(self, nd, order, own, window, send_sems, recv_sems):
        self.nz, self.order, self.own, self.window = nd // 2, order, own, window
        self.send_sems, self.recv_sems = send_sems, recv_sems
        dp, self.x = lax.axis_index("dp"), lax.axis_index("x")
        self.z, self.y = dp // 2, lax.rem(dp, 2)
        nz = self.nz
        self.moves = [((0, 0, 0), (k, 0, 0)) for k in range(1, nz)]
        self.moves += [((0, 0, 0), (0, 1, 0)), ((0, 0, 0), (0, 0, 1))]
        for k in range(1, nz):
            self.moves += [((k, 0, 0), (k, 1, 0)), ((k, 0, 0), (k, 0, 1))]
        self.moves += [((k, 1, 0), (k, 1, 1)) for k in range(nz)]

    def place(self, k, first, second):
        fy, fx = (first, second) if self.order == 0 else (second, first)
        y = 1 - self.y if fy else self.y
        x = 1 - self.x if fx else self.x
        return self.window(lax.rem(self.z + self.nz - k, self.nz) * 2 + y, x)

    def copy(self, index):
        here, there = self.moves[index]
        if here[0] != there[0]:
            target = {"dp": lax.rem(self.z + there[0], self.nz) * 2 + self.y}
        elif (here[1] != there[1]) == (self.order == 0):
            target = {"dp": self.z * 2 + 1 - self.y}
        else:
            target = {"x": 1 - self.x}
        k, first, second = there
        return copy_to(
            self.own if here == (0, 0, 0) else self.place(*here),
            self.place(*here),
            self.send_sems.at[index],
            self.recv_sems.at[k + self.nz * (first + 2 * second)],
            target,
        )

    def arrived(self, k, first, second):
        at = self.place(k, first, second)
        sem = self.recv_sems.at[k + self.nz * (first + 2 * second)]
        copy_to(at, at, self.send_sems.at[0], sem, {"x": 1 - self.x}).wait_recv()

    def begin(self):
        for index in range(self.nz + 1):
            self.copy(index).start()

    def relay_z(self, k):
        self.arrived(k, 0, 0)
        for index in range(2):
            self.copy(self.nz + 1 + 2 * (k - 1) + index).start()

    def relay_first(self, k):
        self.arrived(k, 1, 0)
        self.copy(3 * self.nz - 1 + k).start()

    def finish(self):
        for k in range(self.nz):
            self.arrived(k, 0, 1)
            self.arrived(k, 1, 1)
        for index in range(len(self.moves)):
            self.copy(index).wait_send()


CHUNKS = 4


class Deal:
    def __init__(self, nd, spans, table, rows, out, tok, send, recv, other, sems):
        self.nd, self.spans, self.table, self.rows, self.out = nd, spans, table, rows, out
        self.tok, self.sent, self.recv, self.other = tok, send, recv, other
        self.load_sem, self.a2a_send, self.a2a_recv, self.x_send, self.x_recv, self.c_send, self.c_recv = sems
        self.dp, self.x, self.core = lax.axis_index("dp"), lax.axis_index("x"), lax.axis_index("core")
        self.quarter = out.shape[1] // 4
        self.cap = send.shape[1]
        self.mine = pl.multiple_of((2 * self.x + self.core) * self.quarter, 128)
        self.theirs = pl.multiple_of((2 * (1 - self.x) + self.core) * self.quarter, 128)
        self.load = pltpu.make_async_copy(rows.at[:, :, pl.ds(self.mine, self.quarter)], tok, self.load_sem.at[0])
        self.started = []

    def begin(self):
        self.load.start()

    def exchange(self):
        self.load.wait()
        cap, nd = self.cap, self.nd

        def pick(k, out, base):
            d = lax.rem(self.dp + k, nd)
            for j in range(cap):
                out[base + j] = self.tok[self.table[d * cap + j]]

        here = self.dp * cap
        for k in range(1, nd):
            pick(k, self.sent.at[k], 0)
            copy = copy_to(
                self.sent.at[k],
                self.recv.at[pl.ds(here, cap)],
                self.a2a_send.at[k],
                self.a2a_recv.at[k],
                {"dp": lax.rem(self.dp + k, nd)},
            )
            copy.start()
            self.started.append(copy)
        pick(0, self.recv, here)

    def across(self):
        for copy in self.started:
            copy.wait_recv()
        spans, nd = self.spans, self.nd
        count = spans // CHUNKS
        first = nd * self.cap
        self.x_copies, self.c_copies = [], []
        for c in range(CHUNKS):
            rows = pl.ds(c * count * SPAN, count * SPAN)

            def body(i, _, c=c):
                at = c * count + i
                to = pl.ds(pl.multiple_of(at * SPAN, SPAN), SPAN)
                self.other[to, :] = self.recv[self.table[first + spans + at]]
                return 0

            lax.fori_loop(0, count, body, 0)
            copy = copy_to(
                self.other.at[rows, :],
                self.out.at[rows, pl.ds(self.mine, self.quarter)],
                self.x_send.at[c],
                self.x_recv.at[c],
                {"x": 1 - self.x},
            )
            copy.start()
            self.x_copies.append(copy)

        def body(i, _):
            to = pl.ds(pl.multiple_of(i * SPAN, SPAN), SPAN)
            self.out[to, pl.ds(self.mine, self.quarter)] = self.recv[self.table[first + i]]
            return 0

        lax.fori_loop(0, spans, body, 0)
        self.pass_on(slice(None), self.mine, CHUNKS)

    def pass_on(self, rows, col, sem):
        at = self.out.at[rows, pl.ds(col, self.quarter)]
        copy = copy_to(at, at, self.c_send.at[sem], self.c_recv.at[sem], {"core": 1 - self.core})
        copy.start()
        self.c_copies.append(copy)

    def finish(self):
        count = self.spans // CHUNKS
        for c, copy in enumerate(self.x_copies):
            copy.wait_recv()
            self.pass_on(pl.ds(c * count * SPAN, count * SPAN), self.theirs, c)
        for copy in self.c_copies:
            copy.wait_recv()
        for copy in self.x_copies + self.c_copies:
            copy.wait_send()

    def release(self):
        for copy in self.started:
            copy.wait_send()


def deal_buffers(nd, per_dev, spans, quarter, cap):
    return [
        pltpu.VMEM((per_dev, SPAN, quarter), BF),
        pltpu.VMEM((nd, cap, SPAN, quarter), BF),
        pltpu.VMEM((spans * SPAN, quarter), BF),
        pltpu.VMEM((nd * cap, SPAN, quarter), BF),
        pltpu.VMEM((nd * cap, SPAN, quarter), BF),
    ]


def deal_sems(nd):
    dma = pltpu.SemaphoreType.DMA
    return [dma((1,)), dma((nd,)), dma((nd,)), dma((CHUNKS,)), dma((CHUNKS,)), dma((CHUNKS + 1,)), dma((CHUNKS + 1,))]


class Undeal:
    def __init__(self, nd, spans, table, own, cross, joined, sent, gath, sems):
        self.nd, self.spans, self.table, self.own, self.cross = nd, spans, table, own, cross
        self.joined, self.sent, self.gath = joined, sent, gath
        self.x_send, self.x_recv, self.a2a_send, self.a2a_recv, *self.wide_sems = sems
        self.dp, self.x, self.core = lax.axis_index("dp"), lax.axis_index("x"), lax.axis_index("core")
        self.cap = sent.shape[1]
        self.quarter = own.shape[2]
        self.wide = gath.shape[2] != self.quarter
        self.mine, self.theirs = 0, 0
        if self.wide:
            self.mine = pl.multiple_of((2 * self.x + self.core) * self.quarter, 128)
            self.theirs = pl.multiple_of((2 * (1 - self.x) + self.core) * self.quarter, 128)

    def swap(self):
        return copy_to(
            self.cross,
            self.joined.at[pl.ds(self.x * self.spans, self.spans)],
            self.x_send.at[0],
            self.x_recv.at[0],
            {"x": 1 - self.x},
        )

    def begin(self):
        self.swap().start()

        def body(i, _):
            self.joined[self.x * self.spans + i] = self.own[i]
            return 0

        lax.fori_loop(0, self.spans, body, 0)

    def block(self, dp, col):
        return self.gath.at[pl.ds(dp * self.cap, self.cap), :, pl.ds(col, self.quarter)]

    def a2a(self, k):
        return copy_to(
            self.sent.at[k],
            self.block(self.dp, self.mine),
            self.a2a_send.at[k],
            self.a2a_recv.at[k],
            {"dp": lax.rem(self.dp + k, self.nd)},
        )

    def exchange(self):
        self.swap().wait_recv()
        cap = self.cap
        for k in range(1, self.nd):
            d = lax.rem(self.dp + k, self.nd)
            for j in range(cap):
                self.sent[k, j] = self.joined[self.table[d * cap + j]]
            self.a2a(k).start()
        here = self.block(self.dp, self.mine)
        for j in range(cap):
            here[j] = self.joined[self.table[self.dp * cap + j]]
        if self.wide:
            self.widen(0, 0).start()
            self.widen(0, 1).start()

    def widen(self, k, step):
        at = self.block(lax.rem(self.dp + self.nd - k, self.nd), self.theirs if step == 2 else self.mine)
        send, recv = self.wide_sems
        return copy_to(
            at, at, send.at[3 * k + step], recv.at[3 * k + step],
            {"x": 1 - self.x} if step == 0 else {"core": 1 - self.core},
        )

    def arrive(self, k):
        self.a2a(k).wait_recv()
        if self.wide:
            self.widen(k, 0).start()
            self.widen(k, 1).start()

    def finish(self):
        if self.wide:
            for k in range(self.nd):
                self.widen(k, 0).wait_recv()
                self.widen(k, 2).start()
            for k in range(self.nd):
                self.widen(k, 1).wait_recv()
                self.widen(k, 2).wait_recv()
                for step in range(3):
                    self.widen(k, step).wait_send()
        for k in range(1, self.nd):
            self.a2a(k).wait_send()
        self.swap().wait_send()


def undeal_scratch(nd, per_dev, spans, quarter, cap, wide):
    dma = pltpu.SemaphoreType.DMA
    buffers = [
        pltpu.VMEM((spans, SPAN, quarter), BF),
        pltpu.VMEM((spans, SPAN, quarter), BF),
        pltpu.VMEM((per_dev, SPAN, quarter), BF),
        pltpu.VMEM((nd, cap, SPAN, quarter), BF),
        pltpu.VMEM((nd * cap, SPAN, quarter * (4 if wide else 1)), BF),
    ]
    sems = [dma((1,)), dma((1,)), dma((nd,)), dma((nd,))]
    return buffers, sems + ([dma((3 * nd,)), dma((3 * nd,))] if wide else [])


class Collapse:
    def __init__(self, nd, order, acc, pitch, low, rows, got, sems):
        self.nz, self.order, self.acc, self.pitch, self.low, self.rows = nd // 2, order, acc, pitch, low, rows
        self.got = got
        self.send_sems, self.recv_sems = sems
        self.w = got.shape[2]
        dp, self.x = lax.axis_index("dp"), lax.axis_index("x")
        self.z, self.y = dp // 2, lax.rem(dp, 2)

    def window(self, first, second, kz):
        fx, fy = (first, second) if self.order == 0 else (second, first)
        y = 1 - self.y if fy else self.y
        x = 1 - self.x if fx else self.x
        dp = lax.rem(self.z + kz, self.nz) * 2 + y
        return self.acc.at[
            pl.ds(pl.multiple_of(x * self.pitch + self.low, 16), self.rows),
            pl.ds(pl.multiple_of(dp * self.w, 128), self.w),
        ]

    def partner(self, which):
        if (which == 0) == (self.order == 0):
            return {"x": 1 - self.x}
        return {"dp": self.z * 2 + 1 - self.y}

    def slot(self, phase, second, kz):
        nz = self.nz
        return second * nz + kz if phase == 1 else (2 * nz + kz if phase == 2 else 3 * nz + kz - 1)

    def copy(self, phase, second, kz):
        at = self.slot(phase, second, kz)
        if phase == 1:
            src, target = self.window(1, second, kz), self.partner(0)
        elif phase == 2:
            src, target = self.window(0, 1, kz), self.partner(1)
        else:
            src, target = self.window(0, 0, kz), {"dp": lax.rem(self.z + kz, self.nz) * 2 + self.y}
        return copy_to(src, self.got.at[at], self.send_sems.at[at], self.recv_sems.at[at], target)

    def add(self, second, kz, at):
        here = self.window(0, second, kz)
        here[...] = (here[...].astype(F32) + self.got[at].astype(F32)).astype(BF)

    def begin(self):
        for second in (1, 0):
            for kz in range(self.nz):
                self.copy(1, second, (kz + 1) % self.nz).start()

    def second(self, kz):
        self.copy(1, 1, kz).wait_recv()
        self.add(1, kz, self.slot(1, 1, kz))
        self.copy(2, 1, kz).start()

    def third(self, kz):
        self.copy(1, 0, kz).wait_recv()
        self.add(0, kz, self.slot(1, 0, kz))
        self.copy(2, 1, kz).wait_recv()
        self.add(0, kz, self.slot(2, 1, kz))
        if kz:
            self.copy(3, 0, kz).start()

    def finish(self, out):
        total = self.window(0, 0, 0)[...].astype(F32)
        for kz in range(1, self.nz):
            self.copy(3, 0, kz).wait_recv()
            total = total + self.got[self.slot(3, 0, kz)].astype(F32)
        out[...] = total
        for kz in range(self.nz):
            self.copy(1, 0, kz).wait_send()
            self.copy(1, 1, kz).wait_send()
            self.copy(2, 1, kz).wait_send()
            if kz:
                self.copy(3, 0, kz).wait_send()


def collapse_scratch(nd, rows, w):
    count = 4 * (nd // 2) - 1
    dma = pltpu.SemaphoreType.DMA
    return [pltpu.VMEM((count, rows, w), BF), dma((count,)), dma((count,))]


def progress(chains, nz, between=()):
    between = list(between)
    for kz in [k % nz for k in range(1, nz + 1)]:
        for chain in chains:
            chain.second(kz)
        if between:
            between.pop(0)()
    for kz in [k % nz for k in range(1, nz + 1)]:
        for chain in chains:
            chain.third(kz)
        if between:
            between.pop(0)()
    for work in between:
        work()


PROJ_ROWS = 16 + HEAD + DV
PROJ_CUTS = ((0, 528), (528, 512))


FFN_CUTS = 2
PITCH = 768


def up_to(value, step):
    return -(-value // step) * step


def forward_kernel(nd, spans, reach, gather, table, ints, tokens, cotangent, shard_p, shard_f, gain, up, bias, head_gain,
                   ups, level, *rest):
    outs, rest = rest[:13], rest[13:]
    (src_o, cot_o, wp_o, wf_o, normed_o, qkvg_o, log_decay_o, rank_o, mixed_o, gated_o, attn_o, before_o, attn_other) = outs
    (src, cot, wp, wf, normed, qkvg, log_decay, rank, mixed, gated, attn, before), rest = rest[:12], rest[12:]
    (packet, factors, sent_packets, got_packets), rest = rest[:4], rest[4:]
    (tok, sent, other, recv_t, recv_c), rest = rest[:5], rest[5:]
    sems_t, sems_c, rest = rest[:7], rest[7:14], rest[14:]
    carry_send, carry_recv, core_send, core_recv, out_sems, own_sems, *ag_sems = rest
    tiles = spans * SPAN // TILE
    carry = Carry(nd, reach, 1, packet, sent_packets, got_packets, carry_send, carry_recv)
    enter(nd, carry.shifts())
    deal = Deal(nd, spans, table, tokens, src, tok, sent, recv_t, other, sems_t)
    deal_c = Deal(nd, spans, table, cotangent, cot, tok, sent, recv_c, other, sems_c)
    deal.begin()
    local = []
    spreads_p, spreads_f = [], []
    if gather:
        w = shard_p.shape[1]
        f3 = shard_f.shape[0]
        cuts_f = ((0, f3 // 2), (f3 // 2, f3 // 2))

        def window(buffer, pitch, cut, dp, x):
            low, count = cut
            return buffer.at[
                pl.ds(pl.multiple_of(x * pitch + low, 16), count), pl.ds(pl.multiple_of(dp * w, 128), w)
            ]

        for shard, buffer, cuts, spreads in ((shard_p, wp, PROJ_CUTS, spreads_p), (shard_f, wf, cuts_f, spreads_f)):
            for order, cut in enumerate(cuts):
                piece = shard.at[pl.ds(cut[0], cut[1]), :]
                place = functools.partial(window, buffer, shard.shape[0], cut)
                copy = pltpu.make_async_copy(
                    piece, place(lax.axis_index("dp"), lax.axis_index("x")), own_sems.at[len(local)]
                )
                copy.start()
                local.append(copy)
                k = 2 * (len(local) - 1)
                spreads.append(Spread(nd, order, piece, place, ag_sems[k], ag_sems[k + 1]))
    else:
        for shard, buffer in ((shard_p, wp), (shard_f, wf)):
            local.append(pltpu.make_async_copy(shard, buffer, own_sems.at[len(local)]))
            local[-1].start()
    outgoing = []

    def store(value, out):
        outgoing.append(pltpu.make_async_copy(value, out, out_sems.at[len(outgoing)]))
        outgoing[-1].start()

    def relay_z(spreads, k):
        for spread in spreads:
            spread.relay_z(k)

    def relay_first(spreads, k):
        for spread in spreads:
            spread.relay_first(k)

    nz = nd // 2
    last_z = range(1, nz) if gather else ()
    last_first = range(nz) if gather else ()
    for spread in spreads_p:
        spread.begin()
    deal.exchange()
    for spread in spreads_f:
        spread.begin()
    deal_c.begin()
    for k in last_z:
        relay_z(spreads_p, k)
    for k in last_first:
        relay_first(spreads_p, k)
    deal.across()
    deal.release()
    deal_c.exchange()
    for k in last_z[:1]:
        relay_z(spreads_f, k)
    for k in last_first[:1]:
        relay_first(spreads_f, k)
    deal.finish()
    for spread in spreads_p:
        spread.finish()
    for copy in local:
        copy.wait()
    store(src, src_o)
    store(wp, wp_o)

    def at(ref, i):
        return ref.at[pl.ds(pl.multiple_of(i * TILE, TILE), TILE), :]

    packet[...] = jnp.zeros_like(packet)
    packet[2 * DV : 2 * DV + 2] = jnp.ones((2, DK), F32)

    def project(i, _):
        project_kernel(
            i, ints, at(src, i), gain, wp, up, bias, ups,
            at(normed, i), at(qkvg, i), at(log_decay, i), at(rank, i), packet,
        )
        return 0

    lax.fori_loop(0, tiles // 2, project, 0)
    for k in last_z[1:2]:
        relay_z(spreads_f, k)
    for k in last_first[1:2]:
        relay_first(spreads_f, k)
    lax.fori_loop(tiles // 2, tiles, project, 0)
    factors[...] = packet[2 * DV :]
    carry.send(0)
    store(normed, normed_o)
    store(qkvg, qkvg_o)
    store(log_decay, log_decay_o)
    store(rank, rank_o)
    for k in last_z[2:]:
        relay_z(spreads_f, k)
    for k in last_first[2:]:
        relay_first(spreads_f, k)

    def within(i, _):
        within_kernel(at(qkvg, i), at(log_decay, i), ups, level, at(mixed, i))
        return 0

    stages = carry.run()
    for stage in range(stages):
        lax.fori_loop(tiles * stage // stages, tiles * (stage + 1) // stages, within, 0)
        carry.step(stage)
    deal_c.across()
    per_tile = TILE // SPAN

    def mix(i, _):
        mix_kernel(
            i, ints, at(qkvg, i), at(log_decay, i), packet, ups, head_gain, wp,
            at(mixed, i), at(gated, i), at(attn, i), before.at[pl.ds(i * per_tile, per_tile)],
        )
        return 0

    lax.fori_loop(0, tiles, mix, 0)
    swap_attn = copy_to(
        attn, attn_other, core_send.at[0], core_recv.at[0], {"core": 1 - lax.axis_index("core")}
    )
    swap_attn.start()
    store(mixed, mixed_o)
    store(gated, gated_o)
    store(attn, attn_o)
    store(before, before_o)
    deal_c.finish()
    store(cot, cot_o)
    for spread in spreads_f:
        spread.finish()
    store(wf, wf_o)
    deal_c.release()
    swap_attn.wait()
    for copy in outgoing:
        copy.wait()


def forward(table, ints, tokens, cotangent, shard_p, shard_f, gain, up, bias, head_gain, ups, level, nd, spans, reach, gather):
    d = tokens.shape[1]
    per_dev = tokens.shape[0] // SPAN
    cap = -(-per_dev // nd)
    rows = spans * SPAN
    dma = pltpu.SemaphoreType.DMA
    nz = nd // 2
    wf_rows = shard_f.shape[0] * (2 if gather else 1)
    kept = [
        ((rows, d), BF), ((rows, d), BF), ((2 * PROJ_ROWS, d), BF), ((wf_rows, d), BF), ((rows, d), BF),
        ((rows, 2 * HEAD), BF), ((rows, 2 * DK), F32), ((rows, 16), BF), ((rows, 2 * DV), F32), ((rows, 2 * DV), BF),
        ((rows, d), BF), ((spans, 2, DV, DK), BF),
    ]
    widths, _ = carry_widths(reach)
    steps = len(widths) + 2
    scratch = [pltpu.VMEM(shape, dtype) for shape, dtype in kept]
    scratch += [
        pltpu.VMEM((2 * DV + 16, DK), F32),
        pltpu.VMEM((steps - 1, 2 * DV + 16, DK), BF),
        pltpu.VMEM((steps, 2 * DV + 16, DK), BF),
    ]
    scratch += deal_buffers(nd, per_dev, spans, d // 4, cap) + deal_sems(nd) + deal_sems(nd)
    scratch += [dma((steps,)), dma((steps,)), dma((1,)), dma((1,)), dma((12,)), dma((4,))]
    if gather:
        scratch += [dma((4 * nz - 1,)), dma((4 * nz,))] * 4
    outs = [sds(*shape, dtype=dtype) for shape, dtype in kept] + [sds(rows, d, dtype=BF)]
    outs.append(sds(16, DK))
    specs = [ANY] * 13 + [VMEM]

    def kernel(*refs):
        n_in = 12
        ins, rest = refs[:n_in], refs[n_in:]
        results, factors, buffers = rest[:13], rest[13], rest[14:]
        forward_kernel(
            nd, spans, reach, gather, *ins, *results, *buffers[:12], buffers[12], factors, *buffers[13:]
        )

    return pl.pallas_call(
        kernel,
        in_specs=[SMEM, SMEM, ANY, ANY, ANY, ANY] + [VMEM] * 6,
        out_specs=specs,
        out_shape=outs,
        scratch_shapes=scratch,
        name="forward",
        compiler_params=pltpu.CompilerParams(
            vmem_limit_bytes=VMEM_LIMIT, collective_id=0, has_side_effects=True
        ),
        cost_estimate=cost(150),
    )(
        table, ints, tokens.reshape(per_dev, SPAN, d), cotangent.reshape(per_dev, SPAN, d), shard_p, shard_f,
        gain, up, bias, head_gain, ups, level,
    )


def rms_scale(x):
    return lax.rsqrt(jnp.mean(x * x, axis=-1, keepdims=True) + norm_eps)


def distances(ups, log_decay):
    high = log_decay.astype(BF)
    lower = (log_decay - high.astype(F32)).astype(BF)
    return dot(ups, high) + dot(ups, lower)


def head_cols(h, part):
    start = h * HEAD + (0, DK, 2 * DK, 2 * DK + DV)[part]
    return slice(start, start + (DK, DK, DV, DV)[part])


def in_rows(h):
    return slice(h * PROJ_ROWS + 16, h * PROJ_ROWS + 16 + HEAD)


def out_rows(h):
    return slice(h * PROJ_ROWS + 16 + HEAD, (h + 1) * PROJ_ROWS)


def log_sigmoid(v):
    return jnp.minimum(v, 0.0) - jnp.log(1.0 + jnp.exp(-jnp.abs(v)))


def project_kernel(
    step, ints, src, gain, weights, up, bias, ups,
    normed, qkvg, log_decay, rank, packet,
):
    x = src[...].astype(F32)
    nf = (x * rms_scale(x) * gain[...]).astype(BF)
    normed[...] = nf
    low = dot(nf, weights[0:16, :], 1, 1).astype(BF)
    rank[...] = low
    logits = dot(low, up[...]) + bias[...]
    ld = log_sigmoid(logits) * (1.0 / decay_scale)
    log_decay[...] = ld
    towards = jnp.exp(distances(ups[LEVELS + 1], ld))
    per_tile = TILE // SPAN
    for h in range(2):
        proj = dot(nf, weights[in_rows(h), :], 1, 1)
        qkvg[:, head_cols(h, 0)] = (proj[:, :DK] * scaling).astype(BF)
        qkvg[:, h * HEAD + DK : (h + 1) * HEAD] = proj[:, DK:].astype(BF)
    for j in range(per_tile):
        rows = slice(j * SPAN, (j + 1) * SPAN)
        keep = ints[step * per_tile + j].astype(F32)
        total = jnp.exp(jnp.sum(ld[rows], axis=0, keepdims=True)) * keep
        for h in range(2):
            lanes = slice(h * DK, (h + 1) * DK)
            states = slice(h * DV, (h + 1) * DV)
            f = slice(2 * DV + h, 2 * DV + h + 1)
            packet[f] = packet[f] * total[:, lanes]
            kd = (qkvg[rows, head_cols(h, 1)].astype(F32) * towards[rows, lanes]).astype(BF)
            packet[states] = packet[states] * total[:, lanes] + dot(qkvg[rows, head_cols(h, 2)], kd, 0, 0)


def within_kernel(qkvg, log_decay, ups, level, within):
    ld = log_decay[...]
    high = ld.astype(BF)
    lower = (ld - high.astype(F32)).astype(BF)
    lev = level[...]
    scores = [None, None]
    for l in range(LEVELS + 1):
        if l < LEVELS:
            x = jnp.exp(dot(ups[l], high) + dot(ups[l], lower))
        for h in range(2):
            q, k = qkvg[:, head_cols(h, 0)], qkvg[:, head_cols(h, 1)]
            if l < LEVELS:
                xh = x[:, h * DK : (h + 1) * DK]
                q = (q.astype(F32) * xh).astype(BF)
                k = (k.astype(F32) * xh).astype(BF)
            s = dot(q, k, 1, 1)
            scores[h] = jnp.where(lev == l, s, 0.0 if l == 0 else scores[h])
    for h in range(2):
        within[:, h * DV : (h + 1) * DV] = dot(scores[h].astype(BF), qkvg[:, head_cols(h, 2)])


def mix_kernel(
    step, ints, qkvg, log_decay, packet, ups, head_gain, weights,
    mixed, gated, attn, before,
):
    per_tile = TILE // SPAN
    ld = log_decay[...]
    since = jnp.exp(distances(ups[LEVELS], ld))
    towards = jnp.exp(distances(ups[LEVELS + 1], ld))
    for j in range(per_tile):
        rows = slice(j * SPAN, (j + 1) * SPAN)
        keep = ints[step * per_tile + j].astype(F32)
        for h in range(2):
            lanes = slice(h * DK, (h + 1) * DK)
            values = slice(h * DV, (h + 1) * DV)
            prev = packet[values] * keep
            prev_low = prev.astype(BF)
            before[j, h] = prev_low
            qd = (qkvg[rows, head_cols(h, 0)].astype(F32) * since[rows, lanes]).astype(BF)
            kd = (qkvg[rows, head_cols(h, 1)].astype(F32) * towards[rows, lanes]).astype(BF)
            mixed[rows, values] = mixed[rows, values] + dot(qd, prev_low, 1, 1)
            last = since[j * SPAN + SPAN - 1 : j * SPAN + SPAN, lanes]
            packet[values] = prev * last + dot(qkvg[rows, head_cols(h, 2)], kd, 0, 0)
    for h in range(2):
        values = slice(h * DV, (h + 1) * DV)
        m = mixed[:, values]
        g = qkvg[:, head_cols(h, 3)].astype(F32)
        y = m * rms_scale(m) * head_gain[...] * g * jax.nn.sigmoid(g)
        gated[:, values] = y.astype(BF)
    attn[...] = (
        dot(gated[:, :DV], weights[out_rows(0), :]) + dot(gated[:, DV:], weights[out_rows(1), :])
    ).astype(BF)


def ffn_kernel(
    f, ints, src, attn_a, attn_b, cot, gain, weights,
    hidden, normed, act, grad_gu, keep_out, send_out, grad_second,
    part,
):
    quarter = cot.shape[1] // 4
    hid = src[...].astype(F32) + (attn_a[...].astype(F32) + attn_b[...].astype(F32))
    hidden[...] = hid
    ns = (hid * rms_scale(hid) * gain[...]).astype(BF)
    normed[...] = ns
    c = cot[...]
    back, total = None, None
    for g in range(2):
        base = 3 * f * g
        w_gate, w_out, w_up = (slice(base + k * f, base + (k + 1) * f) for k in range(3))
        gate = dot(ns, weights[w_gate, :], 1, 1)
        upper = dot(ns, weights[w_up, :], 1, 1)
        ga = dot(c, weights[w_out, :], 1, 1)
        sig = jax.nn.sigmoid(gate)
        swish = gate * sig
        low = (swish * upper).astype(BF)
        gg = (ga * upper * sig * (1.0 + gate * (1.0 - sig))).astype(BF)
        gu = (ga * swish).astype(BF)
        pitch = act.shape[1] // 2
        act[:, g * pitch : g * pitch + f] = low
        grad_gu[:, g * pitch : g * pitch + f] = gg
        grad_gu[:, (2 + g) * pitch : (2 + g) * pitch + f] = gu
        out = dot(low, weights[w_out, :])
        e = dot(gg, weights[w_gate, :]) + dot(gu, weights[w_up, :])
        total = out if g == 0 else total + out
        back = e if g == 0 else back + e
    part[...] = total.astype(BF)
    grad_second[...] = back.astype(BF)
    core = ints[4]
    for h in range(2):
        mine = pl.multiple_of((2 * h + core) * quarter, 128)
        theirs = pl.multiple_of((2 * h + 1 - core) * quarter, 128)
        keep_out[:, h * quarter : (h + 1) * quarter] = part[:, pl.ds(mine, quarter)]
        send_out[:, h * quarter : (h + 1) * quarter] = part[:, pl.ds(theirs, quarter)]


def weight_grad_into(acc, lhs, rhs, chunk):
    def body(i, _):
        at = pl.multiple_of(i * chunk, chunk)
        acc[pl.ds(at, chunk), :] = dot(lhs[:, pl.ds(at, chunk)], rhs[...], 0, 0).astype(BF)
        return 0

    lax.fori_loop(0, acc.shape[0] // chunk, body, 0)


def out_back_kernel(
    n, ints, hidden, cot, gs_a, gs_b, gain, weights, gated, mixed, qkvg, log_decay, head_gain, ups,
    keep_out, recv_out,
    grad_hidden, grad_mixed, grad_gate, gain_grad, head_grad, packet, out_own, out_cross, *rest,
):
    w_grads, (acc, state, gain_sum, head_sum) = rest[:-4], rest[-4:]
    step = pl.program_id(0)
    tile = n - 1 - step
    per_tile = TILE // SPAN

    @pl.when(step == 0)
    def _():
        acc[...] = jnp.zeros_like(acc)
        state[...] = jnp.zeros_like(state)
        gain_sum[...] = jnp.zeros_like(gain_sum)
        head_sum[...] = jnp.zeros_like(head_sum)

    x, core = ints[7], ints[4]
    quarter = out_own.shape[1]
    for target, half in ((out_own, x), (out_cross, 1 - x)):
        at = pl.multiple_of((2 * half + core) * quarter, 128)
        pair = pl.multiple_of(half * quarter, 128)
        share = keep_out[:, pl.ds(pair, quarter)].astype(F32) + recv_out[:, pl.ds(pair, quarter)].astype(F32)
        target[...] = (hidden[:, pl.ds(at, quarter)] + share).astype(BF)
    gs = gs_a[...].astype(F32) + gs_b[...].astype(F32)
    hid = hidden[...]
    inv = rms_scale(hid)
    normal = hid * inv
    gain_sum[0:1, :] += jnp.sum(gs * normal, axis=0, keepdims=True)
    e = gs * gain[...]
    gh = cot[...].astype(F32) + inv * (e - normal * jnp.mean(e * normal, axis=-1, keepdims=True))
    grad_hidden[...] = gh
    low = gh.astype(BF)
    acc[...] += dot(gated[...], low, 0, 0)
    for h in range(2):
        values = slice(h * DV, (h + 1) * DV)
        m = mixed[:, values]
        inv_head = rms_scale(m)
        nh = m * inv_head
        g = qkvg[:, head_cols(h, 3)].astype(F32)
        sig = jax.nn.sigmoid(g)
        w = g * sig
        gd = dot(low, weights[out_rows(h), :], 1, 1)
        head_sum[0:1, :] += jnp.sum(gd * nh * w, axis=0, keepdims=True)
        gn = gd * head_gain[...]
        grad_gate[:, values] = (gn * nh * sig * (1.0 + g * (1.0 - sig))).astype(BF)
        gn = gn * w
        gm = inv_head * (gn - nh * jnp.mean(gn * nh, axis=-1, keepdims=True))
        grad_mixed[:, values] = gm.astype(BF)
    since = jnp.exp(distances(ups[LEVELS], log_decay[...]))
    for j in reversed(range(per_tile)):
        rows = slice(j * SPAN, (j + 1) * SPAN)
        keep = ints[8 + tile * per_tile + j].astype(F32)
        for h in range(2):
            lanes = slice(h * DK, (h + 1) * DK)
            values = slice(h * DV, (h + 1) * DV)
            qd = (qkvg[rows, head_cols(h, 0)].astype(F32) * since[rows, lanes]).astype(BF)
            last = since[j * SPAN + SPAN - 1 : j * SPAN + SPAN, lanes]
            state[h] = keep * (state[h] * last + dot(grad_mixed[rows, values], qd, 0, 0))

    @pl.when(step == n - 1)
    def _():
        packet[0:DV] = state[0]
        packet[DV : 2 * DV] = state[1]
        gain_grad[...] = gain_sum[...]
        head_grad[...] = head_sum[...]
        w_grads[0][...] = acc[...].astype(BF)


def within_back_kernel(qkvg, log_decay, grad_mixed, ups, downs, level, level_t, grad_qk, grad_v, grad_ld):
    ld = log_decay[...]
    high = ld.astype(BF)
    lower = (ld - high.astype(F32)).astype(BF)
    lev, lev_t = level[...], level_t[...]
    gd, gd_t = [], []
    for h in range(2):
        v, gm = qkvg[:, head_cols(h, 2)], grad_mixed[:, h * DV : (h + 1) * DV]
        gd.append(dot(gm, v, 1, 1))
        gd_t.append(dot(v, gm, 1, 1))
    scores_t = [None, None]
    grad_q, grad_k = [None, None], [None, None]
    for l in range(LEVELS + 1):
        if l < LEVELS:
            x = jnp.exp(dot(ups[l], high) + dot(ups[l], lower))
        parts = []
        for h in range(2):
            q, k = qkvg[:, head_cols(h, 0)], qkvg[:, head_cols(h, 1)]
            if l < LEVELS:
                xh = x[:, h * DK : (h + 1) * DK]
                qf, kf = q.astype(F32) * xh, k.astype(F32) * xh
                q, k = qf.astype(BF), kf.astype(BF)
            s = dot(k, q, 1, 1)
            scores_t[h] = jnp.where(lev_t == l, s, 0.0 if l == 0 else scores_t[h])
            here = jnp.where(lev == l, gd[h], 0.0).astype(BF)
            here_t = jnp.where(lev_t == l, gd_t[h], 0.0).astype(BF)
            dq, dk = dot(here, k), dot(here_t, q)
            if l < LEVELS:
                parts.append(qf * dq + kf * dk)
                dq, dk = dq * xh, dk * xh
            grad_q[h] = dq if l == 0 else grad_q[h] + dq
            grad_k[h] = dk if l == 0 else grad_k[h] + dk
        if l < LEVELS:
            both = dot(downs[l], jnp.concatenate(parts, axis=1).astype(BF))
            total = both if l == 0 else total + both
    grad_ld[...] = total
    for h in range(2):
        grad_qk[:, 2 * h * DK : (2 * h + 1) * DK] = grad_q[h]
        grad_qk[:, (2 * h + 1) * DK : (2 * h + 2) * DK] = grad_k[h]
        grad_v[:, h * DV : (h + 1) * DV] = dot(
            scores_t[h].astype(BF), grad_mixed[:, h * DV : (h + 1) * DV]
        ).astype(BF)


def project_back_kernel(
    tile, ints, qkvg, log_decay, grad_mixed, before, grad_qk, grad_v, grad_ld, grad_gate, rank, up, bias,
    ups, downs, weights,
    grad_project, grad_first, rank_part, packet, up_sum, bias_sum, d_since, d_towards, ld_sum,
):
    per_tile = TILE // SPAN
    ld = log_decay[...]
    since = jnp.exp(distances(ups[0], ld))
    towards = jnp.exp(distances(ups[1], ld))
    for j in reversed(range(per_tile)):
        rows = slice(j * SPAN, (j + 1) * SPAN)
        keep = ints[tile * per_tile + j].astype(F32)
        for h in range(2):
            lanes = slice(h * DK, (h + 1) * DK)
            values = slice(h * DV, (h + 1) * DV)
            gm = grad_mixed[rows, values]
            v = qkvg[rows, head_cols(h, 2)]
            qd = qkvg[rows, head_cols(h, 0)].astype(F32) * since[rows, lanes]
            kd = qkvg[rows, head_cols(h, 1)].astype(F32) * towards[rows, lanes]
            prev = before[j, h]
            after = packet[values]
            after_low = after.astype(BF)
            dq = dot(gm, prev)
            dk = dot(v, after_low)
            d_since[rows, lanes] = (qd * dq).astype(BF)
            d_towards[rows, lanes] = (kd * dk).astype(BF)
            dq = grad_qk[rows, 2 * h * DK : (2 * h + 1) * DK] + dq * since[rows, lanes]
            dk = grad_qk[rows, (2 * h + 1) * DK : (2 * h + 2) * DK] + dk * towards[rows, lanes]
            dv = grad_v[rows, values].astype(F32) + dot(kd.astype(BF), after_low, 1, 1)
            grad_project[rows, head_cols(h, 0)] = (dq * scaling).astype(BF)
            grad_project[rows, head_cols(h, 1)] = dk.astype(BF)
            grad_project[rows, head_cols(h, 2)] = dv.astype(BF)
            grad_project[rows, head_cols(h, 3)] = grad_gate[rows, values]
            last = since[j * SPAN + SPAN - 1 : j * SPAN + SPAN, lanes]
            d_last = last * jnp.sum(prev.astype(F32) * after, axis=0, keepdims=True)
            ld_sum[rows, lanes] = grad_ld[rows, lanes] + d_last
            packet[values] = keep * (after * last + dot(gm, qd.astype(BF), 0, 0))
    d_log = ld_sum[...] + dot(downs[0], d_since[...]) + dot(downs[1], d_towards[...])
    logits = dot(rank[...], up[...]) + bias[...]
    gl = (d_log * (1.0 / decay_scale) * jax.nn.sigmoid(-logits)).astype(BF)
    up_sum[...] += dot(rank[...], gl, 0, 0)
    bias_sum[0:1, :] += jnp.sum(gl.astype(F32), axis=0, keepdims=True)
    rank_part[...] = dot(up[...], gl, 1, 1)
    grad_first[...] = (
        dot(grad_project[:, :HEAD], weights[in_rows(0), :])
        + dot(grad_project[:, HEAD:], weights[in_rows(1), :])
    ).astype(BF)


def source_back_kernel(
    src, normed, gf_a, gf_b, rank_a, rank_b, w_down, gain, grad_hidden,
    own, cross, dealt, down_sum, gain_sum,
):
    low = (rank_a[...] + rank_b[...]).astype(BF)
    gf = gf_a[...].astype(F32) + gf_b[...].astype(F32) + dot(low, w_down[...], 0, 0)
    x = src[...].astype(F32)
    inv = rms_scale(x)
    normal = x * inv
    gain_sum[0:1, :] += jnp.sum(gf * normal, axis=0, keepdims=True)
    e = gf * gain[...]
    dealt[...] = (
        grad_hidden[...] + inv * (e - normal * jnp.mean(e * normal, axis=-1, keepdims=True))
    ).astype(BF)
    down_sum[...] += dot(low, normed[...])
    quarter = own.shape[2]
    at_x, at_core = lax.axis_index("x"), lax.axis_index("core")
    for out, half in ((own, at_x), (cross, 1 - at_x)):
        col = pl.multiple_of((2 * half + at_core) * quarter, 128)
        for j in range(TILE // SPAN):
            out[j] = dealt[j * SPAN : (j + 1) * SPAN, pl.ds(col, quarter)]


def back_kernel(nd, spans, reach, direct, f, table, act, grad_gu, normed, cot, qkvg, log_decay, grad_mixed, packet_in,
                factors, out_own, out_cross, ups, downs, level, level_t, *rest):
    n_sums = 4 if direct else 3
    (leaving, grad_qk_o, grad_v_o, grad_ld_o, gath_o, *sums), rest = rest[: 5 + n_sums], rest[5 + n_sums :]
    (grad_qk, grad_v, grad_ld, sent_packets, got_packets), rest = rest[:5], rest[5:]
    (carry_send, carry_recv, out_sems), rest = rest[:3], rest[3:]
    (joined, sent, gath), rest = rest[:3], rest[3:]
    undeal_sems, rest = rest[:4], rest[4:]
    pitch = act.shape[1] // 2
    tiles = spans * SPAN // TILE
    nz = nd // 2
    carry = Carry(nd, reach, -1, leaving, sent_packets, got_packets, carry_send, carry_recv)
    enter(nd, carry.shifts())
    undeal = Undeal(nd, spans, table, out_own, out_cross, joined, sent, gath, undeal_sems)
    undeal.begin()
    leaving[: 2 * DV] = packet_in[...]
    leaving[2 * DV :] = factors[...]
    carry.send(0)
    outgoing = []

    def store(value, out):
        outgoing.append(pltpu.make_async_copy(value, out, out_sems.at[len(outgoing)]))
        outgoing[-1].start()

    def at(ref, i):
        return ref.at[pl.ds(pl.multiple_of(i * TILE, TILE), TILE), :]

    def tile(i, _):
        within_back_kernel(
            at(qkvg, i), at(log_decay, i), at(grad_mixed, i), ups, downs, level, level_t,
            at(grad_qk, i), at(grad_v, i), at(grad_ld, i),
        )
        return 0

    def some(first, last):
        return lambda: lax.fori_loop(first, last, tile, 0)

    stages = list(range(carry.run()))

    def advance():
        if stages:
            carry.step(stages.pop(0))

    if direct:
        accs, rest = rest[:3], rest[3:]
        chains = [
            Collapse(nd, order, acc, pitch, low, count, rest[3 * k], rest[3 * k + 1 : 3 * k + 3])
            for k, (acc, order, low, count) in enumerate(
                ((accs[0], 0, 0, f), (accs[1], 1, 0, f), (accs[2], 0, 0, f // 2), (accs[2], 1, f // 2, f // 2))
            )
        ]
        weight_grad_into(accs[0], grad_gu.at[:, pl.ds(0, 2 * pitch)], normed, 128)
        chains[0].begin()
        advance()
        weight_grad_into(accs[1], grad_gu.at[:, pl.ds(2 * pitch, 2 * pitch)], normed, 128)
        chains[1].begin()
        advance()
        undeal.exchange()
        for kz in [k % nz for k in range(1, nz + 1)]:
            chains[0].second(kz)
        weight_grad_into(accs[2], act, cot, 128)
        for kz in [k % nz for k in range(1, nz + 1)]:
            chains[1].second(kz)
        chains[2].begin()
        chains[3].begin()
        advance()
        for kz in [k % nz for k in range(1, nz + 1)]:
            chains[0].third(kz)
            chains[1].third(kz)
            some(kz, kz + 1)()
        progress(chains[2:], nz, [some(nz, tiles)])
        for chain, out in zip(chains, sums):
            chain.finish(out)
    else:
        undeal.exchange()
        weight_grad_into(sums[0], grad_gu.at[:, pl.ds(0, 2 * pitch)], normed, 128)
        weight_grad_into(sums[1], grad_gu.at[:, pl.ds(2 * pitch, 2 * pitch)], normed, 128)
        weight_grad_into(sums[2], act, cot, 128)
        some(0, tiles)()
        while stages:
            advance()
    store(grad_qk, grad_qk_o)
    store(grad_v, grad_v_o)
    store(grad_ld, grad_ld_o)
    for k in range(1, nd):
        undeal.arrive(k)
    store(gath, gath_o)
    undeal.finish()
    for copy in outgoing:
        copy.wait()


def last_kernel(nd, spans, direct, table, keep, qkvg, log_decay, grad_mixed, before, leaving, grad_qk, grad_v, grad_ld,
                grad_gate, rank, up, bias, ups, downs, weights, src, normed, grad_hidden, gain, po_in, *rest):
    n_sums = 4 if direct else 1
    (gath_o, down_sum, gain_sum, up_sum, bias_sum, *sums), rest = rest[: 5 + n_sums], rest[5 + n_sums :]
    (packet, grad_project, grad_first, grad_first_other, rank_part, rank_other), rest = rest[:6], rest[6:]
    (d_since, d_towards, ld_sum, dealt), rest = rest[:4], rest[4:]
    (gf_send, gf_recv, rk_send, rk_recv, out_sems), rest = rest[:5], rest[5:]
    (own, cross, joined, sent, gath), rest = rest[:5], rest[5:]
    undeal_sems, rest = rest[:6], rest[6:]
    tiles = spans * SPAN // TILE
    per_tile = TILE // SPAN
    nz = nd // 2
    enter(nd)
    core = lax.axis_index("core")
    undeal = Undeal(nd, spans, table, own, cross, joined, sent, gath, undeal_sems)
    chains = []
    if direct:
        (po_acc, pi_acc), rest = rest[:2], rest[2:]
        halves = ((pi_acc, 0, HEAD), (pi_acc, 1, HEAD), (po_acc, 0, DV), (po_acc, 1, DV))
        chains = [
            Collapse(
                nd, order, acc, size, order * size // 2, size // 2, rest[3 * k], rest[3 * k + 1 : 3 * k + 3]
            )
            for k, (acc, order, size) in enumerate(halves)
        ]
        fill = pltpu.make_async_copy(po_in, po_acc, out_sems.at[0])
        fill.start()
        fill.wait()
        chains[2].begin()
        chains[3].begin()
    packet[...] = leaving[...]
    for ref in (down_sum, gain_sum, up_sum, bias_sum):
        ref[...] = jnp.zeros_like(ref)

    def at(ref, i):
        return ref.at[pl.ds(pl.multiple_of(i * TILE, TILE), TILE), :]

    def swap_first(i):
        return copy_to(at(grad_first, i), at(grad_first_other, i), gf_send.at[i], gf_recv.at[i], {"core": 1 - core})

    def swap_rank(i):
        return copy_to(rank_part.at[i], rank_other.at[i], rk_send.at[i], rk_recv.at[i], {"core": 1 - core})

    def body(step, _):
        i = tiles - 1 - step
        project_back_kernel(
            i, keep, at(qkvg, i), at(log_decay, i), at(grad_mixed, i), before.at[pl.ds(i * per_tile, per_tile)],
            at(grad_qk, i), at(grad_v, i), at(grad_ld, i), at(grad_gate, i), at(rank, i), up, bias, ups, downs, weights,
            at(grad_project, i), at(grad_first, i), rank_part.at[i], packet, up_sum, bias_sum,
            d_since, d_towards, ld_sum,
        )
        swap_first(i).start()
        swap_rank(i).start()
        return 0

    lax.fori_loop(0, tiles, body, 0)
    if direct:
        for kz in [k % nz for k in range(1, nz + 1)]:
            chains[2].second(kz)
            chains[3].second(kz)

    def finish_tile(step, _):
        i = tiles - 1 - step
        swap_first(i).wait()
        swap_rank(i).wait()
        source_back_kernel(
            at(src, i), at(normed, i), at(grad_first, i), at(grad_first_other, i), rank_part.at[i], rank_other.at[i],
            weights.at[pl.ds(0, 16), :], gain, at(grad_hidden, i),
            own.at[pl.ds(i * per_tile, per_tile)], cross.at[pl.ds(i * per_tile, per_tile)],
            dealt, down_sum, gain_sum,
        )
        return 0

    lax.fori_loop(0, tiles, finish_tile, 0)
    undeal.begin()
    if direct:
        weight_grad_into(pi_acc, grad_project, normed, 128)
        chains[0].begin()
        chains[1].begin()
        for kz in [k % nz for k in range(1, nz + 1)]:
            chains[2].third(kz)
            chains[3].third(kz)
    else:
        weight_grad_into(sums[0], grad_project, normed, 128)
    undeal.exchange()
    arrivals = [functools.partial(undeal.arrive, k) for k in range(1, nd)]
    if direct:
        for kz in [k % nz for k in range(1, nz + 1)]:
            chains[0].second(kz)
            chains[1].second(kz)
            if arrivals:
                arrivals.pop(0)()
        for kz in [k % nz for k in range(1, nz + 1)]:
            chains[0].third(kz)
            chains[1].third(kz)
            if arrivals:
                arrivals.pop(0)()
        chains[2].finish(sums[2])
        chains[3].finish(sums[3])
    for arrive in arrivals:
        arrive()
    undeal.finish()
    out = pltpu.make_async_copy(gath, gath_o, out_sems.at[0])
    out.start()
    if direct:
        chains[0].finish(sums[0])
        chains[1].finish(sums[1])
    out.wait()


def remote(kernel, ins, specs, outs, out_specs, scratch, name, number, us):
    return pl.pallas_call(
        kernel,
        in_specs=specs,
        out_specs=out_specs,
        out_shape=outs,
        scratch_shapes=scratch,
        name=name,
        compiler_params=pltpu.CompilerParams(
            vmem_limit_bytes=VMEM_LIMIT, collective_id=number, has_side_effects=True
        ),
        cost_estimate=cost(us),
    )(*ins)


def all_sum(value, axes, sizes):
    for axis, size in zip(axes, sizes):
        bit = 1
        while bit < size:
            value = value + lax.ppermute(value, axis, [(i, i ^ bit) for i in range(size)])
            bit *= 2
    return value


def square_sum(array):
    return jnp.sum(array * array)


def adam_update(weight, grad, first, second, factor, decay_rate):
    clipped = grad * factor
    first_new = beta_one * first + (1.0 - beta_one) * clipped
    second_new = beta_two * second + (1.0 - beta_two) * clipped * clipped
    first_hat = first_new / (1.0 - beta_one**adam_step)
    second_hat = second_new / (1.0 - beta_two**adam_step)
    master = weight.astype(F32)
    change = -learn_rate * (first_hat / (jnp.sqrt(second_hat) + adam_eps) + decay_rate * master)
    return (grad, first_new, second_new, change)


def swap(value, axis):
    return lax.ppermute(value, axis, [(0, 1), (1, 0)])


def on_device(
    tokens, cotangent, seq_extra, deal, proj_in, decay_down, decay_up, decay_bias, head_gain, proj_out, block_gains,
    ffn_in, ffn_out, first_proj_in, second_proj_in, first_decay_down, second_decay_down, first_decay_up,
    second_decay_up, first_decay_bias, second_decay_bias, first_head_gain, second_head_gain, first_proj_out,
    second_proj_out, first_block_gains, second_block_gains, first_ffn_in, second_ffn_in, first_ffn_out, second_ffn_out,
):
    d = tokens.shape[1]
    nd = lax.axis_size("dp")
    nz = nd // 2
    dp, x, core = lax.axis_index("dp"), lax.axis_index("x"), lax.axis_index("core")
    z, y = dp // 2, dp % 2
    tensor = 2 * x + core
    per_dev = tokens.shape[0] // SPAN
    spans = per_dev // 2
    rows = spans * SPAN
    tiles = rows // TILE
    capacity = -(-per_dev // nd)
    quarter = d // 4
    f = ffn_out.shape[0]
    w = d // nd
    direct = w % 128 == 0

    recv_slot, send_local, back_local, home_slot = deal_tables(deal, nd, per_dev, capacity, dp)
    mine = lax.dynamic_slice_in_dim(recv_slot, x * spans, spans)
    theirs = lax.dynamic_slice_in_dim(recv_slot, (1 - x) * spans, spans)
    span_ids = (dp * 2 + x) * spans + jnp.arange(spans, dtype=jnp.int32)
    keep = 1 - span_starts(seq_extra, span_ids)
    other_quarter = 2 * (1 - x) + core
    quarters = jnp.stack([tensor, other_quarter, 2 * x + 1 - core, 2 * (1 - x) + 1 - core])
    ints = jnp.concatenate([quarters, jnp.stack([core, z, y, x]), keep]).astype(jnp.int32)
    ups, downs, level, level_t = level_matrices()

    hh, ho, hf = HEAD // 2, DV // 2, f // 2
    pitch = up_to(f, 128)
    ffn_t = ffn_in.reshape(w, 2 * f).T
    shard_p = jnp.concatenate([decay_down.T, proj_in.reshape(w, HEAD).T, proj_out.reshape(DV, w)], axis=0)
    shard_f = jnp.concatenate([ffn_t[:f], ffn_out, ffn_t[f:]], axis=0)

    def fit(parts):
        return jnp.concatenate(parts, axis=0)

    table = jnp.concatenate([send_local, mine, theirs]).astype(jnp.int32)
    if not direct:

        def gathered(shard):
            return jnp.swapaxes(lax.all_gather(shard, "dp", axis=0), 0, 1).reshape(shard.shape[0], d)

        def halves(shard):
            own, other = gathered(shard), gathered(swap(shard, "x"))
            return jnp.where(x == 0, fit([own, other]), fit([other, own]))

        shard_p, shard_f = halves(shard_p), halves(shard_f)

    up_own = decay_up.reshape(16, DK)
    bias_own = decay_bias.reshape(1, DK)
    small_own = jnp.concatenate([up_own.astype(F32), bias_own, jnp.zeros((7, DK), F32)], axis=0)
    small_other = swap(small_own, "x")
    small_both = jnp.where(
        x == 0,
        jnp.concatenate([small_own, small_other], axis=1),
        jnp.concatenate([small_other, small_own], axis=1),
    )
    up, bias = small_both[:16].astype(BF), small_both[16:17]
    gain_one, gain_two = block_gains[0:1], block_gains[1:2]
    head_row = head_gain.reshape(1, DV)

    def tall(cols, dtype=BF):
        return sds(rows, cols, dtype=dtype)

    nlev = LEVELS + 2
    sequence = nd * 2
    reach = -(-(MAX_SPANS - 1) // spans)
    (src, cot, weights, w_ffn, normed_first, qkvg, log_decay, rank, mixed, gated, attn, before, attn_other,
     factors) = forward(
        table, keep.astype(jnp.int32), tokens, cotangent, shard_p, shard_f, gain_one, up, bias, head_row, ups, level,
        nd, spans, reach, direct,
    )
    ff = 2 * f
    hidden, normed_second, act, grad_gu, keep_out, send_out, grad_second = run(
        functools.partial(ffn_kernel, f), (tiles,),
        [SMEM] + [rows_spec(d)] * 4 + [whole_spec(1, d), whole_spec(3 * ff, d)],
        [rows_spec(d), rows_spec(d), rows_spec(2 * pitch), rows_spec(4 * pitch), rows_spec(2 * quarter),
         rows_spec(2 * quarter), rows_spec(d)],
        [tall(d, F32), tall(d), tall(2 * pitch), tall(4 * pitch), tall(2 * quarter), tall(2 * quarter), tall(d)],
        [pltpu.VMEM((TILE, d), BF)],
        "ffn", 34,
    )(ints, src, attn, attn_other, cot, gain_two, w_ffn)
    gs_other = swap(grad_second, "core")
    recv_out = swap(send_out, "core")

    def plain_shard(full, f_rows):
        full = jnp.swapaxes(full.reshape(2 * f_rows, nd, w), 0, 1)
        total = lax.psum_scatter(full, "dp", scatter_dimension=0, tiled=True)[0].astype(F32)
        keep_rows = lax.dynamic_slice_in_dim(total, x * f_rows, f_rows)
        give_rows = lax.dynamic_slice_in_dim(total, (1 - x) * f_rows, f_rows)
        return keep_rows + swap(give_rows, "x")

    grad_hidden, grad_mixed, grad_gate, gain_second, head_part, packet_back, out_own, out_cross, acc_po = run(
        functools.partial(out_back_kernel, tiles), (tiles,),
        [SMEM] + [rows_spec(d, tiles)] * 4
        + [whole_spec(1, d), whole_spec(2 * PROJ_ROWS, d), rows_spec(2 * DV, tiles), rows_spec(2 * DV, tiles),
           rows_spec(2 * HEAD, tiles), rows_spec(2 * DK, tiles), whole_spec(1, DV), whole_spec(nlev, TILE, TILE),
           rows_spec(2 * quarter, tiles), rows_spec(2 * quarter, tiles)],
        [rows_spec(d, tiles), rows_spec(2 * DV, tiles), rows_spec(2 * DV, tiles), whole_spec(8, d),
         whole_spec(8, DV), whole_spec(2 * DV, DK), rows_spec(quarter, tiles), rows_spec(quarter, tiles),
         whole_spec(2 * DV, d)],
        [tall(d, F32), tall(2 * DV), tall(2 * DV), sds(8, d), sds(8, DV), sds(2 * DV, DK), tall(quarter),
         tall(quarter), sds(2 * DV, d, dtype=BF)],
        [pltpu.VMEM((2 * DV, d), F32), pltpu.VMEM((2, DV, DK), F32), pltpu.VMEM((8, d), F32), pltpu.VMEM((8, DV), F32)],
        "out_back", 19,
    )(ints, hidden, cot, grad_second, gs_other, gain_two, weights, gated, mixed, qkvg, log_decay, head_row, ups,
      keep_out, recv_out)

    dma = pltpu.SemaphoreType.DMA
    steps = len(carry_widths(reach)[0]) + 2
    shape_qk, shape_v, shape_ld = (rows, 4 * DK), (rows, 2 * DV), (rows, 2 * DK)
    buffers, sems = undeal_scratch(nd, per_dev, spans, quarter, capacity, False)
    scratch = [pltpu.VMEM(shape_qk, F32), pltpu.VMEM(shape_v, BF), pltpu.VMEM(shape_ld, F32)]
    scratch += [pltpu.VMEM((steps - 1, 2 * DV + 16, DK), BF), pltpu.VMEM((steps, 2 * DV + 16, DK), BF)]
    scratch += [dma((steps,)), dma((steps,)), dma((4,))] + buffers[2:] + sems
    if direct:
        sums = [sds(f, w), sds(f, w), sds(f // 2, w), sds(f // 2, w)]
        scratch += [pltpu.VMEM((2 * pitch, d), BF)] * 3
        for out in sums:
            scratch += collapse_scratch(nd, out.shape[0], w)
    else:
        sums = [sds(2 * pitch, d, dtype=BF)] * 3
    leaving, grad_qk, grad_v, grad_ld, back_out, *sums_f = remote(
        functools.partial(back_kernel, nd, spans, reach, direct, f),
        (back_local, act, grad_gu, normed_second, cot, qkvg, log_decay, grad_mixed, packet_back, factors,
         out_own.reshape(spans, SPAN, quarter), out_cross.reshape(spans, SPAN, quarter), ups, downs, level, level_t),
        [SMEM] + [VMEM] * 15,
        [sds(2 * DV + 16, DK), sds(*shape_qk), sds(*shape_v, dtype=BF), sds(*shape_ld),
         sds(nd * capacity, SPAN, quarter, dtype=BF)] + sums,
        [VMEM] + [ANY] * 4 + [VMEM] * len(sums),
        scratch, "back_all", 1, 110,
    )
    if direct:
        shard_gate, shard_up, shard_fo = sums_f[0], sums_f[1], fit(sums_f[2:])
    else:
        shard_gate, shard_up, shard_fo = (plain_shard(v, pitch)[:f] for v in sums_f)
    block_out = home([back_out.reshape(-1, quarter)], home_slot, [jnp.int32(0)], "block_out_home")

    buffers, sems = undeal_scratch(nd, per_dev, spans, quarter, capacity, True)
    scratch = [
        pltpu.VMEM((2 * DV + 16, DK), F32), pltpu.VMEM((rows, 2 * HEAD), BF), pltpu.VMEM((rows, d), BF),
        pltpu.VMEM((rows, d), BF), pltpu.VMEM((tiles, 16, TILE), F32), pltpu.VMEM((tiles, 16, TILE), F32),
        pltpu.VMEM((TILE, 2 * DK), BF), pltpu.VMEM((TILE, 2 * DK), BF), pltpu.VMEM((TILE, 2 * DK), F32),
        pltpu.VMEM((TILE, d), BF), dma((tiles,)), dma((tiles,)), dma((tiles,)), dma((tiles,)), dma((1,)),
    ] + buffers + sems
    if direct:
        sums = [sds(hh, w), sds(hh, w), sds(ho, w), sds(ho, w)]
        scratch += [pltpu.VMEM((2 * DV, d), BF), pltpu.VMEM((2 * HEAD, d), BF)]
        for out in sums:
            scratch += collapse_scratch(nd, out.shape[0], w)
    else:
        sums = [sds(2 * HEAD, d, dtype=BF)]
    back_grad, down_grad, gain_first, up_grad, bias_grad, *sums_p = remote(
        functools.partial(last_kernel, nd, spans, direct),
        (back_local, keep.astype(jnp.int32), qkvg, log_decay, grad_mixed, before, leaving, grad_qk, grad_v, grad_ld,
         grad_gate, rank, up, bias, ups[LEVELS:], downs[LEVELS:], weights, src, normed_first, grad_hidden, gain_one,
         acc_po),
        [SMEM, SMEM] + [VMEM] * 19 + [ANY],
        [sds(nd * capacity, SPAN, d, dtype=BF), sds(16, d), sds(8, d), sds(16, 2 * DK), sds(8, 2 * DK)] + sums,
        [ANY] + [VMEM] * (4 + len(sums)),
        scratch, "finish_all", 2, 100,
    )
    if direct:
        shard_pi, shard_po = fit(sums_p[:2]), fit(sums_p[2:])
    else:
        shard_pi, shard_po = plain_shard(sums_p[0], HEAD), plain_shard(acc_po, DV)
    token_grad = home([back_grad.reshape(-1, d)], home_slot, [jnp.int32(0)], "token_grad_home")

    small = jnp.concatenate(
        [
            gain_first[0].reshape(-1, 128),
            gain_second[0].reshape(-1, 128),
            down_grad.reshape(-1, 128),
            up_grad.reshape(-1, 128),
            bias_grad[0].reshape(-1, 128),
            head_part[0].reshape(-1, 128),
        ],
        axis=0,
    )
    small = all_sum(small, ("x", "dp"), (2, nd))
    rows_d = d // 128
    cuts = [rows_d, rows_d, 16 * rows_d, 32, 2, 2]
    starts = [sum(cuts[:k]) for k in range(len(cuts) + 1)]
    gain_first, gain_second, down_total, up_total, bias_total, head_total = (
        small[starts[k] : starts[k + 1]].reshape(-1) for k in range(len(cuts))
    )
    head_total = head_total + swap(head_total, "core")
    gains_total = jnp.stack([gain_first, gain_second])
    down_total = down_total.reshape(16, d)
    shard_down = lax.dynamic_slice_in_dim(down_total, dp * w, w, 1).T
    up_total = up_total.reshape(16, 2, DK)
    up_total = jnp.where(x == 0, up_total[:, 0:1], up_total[:, 1:2])
    bias_total = bias_total.reshape(2, DK)
    bias_total = jnp.where(x == 0, bias_total[0:1], bias_total[1:2])

    shard_in = shard_pi.T.reshape(proj_in.shape)
    shard_out = shard_po.reshape(proj_out.shape)
    shard_ffn_in = jnp.stack([shard_gate.T, shard_up.T], axis=1)
    shard_ffn_out = shard_fo
    n_dev = 4 * nd
    local_sq = (
        square_sum(shard_pi)
        + square_sum(shard_po)
        + square_sum(shard_gate)
        + square_sum(shard_up)
        + square_sum(shard_fo)
        + square_sum(shard_down) / 4
        + (square_sum(up_total) + square_sum(bias_total)) / nd
        + (square_sum(head_total) + square_sum(gains_total)) / n_dev
    )
    norm_sq = all_sum(jnp.broadcast_to(local_sq, (8, 128)), ("core", "x", "dp"), (2, 2, nd))
    grad_norm = jnp.sqrt(norm_sq[0, 0])
    clip_norm = clip_scale * math.sqrt(PARAMS)
    factor = jnp.minimum(1.0, clip_norm / (grad_norm + 1e-06))
    update_in = adam_update(proj_in, shard_in, first_proj_in, second_proj_in, factor, weight_decay)
    update_down = adam_update(decay_down, shard_down, first_decay_down, second_decay_down, factor, weight_decay)
    update_up = adam_update(decay_up, up_total, first_decay_up, second_decay_up, factor, weight_decay)
    update_bias = adam_update(decay_bias, bias_total, first_decay_bias, second_decay_bias, factor, 0.0)
    update_head = adam_update(head_gain, head_total, first_head_gain, second_head_gain, factor, 0.0)
    update_out = adam_update(proj_out, shard_out, first_proj_out, second_proj_out, factor, weight_decay)
    update_gains = adam_update(block_gains, gains_total, first_block_gains, second_block_gains, factor, 0.0)
    update_ffn_in = adam_update(ffn_in, shard_ffn_in, first_ffn_in, second_ffn_in, factor, weight_decay)
    update_ffn_out = adam_update(ffn_out, shard_ffn_out, first_ffn_out, second_ffn_out, factor, weight_decay)
    return (
        block_out, token_grad, grad_norm, *update_in, *update_down, *update_up, *update_bias, *update_head,
        *update_out, *update_gains, *update_ffn_in, *update_ffn_out,
    )


def solution(mesh):
    nd, nt = mesh.shape["dp"], mesh.shape["tensor"]
    fine = Mesh(mesh.devices.reshape(nd, nt // 2, 2), ("dp", "x", "core"))
    t = ("x", "core")
    w_specs = {
        "proj_in": P("dp", t, None),
        "decay_down": P("dp", None),
        "decay_up": P(None, t, None),
        "decay_bias": P(t, None),
        "head_gain": P(),
        "proj_out": P(t, None, "dp"),
        "block_gains": P(),
        "ffn_in": P("dp", None, t),
        "ffn_out": P(t, "dp"),
    }
    specs = list(w_specs.values())
    placed = [P("dp", None), P("dp", None), P(), P()] + specs
    results = [P("dp", t), P("dp", None), P()]
    for spec in specs:
        placed += [spec] * 2
        results += [spec] * 4
    return jax.shard_map(
        on_device,
        mesh=fine,
        in_specs=tuple(placed),
        out_specs=tuple(results),
        check_vma=False,
    )
```

time: 803 us -> 629 us (0.78)
  Pallas kernels: 226 us -> 526 us
  waiting for transfers between devices: 243 us -> 19.8 us
  starting transfers between devices: 188 us -> 10.3 us
  other arithmetic: 83.8 us -> 32.6 us
  local copies, waits for them, and re-layouts: 39.9 us -> 26.9 us
    pallas_call x20 -> x5, Pallas kernels: 215 us -> 515 us  [the longest x2 262 us: remote(): pl.pallas_call(kernel, in_specs=specs, out_specs=out_specs, out_shape=out...]
    ppermute x78 -> x0, starting transfers between devices: 133 us -> none  [the longest x21 33.9 us: ring_sum(): a = lax.ppermute(a, 'dp', forward).astype(F32) + first(s + 1).astype(F32)]
    ppermute x78 -> x0, waiting for transfers between devices: 119 us -> none  [the longest x21 32.7 us: ring_sum(): a = lax.ppermute(a, 'dp', forward).astype(F32) + first(s + 1).astype(F32)]
    ppermute x46 -> x4, waiting for transfers between devices: 99.2 us -> 2.1 us  [swap(): return lax.ppermute(value, axis, [(0, 1), (1, 0)])]
    convert_element_type x36 -> x1, other arithmetic: 30.5 us -> 0.73 us  [on_device(): up_own.astype(F32)]
    ppermute x46 -> x4, starting transfers between devices: 25 us -> 3.58 us  [swap(): return lax.ppermute(value, axis, [(0, 1), (1, 0)])]
    all_to_all x4 -> x0, starting transfers between devices: 21.1 us -> none  [the longest x2 10.7 us: dealt(): lax.all_to_all(picked, 'dp', split_axis=0, concat_axis=0, tiled=True)]
    unnamed x203 -> x92, local copies, waits for them, and re-layouts: 17.2 us -> 9.76 us
  transfers between devices with their start and end apart: 137 -> 13, of which waited for: 54 -> 10; matrix products, arithmetic and copies ran while one was open for 14% -> 4% of each run, Pallas kernels for 23% -> 2%
where the time goes in v2:
time: 629 us; the launch traced here: 626 us
  Pallas kernels  526 us (84%)
  other arithmetic  32.6 us (5%)
  local copies, waits for them, and re-layouts  26.9 us (4%)
  waiting for transfers between devices  19.8 us (3%)
  starting transfers between devices  10.3 us (2%)
  between operations  9.95 us (2%)
    pallas_call x2, Pallas kernels, remote(): pl.pallas_call(kernel, in_specs=specs, out_specs=out_specs, out_shape=out...  262 us
    pallas_call x1, Pallas kernels, forward(): pl.pallas_call(kernel, in_specs=[SMEM, SMEM, ANY, ANY, ANY, ANY] + [VMEM]...  194 us
    pallas_call x1, Pallas kernels, on_device(): run(functools.partial(ffn_kernel, f), (tiles,), [SMEM] + [rows_spec(d)] *...  40.6 us
    pallas_call x1, Pallas kernels, on_device(): run(functools.partial(out_back_kernel, tiles), (tiles,), [SMEM] + [rows_s...  18.9 us
    ppermute x9, waiting for transfers between devices, all_sum(): lax.ppermute(value, axis, [(i, i ^ bit) for i in range(size)])  17.7 us
  transfers between devices with their start and end apart: 13, of which 10 were waited for; matrix products, arithmetic and copies ran while one was open for 4% of the time, Pallas kernels for 2%

profile of v2, /device:TPU:0, one launch (start us, length us, event | category | flops | bytes accessed | tf_op | source)
XLA Modules:
  0.0 625.8 jit_solution(3499321320024895240)
XLA Ops:
  2.1 2.9 collective-permute-start
  11.9 1.4 fusion.78
  17.5 2.2 select_select_fusion
  23.4 194.2 %forward.1 = (bf16[1280,1024]{1,0:T(8,128)(2,1)}, bf16[1280,1024]{1,0:T(8,128)(2,1)}, bf16[2080,1024]{1,0:T(8,128)(2,1)}, bf16[4224,1024]{1,0:T(8,128)(2,1)}, bf...) custom-call(s32[80]{0:T(128)} %pad_add_fusion.1.refs_0_, ...), custom_call_target="tpu_custom_call" | custom-call | flops 149999992832 | bytes 150000000 | tf_op jit(solution)/shard_map/forward/pallas_call | solution.py:833
  217.6 40.6 %ffn.1 = (f32[1280,1024]{1,0:T(8,128)}, bf16[1280,1024]{1,0:T(8,128)(2,1)}, bf16[1280,1536]{1,0:T(8,128)(2,1)}, bf16[1280,3072]{1,0:T(8,128)(2,1)}, bf16[1280,51...) custom-call(s32[28]{0:T(128)} %concatenate.55.ints, ...), custom_call_target="tpu_custom_call" | custom-call | flops 33999998976 | bytes 34000000 | tf_op jit(solution)/shard_map/ffn/pallas_call | solution.py:1520
  261.5 1.7 slice.97.downs
  263.2 1.9 collective-permute-done.2.recv_out
  265.3 1.5 copy-done.40
  266.8 18.9 %out_back.1 = (f32[1280,1024]{1,0:T(8,128)}, bf16[1280,512]{1,0:T(8,128)(2,1)}, bf16[1280,512]{1,0:T(8,128)(2,1)}, f32[8,1024]{1,0:T(8,128)}, f32[8,256]{1,0:T(8...) custom-call(s32[28]{0:T(128)} %concatenate.55.ints, ...), custom_call_target="tpu_custom_call" | custom-call | flops 19000000512 | bytes 19000000 | tf_op jit(solution)/shard_map/out_back/pallas_call | solution.py:1539
  285.7 147.6 %back_all.1 = (f32[528,128]{1,0:T(8,128)}, f32[1280,512]{1,0:T(8,128)}, bf16[1280,512]{1,0:T(8,128)(2,1)}, f32[1280,256]{1,0:T(8,128)}, bf16[40,64,256]{2,1,0:T(...) custom-call(s32[40]{0:T(128)} %reshape.2171.table, ...), custom_call_target="tpu_custom_call" | custom-call | flops 109999996928 | bytes 110000000 | tf_op jit(solution)/shard_map/back_all/pallas_call | solution.py:1400
  433.3 114.1 %finish_all.1 = (bf16[40,64,1024]{2,1,0:T(8,128)(2,1)}, f32[16,1024]{1,0:T(8,128)}, f32[8,1024]{1,0:T(8,128)}, f32[16,256]{1,0:T(8,128)}, f32[8,256]{1,0:T(8,128...) custom-call(s32[40]{0:T(128)} %reshape.2171.table, s32[20]{0:T(128)} %copy-done.39, ...), custom_call_target="tpu_custom_call" | custom-call | flops 99999997952 | bytes 100000000 | tf_op jit(solution)/shard_map/finish_all/pallas_call | solution.py:1400
  561.1 1.7 collective-permute-done.3
  562.8 2.0 collective-permute-start.4
  564.7 2.6 collective-permute-done.4
  568.1 4.0 collective-permute-done.5
  574.1 4.6 collective-permute-done.6
  588.3 2.9 collective-permute-done.9
  591.2 1.3 collective-permute-start.10
  594.8 3.3 block_out_home.1
  599.4 7.6 %token_grad_home.1 = f32[2560,1024]{1,0:T(8,128)} custom-call(s32[41]{0:T(128)} %pad_add_fusion.table, bf16[2560,1024]{1,0:T(8,128)(2,1)} %bitcast.82), custom_call_target="tpu_custom_call" | custom-call | flops 4000000000 | bytes 4000000 | tf_op jit(solution)/shard_map/token_grad_home/pallas_call | solution.py:159
  612.6 2.3 add_multiply_fusion.2
  616.3 1.3 fusion.50
  620.8 1.8 add_multiply_fusion.3
  622.7 1.8 add_multiply_fusion
  (220 shorter events, 51.8 us)
Async XLA Ops:
  2.1 20.1 %collective-permute-start = (f32[24,128]{1,0:T(8,128)S(1)}, f32[24,128]{1,0:T(8,128)S(1)}, u32[]{:S(2)}, u32[]{:S(2)}) collective-permute-start(f32[24,128]{1,0:T(8,128)S(1)} %pad_maximum_fusion.3), channel_id=1, source_target_pairs={{0,2},{2,0},{1,3},{3,1},{4,6},{6,4},{5,7},{7,5},{8,10},{10,8},{9,1... | collective-permute-start | bytes 36872 | tf_op jit(solution)/shard_map/ppermute | solution.py:1439
  15.7 201.9 %copy-start = (bf16[8,256,256]{1,2,0:T(8,128)(2,1)}, bf16[8,256,256]{1,2,0:T(8,128)(2,1)S(1)}, u32[]{:S(2)}) copy-start(bf16[8,256,256]{1,2,0:T(8,128)(2,1)S(1)} %get-tuple-element.293) | copy-start | bytes 3145732
  217.6 42.2 %copy-start.38 = (s32[40]{0:T(128)S(1)}, s32[40]{0:T(128)}, u32[]{:S(2)}) copy-start(s32[40]{0:T(128)} %copy-done.37) | copy-start | bytes 484
  217.6 42.2 %copy-start.36 = (s32[40]{0:T(128)S(1)}, s32[40]{0:T(128)}, u32[]{:S(2)}) copy-start(s32[40]{0:T(128)} %copy-done.35) | copy-start | bytes 484
  258.2 7.1 %collective-permute-start.1 = (bf16[1280,1024]{1,0:T(8,128)(2,1)}, bf16[1280,1024]{1,0:T(8,128)(2,1)S(1)}, u32[]{:S(2)}, u32[]{:S(2)}) collective-permute-start(bf16[1280,1024]{1,0:T(8,128)(2,1)} %get-tuple-element.98.gs_a), channel_id=1, source_target_pairs={{0,1},{1,0},{2,3},{3,2},{4,5},{5,4},{6,7},{7,6},{8,9},{9,8},{10,11... | collective-permute-start | bytes 7864328 | tf_op jit(solution)/shard_map/ppermute | solution.py:1439
  258.3 6.7 %collective-permute-start.2 = (bf16[1280,512]{1,0:T(8,128)(2,1)}, bf16[1280,512]{1,0:T(8,128)(2,1)}, u32[]{:S(2)}, u32[]{:S(2)}) collective-permute-start(bf16[1280,512]{1,0:T(8,128)(2,1)} %get-tuple-element.103), channel_id=1, source_target_pairs={{0,1},{1,0},{2,3},{3,2},{4,5},{5,4},{6,7},{7,6},{8,9},{9,8},{10,11... | collective-permute-start | bytes 3932168 | tf_op jit(solution)/shard_map/ppermute | solution.py:1439
  433.3 119.2 %copy-start.5 = (f32[704,128]{1,0:T(8,128)S(1)}, f32[704,128]{1,0:T(8,128)}, u32[]{:S(2)}) copy-start(f32[704,128]{1,0:T(8,128)} %get-tuple-element.125) | copy-start | bytes 1081348
  433.3 126.5 %copy-start.6 = (f32[704,128]{1,0:T(8,128)S(1)}, f32[704,128]{1,0:T(8,128)}, u32[]{:S(2)}) copy-start(f32[704,128]{1,0:T(8,128)} %get-tuple-element.126) | copy-start | bytes 1081348
  547.4 40.6 %copy-start.20 = (s32[8,40]{1,0:T(8,128)S(1)}, s32[8,40]{1,0:T(8,128)}, u32[]{:S(2)}) copy-start(s32[8,40]{1,0:T(8,128)} %copy-done.19) | copy-start | bytes 3844
  547.4 40.6 %copy-start.22 = (s32[8,40]{1,0:T(8,128)S(1)}, s32[8,40]{1,0:T(8,128)}, u32[]{:S(2)}) copy-start(s32[8,40]{1,0:T(8,128)} %copy-done.21) | copy-start | bytes 3844
  547.4 40.6 %copy-start.29 = (s32[8,40]{1,0:T(8,128)S(1)}, s32[8,40]{1,0:T(8,128)}, u32[]{:S(2)}) copy-start(s32[8,40]{1,0:T(8,128)} %get-tuple-element.335) | copy-start | bytes 3844
  547.5 45.6 %copy-start.12 = (f32[128,1,768]{2,1,0:T(1,128)S(1)}, f32[128,1,768]{2,1,0:T(1,128)}, u32[]{:S(2)}) copy-start(f32[128,1,768]{2,1,0:T(1,128)} %param.45) | copy-start | bytes 1179652
  549.4 44.0 %copy-start.13 = (f32[128,1,768]{2,1,0:T(1,128)S(1)}, f32[128,1,768]{2,1,0:T(1,128)}, u32[]{:S(2)}) copy-start(f32[128,1,768]{2,1,0:T(1,128)} %param.44) | copy-start | bytes 1179652
  557.7 5.0 collective-permute-start.3
  562.8 4.6 collective-permute-start.4
  567.4 4.6 collective-permute-start.5
  568.1 44.5 %copy-start.1 = (f32[704,128]{1,0:T(8,128)}, f32[704,128]{1,0:T(8,128)S(1)}, u32[]{:S(2)}) copy-start(f32[704,128]{1,0:T(8,128)S(1)} %constant_dynamic-update-slice_fusion.4) | copy-start | bytes 1081348
  572.1 6.5 %collective-permute-start.6 = (f32[180,128]{1,0:T(8,128)S(1)}, f32[180,128]{1,0:T(8,128)S(1)}, u32[]{:S(2)}, u32[]{:S(2)}) collective-permute-start(f32[180,128]{1,0:T(8,128)S(1)} %add.663), channel_id=1, source_target_pairs={{0,16},{4,20},{8,24},{12,28},{16,0},{20,4},{24,8},{28,12},{1,17},{... | collective-permute-start | bytes 276488 | tf_op jit(solution)/shard_map/ppermute | solution.py:1418
  579.8 3.9 collective-permute-start.7
  586.2 1.4 collective-permute-start.8
  587.6 3.6 collective-permute-start.9
  591.2 3.6 collective-permute-start.10
  594.8 3.6 collective-permute-start.11
  598.4 9.6 %collective-permute-start.12 = (f32[8,128]{1,0:T(8,128)S(1)}, f32[8,128]{1,0:T(8,128)S(1)}, u32[]{:S(2)}, u32[]{:S(2)}) collective-permute-start(f32[8,128]{1,0:T(8,128)S(1)} %add.675), channel_id=1, source_target_pairs={{0,16},{4,20},{8,24},{12,28},{16,0},{20,4},{24,8},{28,12},{1,17},{... | collective-permute-start | bytes 12296 | tf_op jit(solution)/shard_map/ppermute | solution.py:1418
  (30 other events, 355.1 us)

commit v3 on v2

--- a/solution.py
+++ b/solution.py
@@ -3,6 +3,7 @@
 
 import jax
 import jax.numpy as jnp
+import numpy as np
 from jax import lax
 from jax.experimental import pallas as pl
 from jax.experimental.pallas import tpu as pltpu
@@ -18,7 +19,7 @@
 TILE = 256
 LEVELS = 6
 HEAD = 2 * DK + 2 * DV
-VMEM_LIMIT = 60 * 1024 * 1024
+VMEM_LIMIT = 61 * 1024 * 1024
 BF = jnp.bfloat16
 F32 = jnp.float32
 
@@ -115,10 +116,10 @@
 
 
 def level_matrices():
-    t = jnp.arange(TILE, dtype=jnp.int32)[:, None]
-    u = jnp.arange(TILE, dtype=jnp.int32)[None, :]
+    t = np.arange(TILE, dtype=np.int32)[:, None]
+    u = np.arange(TILE, dtype=np.int32)[None, :]
     ups = []
-    level = jnp.full((TILE, TILE), LEVELS + 1, jnp.int32)
+    level = np.full((TILE, TILE), LEVELS + 1, np.int32)
     for l in range(LEVELS):
         block = SPAN >> l
         half = block // 2
@@ -128,13 +129,13 @@
         left = (t < mid) & (u > t) & (u < mid)
         ups.append(same & (right | left))
         hit = same & (t % block >= half) & (u % block < half)
-        level = jnp.where(hit, l, level)
-    level = jnp.where(t == u, LEVELS, level)
+        level = np.where(hit, l, level)
+    level = np.where(t == u, LEVELS, level)
     same = (t // SPAN) == (u // SPAN)
     ups.append(same & (u <= t))
     ups.append(same & (u > t))
-    ups = jnp.stack(ups).astype(BF)
-    return ups, jnp.swapaxes(ups, 1, 2), level, level.T
+    ups = np.stack(ups).astype(np.float32).astype(BF)
+    return ups, np.ascontiguousarray(np.swapaxes(ups, 1, 2)), level, np.ascontiguousarray(level.T)
 
 
 def home_kernel(count, table, *refs):
@@ -431,6 +432,115 @@
     return [dma((1,)), dma((nd,)), dma((nd,)), dma((CHUNKS,)), dma((CHUNKS,)), dma((CHUNKS + 1,)), dma((CHUNKS + 1,))]
 
 
+SMALL = 184
+
+
+class Small:
+    def __init__(self, nd, pack, sent, got, norms, sems):
+        self.nd, self.pack, self.sent, self.got, self.norms = nd, pack, sent, got, norms
+        self.send, self.recv, self.norm_send, self.norm_recv, self.end_send, self.end_recv = sems
+        self.dp, self.x, self.core = lax.axis_index("dp"), lax.axis_index("x"), lax.axis_index("core")
+
+    def fill(self, gain_first, gain_second, down, up, bias, head):
+        pack = self.pack
+        for r in range(8):
+            lanes = slice(r * 128, (r + 1) * 128)
+            pack[r : r + 1] = gain_first[0:1, lanes]
+            pack[8 + r : 9 + r] = gain_second[0:1, lanes]
+            pack[16 + 16 * r : 32 + 16 * r] = down[:, lanes]
+        for h in range(2):
+            lanes = slice(h * 128, (h + 1) * 128)
+            pack[144 + 16 * h : 160 + 16 * h] = up[:, lanes]
+            pack[176 + h : 177 + h] = bias[0:1, lanes]
+            pack[178 + h : 179 + h] = head[0:1, lanes]
+        pack[180:] = jnp.zeros((4, 128), F32)
+
+    def copy(self, step):
+        if step == 0:
+            target = {"x": 1 - self.x}
+        else:
+            bit = 1 << (step - 1)
+            on = lax.rem(self.dp // bit, 2)
+            target = {"dp": self.dp + bit - 2 * bit * on}
+        return copy_to(self.sent.at[step], self.got.at[step], self.send.at[step], self.recv.at[step], target)
+
+    def steps(self):
+        return self.nd.bit_length()
+
+    def begin(self, step):
+        self.sent[step] = self.pack[...]
+        self.copy(step).start()
+
+    def end(self, step):
+        self.copy(step).wait()
+        self.pack[...] = self.pack[...] + self.got[step]
+
+    def core_copy(self, step, src, dst, target):
+        return copy_to(src, dst, self.end_send.at[step], self.end_recv.at[step], target)
+
+    def head(self):
+        at = self.nd + 5
+        return self.core_copy(0, self.norms.at[at], self.norms.at[at + 1], {"core": 1 - self.core})
+
+    def begin_head(self):
+        self.norms[self.nd + 5] = self.pack[176:184]
+        self.head().start()
+
+    def end_head(self):
+        self.head().wait()
+        self.pack[178:180] = self.pack[178:180] + self.norms[self.nd + 6, 2:4]
+
+    def squares(self):
+        nd, v = self.nd, self.pack[...]
+        v = v * v
+        down = fold(v[16:144])
+        up = fold(v[144:176])
+        row = lax.broadcasted_iota(jnp.int32, (8, 128), 0)
+        tail = v[176:184]
+        tail = jnp.where(row < 2, tail / (2 * nd), jnp.where(row < 4, tail / (4 * nd), 0.0))
+        return (v[0:8] + v[8:16] + down) / (4 * nd) + up / (2 * nd) + tail
+
+    def norm_copy(self, k):
+        return copy_to(
+            self.norms.at[self.nd],
+            self.norms.at[self.dp],
+            self.norm_send.at[k],
+            self.norm_recv.at[k],
+            {"dp": lax.rem(self.dp + k, self.nd)},
+        )
+
+    def begin_norm(self, value):
+        self.norms[self.nd] = value
+        self.norms[self.dp] = value
+        for k in range(1, self.nd):
+            self.norm_copy(k).start()
+
+    def end_norm(self, out):
+        nd = self.nd
+        for k in range(1, nd):
+            self.norm_copy(k).wait()
+        total = self.norms[0]
+        for k in range(1, nd):
+            total = total + self.norms[k]
+        for step, target in ((1, {"x": 1 - self.x}), (2, {"core": 1 - self.core})):
+            at = nd - 1 + 2 * step
+            self.norms[at] = total
+            copy = self.core_copy(step, self.norms.at[at], self.norms.at[at + 1], target)
+            copy.start()
+            copy.wait()
+            total = total + self.norms[at + 1]
+        out[...] = total
+
+
+def small_scratch(nd):
+    dma = pltpu.SemaphoreType.DMA
+    steps = nd.bit_length()
+    return [
+        pltpu.VMEM((steps, SMALL, 128), F32), pltpu.VMEM((steps, SMALL, 128), F32), pltpu.VMEM((nd + 7, 8, 128), F32),
+        dma((steps,)), dma((steps,)), dma((nd,)), dma((nd,)), dma((3,)), dma((3,)),
+    ]
+
+
 class Undeal:
     def __init__(self, nd, spans, table, own, cross, joined, sent, gath, sems):
         self.nd, self.spans, self.table, self.own, self.cross = nd, spans, table, own, cross
@@ -532,6 +642,10 @@
     return buffers, sems + ([dma((3 * nd,)), dma((3 * nd,))] if wide else [])
 
 
+def fold(value):
+    return jnp.sum(value.reshape(-1, 8, 128), axis=0)
+
+
 class Collapse:
     def __init__(self, nd, order, acc, pitch, low, rows, got, sems):
         self.nz, self.order, self.acc, self.pitch, self.low, self.rows = nd // 2, order, acc, pitch, low, rows
@@ -592,12 +706,13 @@
         if kz:
             self.copy(3, 0, kz).start()
 
-    def finish(self, out):
+    def finish(self, out, squares):
         total = self.window(0, 0, 0)[...].astype(F32)
         for kz in range(1, self.nz):
             self.copy(3, 0, kz).wait_recv()
             total = total + self.got[self.slot(3, 0, kz)].astype(F32)
         out[...] = total
+        squares[...] += fold(total * total)
         for kz in range(self.nz):
             self.copy(1, 0, kz).wait_send()
             self.copy(1, 1, kz).wait_send()
@@ -630,14 +745,6 @@
 
 PROJ_ROWS = 16 + HEAD + DV
 PROJ_CUTS = ((0, 528), (528, 512))
-
-
-FFN_CUTS = 2
-PITCH = 768
-
-
-def up_to(value, step):
-    return -(-value // step) * step
 
 
 def forward_kernel(nd, spans, reach, gather, table, ints, tokens, cotangent, shard_p, shard_f, gain, up, bias, head_gain,
@@ -660,18 +767,21 @@
     if gather:
         w = shard_p.shape[1]
         f3 = shard_f.shape[0]
-        cuts_f = ((0, f3 // 2), (f3 // 2, f3 // 2))
-
-        def window(buffer, pitch, cut, dp, x):
-            low, count = cut
+        f = f3 // 3
+        cuts_p = [(k, low, count, PROJ_ROWS, low) for k, (low, count) in enumerate(PROJ_CUTS)]
+        cuts_f = [
+            (0, 0, f, f, 0), (1, 2 * f, f, f, 4 * f), (0, f, f // 2, f, 2 * f), (1, f + f // 2, f // 2, f, 2 * f + f // 2),
+        ]
+
+        def window(buffer, count, pitch, base, dp, x):
             return buffer.at[
-                pl.ds(pl.multiple_of(x * pitch + low, 16), count), pl.ds(pl.multiple_of(dp * w, 128), w)
+                pl.ds(pl.multiple_of(x * pitch + base, 16), count), pl.ds(pl.multiple_of(dp * w, 128), w)
             ]
 
-        for shard, buffer, cuts, spreads in ((shard_p, wp, PROJ_CUTS, spreads_p), (shard_f, wf, cuts_f, spreads_f)):
-            for order, cut in enumerate(cuts):
-                piece = shard.at[pl.ds(cut[0], cut[1]), :]
-                place = functools.partial(window, buffer, shard.shape[0], cut)
+        for shard, buffer, cuts, spreads in ((shard_p, wp, cuts_p, spreads_p), (shard_f, wf, cuts_f, spreads_f)):
+            for order, low, count, pitch, base in cuts:
+                piece = shard.at[pl.ds(low, count), :]
+                place = functools.partial(window, buffer, count, pitch, base)
                 copy = pltpu.make_async_copy(
                     piece, place(lax.axis_index("dp"), lax.axis_index("x")), own_sems.at[len(local)]
                 )
@@ -703,21 +813,35 @@
     for spread in spreads_p:
         spread.begin()
     deal.exchange()
+    for k in last_first[0:1]:
+        relay_first(spreads_p, k)
+    deal_c.begin()
+    for k in last_z[0:1]:
+        relay_z(spreads_p, k)
+    for k in last_z[1:2]:
+        relay_z(spreads_p, k)
+    for k in last_first[1:2]:
+        relay_first(spreads_p, k)
     for spread in spreads_f:
         spread.begin()
-    deal_c.begin()
-    for k in last_z:
+    for k in last_z[2:3]:
         relay_z(spreads_p, k)
-    for k in last_first:
+    for k in last_first[2:3]:
         relay_first(spreads_p, k)
+    for k in last_first[3:4]:
+        relay_first(spreads_p, k)
+    for k in last_first[0:1]:
+        relay_first(spreads_f, k)
     deal.across()
     deal.release()
     deal_c.exchange()
-    for k in last_z[:1]:
+    for k in last_z[0:1]:
         relay_z(spreads_f, k)
-    for k in last_first[:1]:
+    for k in last_first[1:2]:
         relay_first(spreads_f, k)
     deal.finish()
+    for k in last_z[1:2]:
+        relay_z(spreads_f, k)
     for spread in spreads_p:
         spread.finish()
     for copy in local:
@@ -739,9 +863,9 @@
         return 0
 
     lax.fori_loop(0, tiles // 2, project, 0)
-    for k in last_z[1:2]:
+    for k in last_z[2:3]:
         relay_z(spreads_f, k)
-    for k in last_first[1:2]:
+    for k in last_first[2:3]:
         relay_first(spreads_f, k)
     lax.fori_loop(tiles // 2, tiles, project, 0)
     factors[...] = packet[2 * DV :]
@@ -750,9 +874,7 @@
     store(qkvg, qkvg_o)
     store(log_decay, log_decay_o)
     store(rank, rank_o)
-    for k in last_z[2:]:
-        relay_z(spreads_f, k)
-    for k in last_first[2:]:
+    for k in last_first[3:4]:
         relay_first(spreads_f, k)
 
     def within(i, _):
@@ -815,9 +937,9 @@
         pltpu.VMEM((steps, 2 * DV + 16, DK), BF),
     ]
     scratch += deal_buffers(nd, per_dev, spans, d // 4, cap) + deal_sems(nd) + deal_sems(nd)
-    scratch += [dma((steps,)), dma((steps,)), dma((1,)), dma((1,)), dma((12,)), dma((4,))]
+    scratch += [dma((steps,)), dma((steps,)), dma((1,)), dma((1,)), dma((12,)), dma((6,))]
     if gather:
-        scratch += [dma((4 * nz - 1,)), dma((4 * nz,))] * 4
+        scratch += [dma((4 * nz - 1,)), dma((4 * nz,))] * 6
     outs = [sds(*shape, dtype=dtype) for shape, dtype in kept] + [sds(rows, d, dtype=BF)]
     outs.append(sds(16, DK))
     specs = [ANY] * 13 + [VMEM]
@@ -960,7 +1082,7 @@
 
 
 def ffn_kernel(
-    f, ints, src, attn_a, attn_b, cot, gain, weights,
+    ints, src, attn_a, attn_b, cot, gain, weights,
     hidden, normed, act, grad_gu, keep_out, send_out, grad_second,
     part,
 ):
@@ -969,29 +1091,21 @@
     hidden[...] = hid
     ns = (hid * rms_scale(hid) * gain[...]).astype(BF)
     normed[...] = ns
-    c = cot[...]
-    back, total = None, None
-    for g in range(2):
-        base = 3 * f * g
-        w_gate, w_out, w_up = (slice(base + k * f, base + (k + 1) * f) for k in range(3))
-        gate = dot(ns, weights[w_gate, :], 1, 1)
-        upper = dot(ns, weights[w_up, :], 1, 1)
-        ga = dot(c, weights[w_out, :], 1, 1)
-        sig = jax.nn.sigmoid(gate)
-        swish = gate * sig
-        low = (swish * upper).astype(BF)
-        gg = (ga * upper * sig * (1.0 + gate * (1.0 - sig))).astype(BF)
-        gu = (ga * swish).astype(BF)
-        pitch = act.shape[1] // 2
-        act[:, g * pitch : g * pitch + f] = low
-        grad_gu[:, g * pitch : g * pitch + f] = gg
-        grad_gu[:, (2 + g) * pitch : (2 + g) * pitch + f] = gu
-        out = dot(low, weights[w_out, :])
-        e = dot(gg, weights[w_gate, :]) + dot(gu, weights[w_up, :])
-        total = out if g == 0 else total + out
-        back = e if g == 0 else back + e
-    part[...] = total.astype(BF)
-    grad_second[...] = back.astype(BF)
+    f = act.shape[1]
+    w_gate, w_out, w_up = (slice(k * f, (k + 1) * f) for k in range(3))
+    gate = dot(ns, weights[w_gate, :], 1, 1)
+    upper = dot(ns, weights[w_up, :], 1, 1)
+    sig = jax.nn.sigmoid(gate)
+    swish = gate * sig
+    low = (swish * upper).astype(BF)
+    act[...] = low
+    ga = dot(cot[...], weights[w_out, :], 1, 1)
+    part[...] = dot(low, weights[w_out, :]).astype(BF)
+    gg = (ga * upper * sig * (1.0 + gate * (1.0 - sig))).astype(BF)
+    gu = (ga * swish).astype(BF)
+    grad_gu[:, :f] = gg
+    grad_gu[:, f:] = gu
+    grad_second[...] = (dot(gg, weights[w_gate, :]) + dot(gu, weights[w_up, :])).astype(BF)
     core = ints[4]
     for h in range(2):
         mine = pl.multiple_of((2 * h + core) * quarter, 128)
@@ -1196,7 +1310,7 @@
 
 def back_kernel(nd, spans, reach, direct, f, table, act, grad_gu, normed, cot, qkvg, log_decay, grad_mixed, packet_in,
                 factors, out_own, out_cross, ups, downs, level, level_t, *rest):
-    n_sums = 4 if direct else 3
+    n_sums = 5 if direct else 3
     (leaving, grad_qk_o, grad_v_o, grad_ld_o, gath_o, *sums), rest = rest[: 5 + n_sums], rest[5 + n_sums :]
     (grad_qk, grad_v, grad_ld, sent_packets, got_packets), rest = rest[:5], rest[5:]
     (carry_send, carry_recv, out_sems), rest = rest[:3], rest[3:]
@@ -1265,8 +1379,10 @@
             chains[1].third(kz)
             some(kz, kz + 1)()
         progress(chains[2:], nz, [some(nz, tiles)])
+        squares = sums[-1]
+        squares[...] = jnp.zeros_like(squares)
         for chain, out in zip(chains, sums):
-            chain.finish(out)
+            chain.finish(out, squares)
     else:
         undeal.exchange()
         weight_grad_into(sums[0], grad_gu.at[:, pl.ds(0, 2 * pitch)], normed, 128)
@@ -1287,8 +1403,9 @@
 
 
 def last_kernel(nd, spans, direct, table, keep, qkvg, log_decay, grad_mixed, before, leaving, grad_qk, grad_v, grad_ld,
-                grad_gate, rank, up, bias, ups, downs, weights, src, normed, grad_hidden, gain, po_in, *rest):
-    n_sums = 4 if direct else 1
+                grad_gate, rank, up, bias, ups, downs, weights, src, normed, grad_hidden, gain, po_in, gain_second, head_part, squares_in,
+                *rest):
+    n_sums = 6 if direct else 1
     (gath_o, down_sum, gain_sum, up_sum, bias_sum, *sums), rest = rest[: 5 + n_sums], rest[5 + n_sums :]
     (packet, grad_project, grad_first, grad_first_other, rank_part, rank_other), rest = rest[:6], rest[6:]
     (d_since, d_towards, ld_sum, dealt), rest = rest[:4], rest[4:]
@@ -1304,6 +1421,19 @@
     chains = []
     if direct:
         (po_acc, pi_acc), rest = rest[:2], rest[2:]
+        (small_sent, small_got, small_norms), rest = rest[:3], rest[3:]
+        small_sems, rest = rest[:6], rest[6:]
+        small = Small(nd, sums[4], small_sent, small_got, small_norms, small_sems)
+        squares = sums[5]
+        squares[...] = squares_in[...]
+        small_left = list(range(small.steps()))
+
+        def advance_small():
+            if small_left:
+                small.end(small_left.pop(0))
+                if small_left:
+                    small.begin(small_left[0])
+
         halves = ((pi_acc, 0, HEAD), (pi_acc, 1, HEAD), (po_acc, 0, DV), (po_acc, 1, DV))
         chains = [
             Collapse(
@@ -1362,9 +1492,12 @@
     lax.fori_loop(0, tiles, finish_tile, 0)
     undeal.begin()
     if direct:
+        small.fill(gain_sum, gain_second, down_sum, up_sum, bias_sum, head_part)
+        small.begin(0)
         weight_grad_into(pi_acc, grad_project, normed, 128)
         chains[0].begin()
         chains[1].begin()
+        advance_small()
         for kz in [k % nz for k in range(1, nz + 1)]:
             chains[2].third(kz)
             chains[3].third(kz)
@@ -1376,23 +1509,31 @@
         for kz in [k % nz for k in range(1, nz + 1)]:
             chains[0].second(kz)
             chains[1].second(kz)
+            advance_small()
             if arrivals:
                 arrivals.pop(0)()
+        while small_left:
+            advance_small()
+        small.begin_head()
         for kz in [k % nz for k in range(1, nz + 1)]:
             chains[0].third(kz)
             chains[1].third(kz)
             if arrivals:
                 arrivals.pop(0)()
-        chains[2].finish(sums[2])
-        chains[3].finish(sums[3])
+        chains[2].finish(sums[2], squares)
+        chains[3].finish(sums[3], squares)
+        small.end_head()
     for arrive in arrivals:
         arrive()
+    if direct:
+        chains[0].finish(sums[0], squares)
+        chains[1].finish(sums[1], squares)
+        small.begin_norm(squares[...] + small.squares())
     undeal.finish()
     out = pltpu.make_async_copy(gath, gath_o, out_sems.at[0])
     out.start()
     if direct:
-        chains[0].finish(sums[0])
-        chains[1].finish(sums[1])
+        small.end_norm(squares)
     out.wait()
 
 
@@ -1469,10 +1610,11 @@
     other_quarter = 2 * (1 - x) + core
     quarters = jnp.stack([tensor, other_quarter, 2 * x + 1 - core, 2 * (1 - x) + 1 - core])
     ints = jnp.concatenate([quarters, jnp.stack([core, z, y, x]), keep]).astype(jnp.int32)
-    ups, downs, level, level_t = level_matrices()
+    ups, downs, level, level_t = (jnp.asarray(v) for v in level_matrices())
+    ups_last, downs_last = (jnp.asarray(v[LEVELS:]) for v in level_matrices()[:2])
 
     hh, ho, hf = HEAD // 2, DV // 2, f // 2
-    pitch = up_to(f, 128)
+    pitch = f
     ffn_t = ffn_in.reshape(w, 2 * f).T
     shard_p = jnp.concatenate([decay_down.T, proj_in.reshape(w, HEAD).T, proj_out.reshape(DV, w)], axis=0)
     shard_f = jnp.concatenate([ffn_t[:f], ffn_out, ffn_t[f:]], axis=0)
@@ -1490,7 +1632,8 @@
             own, other = gathered(shard), gathered(swap(shard, "x"))
             return jnp.where(x == 0, fit([own, other]), fit([other, own]))
 
-        shard_p, shard_f = halves(shard_p), halves(shard_f)
+        shard_p = halves(shard_p)
+        shard_f = fit([halves(ffn_t[:f]), halves(ffn_out), halves(ffn_t[f:])])
 
     up_own = decay_up.reshape(16, DK)
     bias_own = decay_bias.reshape(1, DK)
@@ -1518,7 +1661,7 @@
     )
     ff = 2 * f
     hidden, normed_second, act, grad_gu, keep_out, send_out, grad_second = run(
-        functools.partial(ffn_kernel, f), (tiles,),
+        ffn_kernel, (tiles,),
         [SMEM] + [rows_spec(d)] * 4 + [whole_spec(1, d), whole_spec(3 * ff, d)],
         [rows_spec(d), rows_spec(d), rows_spec(2 * pitch), rows_spec(4 * pitch), rows_spec(2 * quarter),
          rows_spec(2 * quarter), rows_spec(d)],
@@ -1560,9 +1703,9 @@
     scratch += [pltpu.VMEM((steps - 1, 2 * DV + 16, DK), BF), pltpu.VMEM((steps, 2 * DV + 16, DK), BF)]
     scratch += [dma((steps,)), dma((steps,)), dma((4,))] + buffers[2:] + sems
     if direct:
-        sums = [sds(f, w), sds(f, w), sds(f // 2, w), sds(f // 2, w)]
+        sums = [sds(f, w), sds(f, w), sds(f // 2, w), sds(f // 2, w), sds(8, 128)]
         scratch += [pltpu.VMEM((2 * pitch, d), BF)] * 3
-        for out in sums:
+        for out in sums[:4]:
             scratch += collapse_scratch(nd, out.shape[0], w)
     else:
         sums = [sds(2 * pitch, d, dtype=BF)] * 3
@@ -1577,7 +1720,7 @@
         scratch, "back_all", 1, 110,
     )
     if direct:
-        shard_gate, shard_up, shard_fo = sums_f[0], sums_f[1], fit(sums_f[2:])
+        shard_gate, shard_up, shard_fo = sums_f[0], sums_f[1], fit(sums_f[2:4])
     else:
         shard_gate, shard_up, shard_fo = (plain_shard(v, pitch)[:f] for v in sums_f)
     block_out = home([back_out.reshape(-1, quarter)], home_slot, [jnp.int32(0)], "block_out_home")
@@ -1590,72 +1733,66 @@
         pltpu.VMEM((TILE, d), BF), dma((tiles,)), dma((tiles,)), dma((tiles,)), dma((tiles,)), dma((1,)),
     ] + buffers + sems
     if direct:
-        sums = [sds(hh, w), sds(hh, w), sds(ho, w), sds(ho, w)]
-        scratch += [pltpu.VMEM((2 * DV, d), BF), pltpu.VMEM((2 * HEAD, d), BF)]
-        for out in sums:
+        sums = [sds(hh, w), sds(hh, w), sds(ho, w), sds(ho, w), sds(SMALL, 128), sds(8, 128)]
+        scratch += [pltpu.VMEM((2 * DV, d), BF), pltpu.VMEM((2 * HEAD, d), BF)] + small_scratch(nd)
+        for out in sums[:4]:
             scratch += collapse_scratch(nd, out.shape[0], w)
     else:
         sums = [sds(2 * HEAD, d, dtype=BF)]
     back_grad, down_grad, gain_first, up_grad, bias_grad, *sums_p = remote(
         functools.partial(last_kernel, nd, spans, direct),
         (back_local, keep.astype(jnp.int32), qkvg, log_decay, grad_mixed, before, leaving, grad_qk, grad_v, grad_ld,
-         grad_gate, rank, up, bias, ups[LEVELS:], downs[LEVELS:], weights, src, normed_first, grad_hidden, gain_one,
-         acc_po),
-        [SMEM, SMEM] + [VMEM] * 19 + [ANY],
+         grad_gate, rank, up, bias, ups_last, downs_last, weights, src, normed_first, grad_hidden, gain_one,
+         acc_po, gain_second, head_part, sums_f[4] if direct else gain_second),
+        [SMEM, SMEM] + [VMEM] * 19 + [ANY] + [VMEM] * 3,
         [sds(nd * capacity, SPAN, d, dtype=BF), sds(16, d), sds(8, d), sds(16, 2 * DK), sds(8, 2 * DK)] + sums,
         [ANY] + [VMEM] * (4 + len(sums)),
         scratch, "finish_all", 2, 100,
     )
     if direct:
-        shard_pi, shard_po = fit(sums_p[:2]), fit(sums_p[2:])
+        shard_pi, shard_po = fit(sums_p[:2]), fit(sums_p[2:4])
     else:
         shard_pi, shard_po = plain_shard(sums_p[0], HEAD), plain_shard(acc_po, DV)
     token_grad = home([back_grad.reshape(-1, d)], home_slot, [jnp.int32(0)], "token_grad_home")
 
-    small = jnp.concatenate(
-        [
-            gain_first[0].reshape(-1, 128),
-            gain_second[0].reshape(-1, 128),
-            down_grad.reshape(-1, 128),
-            up_grad.reshape(-1, 128),
-            bias_grad[0].reshape(-1, 128),
-            head_part[0].reshape(-1, 128),
-        ],
-        axis=0,
-    )
-    small = all_sum(small, ("x", "dp"), (2, nd))
-    rows_d = d // 128
-    cuts = [rows_d, rows_d, 16 * rows_d, 32, 2, 2]
-    starts = [sum(cuts[:k]) for k in range(len(cuts) + 1)]
-    gain_first, gain_second, down_total, up_total, bias_total, head_total = (
-        small[starts[k] : starts[k + 1]].reshape(-1) for k in range(len(cuts))
-    )
-    head_total = head_total + swap(head_total, "core")
+    if direct:
+        small, norm_block = sums_p[4], sums_p[5]
+        gain_first, gain_second = small[0:8].reshape(d), small[8:16].reshape(d)
+        shard_down = lax.dynamic_slice_in_dim(small, 16 + 16 * dp, 16, 0).T
+        up_total = lax.dynamic_slice_in_dim(small, 144 + 16 * x, 16, 0)
+        bias_total = lax.dynamic_slice_in_dim(small, 176 + x, 1, 0)
+        head_total = small[178:180].reshape(DV)
+        norm_sq = jnp.sum(norm_block)
+    else:
+        parts = (gain_first[0], gain_second[0], down_grad, up_grad, bias_grad[0], head_part[0])
+        small = jnp.concatenate([v.reshape(-1) for v in parts]).reshape(-1, 128)
+        small = all_sum(small, ("x", "dp"), (2, nd)).reshape(-1)
+        cuts = [d, d, 16 * d, 32 * DK, 2 * DK, DV]
+        starts = [sum(cuts[:k]) for k in range(len(cuts) + 1)]
+        gain_first, gain_second, down_total, up_total, bias_total, head_total = (
+            small[starts[k] : starts[k + 1]] for k in range(len(cuts))
+        )
+        head_total = head_total + swap(head_total, "core")
+        shard_down = lax.dynamic_slice_in_dim(down_total.reshape(16, d), dp * w, w, 1).T
+        up_total = up_total.reshape(16, 2, DK)
+        up_total = jnp.where(x == 0, up_total[:, 0], up_total[:, 1])
+        bias_total = bias_total.reshape(2, DK)
+        bias_total = jnp.where(x == 0, bias_total[0:1], bias_total[1:2])
+        local_sq = (
+            square_sum(shard_pi) + square_sum(shard_po) + square_sum(shard_gate) + square_sum(shard_up)
+            + square_sum(shard_fo) + square_sum(shard_down) / 4
+            + (square_sum(up_total) + square_sum(bias_total)) / nd
+            + (square_sum(head_total) + square_sum(gain_first) + square_sum(gain_second)) / (4 * nd)
+        )
+        norm_sq = all_sum(jnp.broadcast_to(local_sq, (8, 128)), ("core", "x", "dp"), (2, 2, nd))[0, 0]
+    up_total = up_total.reshape(decay_up.shape)
+    bias_total = bias_total.reshape(decay_bias.shape)
     gains_total = jnp.stack([gain_first, gain_second])
-    down_total = down_total.reshape(16, d)
-    shard_down = lax.dynamic_slice_in_dim(down_total, dp * w, w, 1).T
-    up_total = up_total.reshape(16, 2, DK)
-    up_total = jnp.where(x == 0, up_total[:, 0:1], up_total[:, 1:2])
-    bias_total = bias_total.reshape(2, DK)
-    bias_total = jnp.where(x == 0, bias_total[0:1], bias_total[1:2])
-
     shard_in = shard_pi.T.reshape(proj_in.shape)
     shard_out = shard_po.reshape(proj_out.shape)
     shard_ffn_in = jnp.stack([shard_gate.T, shard_up.T], axis=1)
     shard_ffn_out = shard_fo
-    n_dev = 4 * nd
-    local_sq = (
-        square_sum(shard_pi)
-        + square_sum(shard_po)
-        + square_sum(shard_gate)
-        + square_sum(shard_up)
-        + square_sum(shard_fo)
-        + square_sum(shard_down) / 4
-        + (square_sum(up_total) + square_sum(bias_total)) / nd
-        + (square_sum(head_total) + square_sum(gains_total)) / n_dev
-    )
-    norm_sq = all_sum(jnp.broadcast_to(local_sq, (8, 128)), ("core", "x", "dp"), (2, 2, nd))
-    grad_norm = jnp.sqrt(norm_sq[0, 0])
+    grad_norm = jnp.sqrt(norm_sq)
     clip_norm = clip_scale * math.sqrt(PARAMS)
     factor = jnp.minimum(1.0, clip_norm / (grad_norm + 1e-06))
     update_in = adam_update(proj_in, shard_in, first_proj_in, second_proj_in, factor, weight_decay)

time: 629 us -> 580 us (0.922)
  waiting for transfers between devices: 19.8 us -> 2.81 us
  local copies, waits for them, and re-layouts: 26.9 us -> 17 us
  other arithmetic: 32.6 us -> 22.8 us
  starting transfers between devices: 10.3 us -> 3.51 us
  between operations: 9.95 us -> 3.47 us
    ppermute x9 -> x0, waiting for transfers between devices: 17.7 us -> none  [all_sum(): lax.ppermute(value, axis, [(i, i ^ bit) for i in range(size)])]
    reduce_sum x10 -> x1, other arithmetic: 7.5 us -> 0.6 us  [on_device(): norm_sq = jnp.sum(norm_block)]
    ppermute x9 -> x0, starting transfers between devices: 6.71 us -> none  [all_sum(): lax.ppermute(value, axis, [(i, i ^ bit) for i in range(size)])]
  transfers between devices with their start and end apart: 13 -> 3, of which waited for: 10 -> 2; matrix products, arithmetic and copies ran while one was open for 4% -> 3% of each run, Pallas kernels for 2% -> 0%
where the time goes in v3:
time: 580 us; the launch traced here: 572 us
  Pallas kernels  522 us (90%)
  other arithmetic  22.8 us (4%)
  local copies, waits for them, and re-layouts  17 us (3%)
    pallas_call x2, Pallas kernels, remote(): pl.pallas_call(kernel, in_specs=specs, out_specs=out_specs, out_shape=out...  266 us
    pallas_call x1, Pallas kernels, forward(): pl.pallas_call(kernel, in_specs=[SMEM, SMEM, ANY, ANY, ANY, ANY] + [VMEM]...  191 us
    pallas_call x1, Pallas kernels, on_device(): run(ffn_kernel, (tiles,), [SMEM] + [rows_spec(d)] * 4 + [whole_spec(1, d)...  34.9 us
    pallas_call x1, Pallas kernels, on_device(): run(functools.partial(out_back_kernel, tiles), (tiles,), [SMEM] + [rows_s...  18.9 us
  transfers between devices with their start and end apart: 3, of which 2 were waited for; matrix products, arithmetic and copies ran while one was open for 3% of the time, Pallas kernels for 0%

profile of v3, /device:TPU:0, one launch (start us, length us, event | category | flops | bytes accessed | tf_op | source)
XLA Modules:
  0.0 571.7 jit_solution(2750366621627696884)
XLA Ops:
  2.1 2.9 collective-permute-start
  9.7 1.1 copy.91
  10.8 1.1 fusion.24
  11.9 1.4 fusion.26
  13.3 1.6 pad_maximum_fusion.2.refs_4_
  14.9 1.8 pad_maximum_fusion.1.refs_5_
  19.0 191.5 %forward.1 = (bf16[1280,1024]{1,0:T(8,128)(2,1)}, bf16[1280,1024]{1,0:T(8,128)(2,1)}, bf16[2080,1024]{1,0:T(8,128)(2,1)}, bf16[4224,1024]{1,0:T(8,128)(2,1)}, bf...) custom-call(s32[80]{0:T(128)} %pad_add_fusion.1.refs_0_, ...), custom_call_target="tpu_custom_call" | custom-call | flops 149999992832 | bytes 150000000 | tf_op jit(solution)/shard_map/forward/pallas_call | solution.py:955
  210.6 34.9 %ffn.1 = (f32[1280,1024]{1,0:T(8,128)}, bf16[1280,1024]{1,0:T(8,128)(2,1)}, bf16[1280,1408]{1,0:T(8,128)(2,1)}, bf16[1280,2816]{1,0:T(8,128)(2,1)}, bf16[1280,51...) custom-call(s32[28]{0:T(128)} %concatenate.52.ints, ...), custom_call_target="tpu_custom_call" | custom-call | flops 33999998976 | bytes 34000000 | tf_op jit(solution)/shard_map/ffn/pallas_call | solution.py:1663
  247.0 1.1 copy.93
  248.0 1.1 copy.92
  249.9 2.7 collective-permute-done.2.recv_out
  253.6 18.9 %out_back.1 = (f32[1280,1024]{1,0:T(8,128)}, bf16[1280,512]{1,0:T(8,128)(2,1)}, bf16[1280,512]{1,0:T(8,128)(2,1)}, f32[8,1024]{1,0:T(8,128)}, f32[8,256]{1,0:T(8...) custom-call(s32[28]{0:T(128)} %concatenate.52.ints, ...), custom_call_target="tpu_custom_call" | custom-call | flops 19000000512 | bytes 19000000 | tf_op jit(solution)/shard_map/out_back/pallas_call | solution.py:1682
  272.5 144.5 %back_all.1 = (f32[528,128]{1,0:T(8,128)}, f32[1280,512]{1,0:T(8,128)}, bf16[1280,512]{1,0:T(8,128)(2,1)}, f32[1280,256]{1,0:T(8,128)}, bf16[40,64,256]{2,1,0:T(...) custom-call(s32[40]{0:T(128)} %reshape.339.table, ...), custom_call_target="tpu_custom_call" | custom-call | flops 109999996928 | bytes 110000000 | tf_op jit(solution)/shard_map/back_all/pallas_call | solution.py:1541
  417.0 3.3 block_out_home.1
  420.3 121.5 %finish_all.1 = (bf16[40,64,1024]{2,1,0:T(8,128)(2,1)}, f32[16,1024]{1,0:T(8,128)}, f32[8,1024]{1,0:T(8,128)}, f32[16,256]{1,0:T(8,128)}, f32[8,256]{1,0:T(8,128...) custom-call(s32[40]{0:T(128)} %reshape.339.table, ...), custom_call_target="tpu_custom_call" | custom-call | flops 99999997952 | bytes 100000000 | tf_op jit(solution)/shard_map/finish_all/pallas_call | solution.py:1541
  541.8 7.7 %token_grad_home.1 = f32[2560,1024]{1,0:T(8,128)} custom-call(s32[41]{0:T(128)} %pad_add_fusion.table, bf16[2560,1024]{1,0:T(8,128)(2,1)} %bitcast.79), custom_call_target="tpu_custom_call" | custom-call | flops 4000000000 | bytes 4000000 | tf_op jit(solution)/shard_map/token_grad_home/pallas_call | solution.py:160
  557.0 1.3 add_multiply_fusion.6
  558.4 1.5 maximum_bitcast_fusion
  560.9 1.5 add_multiply_fusion.5
  562.3 1.4 fusion.7
  563.7 1.3 add_multiply_fusion.7
  565.0 1.2 add_multiply_fusion.2
  567.0 1.4 add_multiply_fusion.4
  568.4 1.8 add_multiply_fusion
  (129 shorter events, 20.2 us)
Async XLA Ops:
  0.7 17.2 %copy-start.30 = (f32[1,128]{1,0:T(1,128)S(1)}, f32[1,128]{1,0:T(1,128)}, u32[]{:S(2)}) copy-start(f32[1,128]{1,0:T(1,128)} %param.44) | copy-start | bytes 1540
  2.1 15.8 %collective-permute-start = (f32[24,128]{1,0:T(8,128)S(1)}, f32[24,128]{1,0:T(8,128)S(1)}, u32[]{:S(2)}, u32[]{:S(2)}) collective-permute-start(f32[24,128]{1,0:T(8,128)S(1)} %pad_maximum_fusion.3), channel_id=1, source_target_pairs={{0,2},{2,0},{1,3},{3,1},{4,6},{6,4},{5,7},{7,5},{8,10},{10,8},{9,1... | collective-permute-start | bytes 36872 | tf_op jit(solution)/shard_map/ppermute | solution.py:1580
  7.6 11.5 %copy-start.36 = (s32[20]{0:T(128)}, s32[20]{0:T(128)S(1)}, u32[]{:S(2)}) copy-start(s32[20]{0:T(128)S(1)} %convert_subtract_fusion.refs_1_.keep) | copy-start | bytes 244
  210.5 35.5 %copy-start.35 = (s32[40]{0:T(128)S(1)}, s32[40]{0:T(128)}, u32[]{:S(2)}) copy-start(s32[40]{0:T(128)} %copy-done.34) | copy-start | bytes 484
  210.6 35.5 %copy-start.33 = (s32[40]{0:T(128)S(1)}, s32[40]{0:T(128)}, u32[]{:S(2)}) copy-start(s32[40]{0:T(128)} %copy-done.32) | copy-start | bytes 484
  210.6 36.4 %copy-start.9 = (f32[128,1,768]{2,1,0:T(1,128)S(1)}, f32[128,1,768]{2,1,0:T(1,128)}, u32[]{:S(2)}) copy-start(f32[128,1,768]{2,1,0:T(1,128)} %param.51) | copy-start | bytes 1179652
  210.6 37.4 %copy-start.10 = (f32[128,1,768]{2,1,0:T(1,128)S(1)}, f32[128,1,768]{2,1,0:T(1,128)}, u32[]{:S(2)}) copy-start(f32[128,1,768]{2,1,0:T(1,128)} %param.50) | copy-start | bytes 1179652
  210.6 38.5 %copy-start.23 = (s32[8,40]{1,0:T(8,128)S(1)}, s32[8,40]{1,0:T(8,128)}, u32[]{:S(2)}) copy-start(s32[8,40]{1,0:T(8,128)} %copy-done.22) | copy-start | bytes 3844
  210.6 38.5 %copy-start.25 = (s32[8,40]{1,0:T(8,128)S(1)}, s32[8,40]{1,0:T(8,128)}, u32[]{:S(2)}) copy-start(s32[8,40]{1,0:T(8,128)} %copy-done.24) | copy-start | bytes 3844
  210.6 38.5 %copy-start.28 = (s32[8,40]{1,0:T(8,128)S(1)}, s32[8,40]{1,0:T(8,128)}, u32[]{:S(2)}) copy-start(s32[8,40]{1,0:T(8,128)} %get-tuple-element.261) | copy-start | bytes 3844
  245.5 7.2 %collective-permute-start.1 = (bf16[1280,1024]{1,0:T(8,128)(2,1)}, bf16[1280,1024]{1,0:T(8,128)(2,1)}, u32[]{:S(2)}, u32[]{:S(2)}) collective-permute-start(bf16[1280,1024]{1,0:T(8,128)(2,1)} %get-tuple-element.97.gs_a), channel_id=1, source_target_pairs={{0,1},{1,0},{2,3},{3,2},{4,5},{5,4},{6,7},{7,6},{8,9},{9,8},{10,11... | collective-permute-start | bytes 7864328 | tf_op jit(solution)/shard_map/ppermute | solution.py:1580
  245.9 6.6 %collective-permute-start.2 = (bf16[1280,512]{1,0:T(8,128)(2,1)}, bf16[1280,512]{1,0:T(8,128)(2,1)S(1)}, u32[]{:S(2)}, u32[]{:S(2)}) collective-permute-start(bf16[1280,512]{1,0:T(8,128)(2,1)} %get-tuple-element.102), channel_id=1, source_target_pairs={{0,1},{1,0},{2,3},{3,2},{4,5},{5,4},{6,7},{7,6},{8,9},{9,8},{10,11... | collective-permute-start | bytes 3932168 | tf_op jit(solution)/shard_map/ppermute | solution.py:1580
  552.0 13.0 %copy-start.8 = (bf16[704,128]{1,0:T(8,128)(2,1)S(1)}, bf16[704,128]{1,0:T(8,128)(2,1)}, u32[]{:S(2)}) copy-start(bf16[704,128]{1,0:T(8,128)(2,1)} %param.49) | copy-start | bytes 540676
  552.0 13.0 %copy-start.11 = (f32[704,128]{1,0:T(8,128)S(1)}, f32[704,128]{1,0:T(8,128)}, u32[]{:S(2)}) copy-start(f32[704,128]{1,0:T(8,128)} %param.67) | copy-start | bytes 1081348
  552.0 13.0 %copy-start.12 = (f32[704,128]{1,0:T(8,128)S(1)}, f32[704,128]{1,0:T(8,128)}, u32[]{:S(2)}) copy-start(f32[704,128]{1,0:T(8,128)} %param.66) | copy-start | bytes 1081348
  553.3 12.8 %copy-start.15 = (f32[128,128]{1,0:T(8,128)S(1)}, f32[128,128]{1,0:T(8,128)}, u32[]{:S(2)}) copy-start(f32[128,128]{1,0:T(8,128)} %get-tuple-element.127) | copy-start | bytes 196612
  554.3 12.7 %copy-start.26 = (f32[2,1024]{1,0:T(2,128)S(1)}, f32[2,1024]{1,0:T(2,128)}, u32[]{:S(2)}) copy-start(f32[2,1024]{1,0:T(2,128)} %param.47) | copy-start | bytes 24580
  554.3 14.0 %copy-start.4 = (bf16[128,2,704]{0,2,1:T(8,128)(2,1)S(1)}, bf16[128,2,704]{0,2,1:T(8,128)(2,1)}, u32[]{:S(2)}) copy-start(bf16[128,2,704]{0,2,1:T(8,128)(2,1)} %param.48) | copy-start | bytes 1081348
  554.3 14.0 %copy-start.6 = (f32[128,2,704]{0,2,1:T(8,128)S(1)}, f32[128,2,704]{0,2,1:T(8,128)}, u32[]{:S(2)}) copy-start(f32[128,2,704]{0,2,1:T(8,128)} %param.65) | copy-start | bytes 2162692
  554.3 14.0 %copy-start.7 = (f32[128,2,704]{0,2,1:T(8,128)S(1)}, f32[128,2,704]{0,2,1:T(8,128)}, u32[]{:S(2)}) copy-start(f32[128,2,704]{0,2,1:T(8,128)} %param.64) | copy-start | bytes 2162692
  554.3 14.0 %copy-start.13 = (f32[704,128]{1,0:T(8,128)S(1)}, f32[704,128]{1,0:T(8,128)}, u32[]{:S(2)}) copy-start(f32[704,128]{1,0:T(8,128)} %get-tuple-element.129) | copy-start | bytes 1081348
  555.3 10.8 %copy-start.20 = (f32[1,256,128]{2,1,0:T(8,128)S(1)}, f32[1,256,128]{2,1,0:T(8,128)}, u32[]{:S(2)}) copy-start(f32[1,256,128]{2,1,0:T(8,128)} %param.61) | copy-start | bytes 393220
  555.3 10.8 %copy-start.21 = (f32[1,256,128]{2,1,0:T(8,128)S(1)}, f32[1,256,128]{2,1,0:T(8,128)}, u32[]{:S(2)}) copy-start(f32[1,256,128]{2,1,0:T(8,128)} %param.60) | copy-start | bytes 393220
  555.3 13.0 %copy-start.14 = (f32[704,128]{1,0:T(8,128)S(1)}, f32[704,128]{1,0:T(8,128)}, u32[]{:S(2)}) copy-start(f32[704,128]{1,0:T(8,128)} %get-tuple-element.130) | copy-start | bytes 1081348
  (17 other events, 114.5 us)

commit v4 on v3

--- a/solution.py
+++ b/solution.py
@@ -138,34 +138,26 @@
     return ups, np.ascontiguousarray(np.swapaxes(ups, 1, 2)), level, np.ascontiguousarray(level.T)
 
 
-def home_kernel(count, table, *refs):
-    srcs, out = refs[:-1], refs[-1]
-    width = srcs[0].shape[1]
-
-    def body(i, _):
-        row = pl.multiple_of(table[i] * SPAN, SPAN)
-        to = pl.multiple_of(i * SPAN, SPAN)
-        for k, src in enumerate(srcs):
-            col = pl.multiple_of(table[count + k], 128)
-            out[pl.ds(to, SPAN), pl.ds(col, width)] = src[pl.ds(row, SPAN), :].astype(F32)
-        return 0
-
-    lax.fori_loop(0, count, body, 0)
-
-
-def home(pieces, table, cols, name):
-    count = table.shape[0]
-    width = pieces[0].shape[1]
-    total = width * len(pieces)
+def home_kernel(count, table, src, out):
+    step = pl.program_id(0)
+    for i in range(count):
+        out[i * SPAN : (i + 1) * SPAN, :] = src[table[step * count + i]].astype(F32)
+
+
+def home(spans, table, name):
+    total = table.shape[0]
+    count = 5
+    d = spans.shape[2]
     return pl.pallas_call(
         functools.partial(home_kernel, count),
-        in_specs=[SMEM] + [VMEM] * len(pieces),
-        out_specs=VMEM,
-        out_shape=sds(count * SPAN, total),
+        grid=(total // count,),
+        in_specs=[SMEM, whole_spec(*spans.shape)],
+        out_specs=pl.BlockSpec((count * SPAN, d), lambda i: (i, 0)),
+        out_shape=sds(total * SPAN, d),
         name=name,
         compiler_params=pltpu.CompilerParams(vmem_limit_bytes=VMEM_LIMIT),
-        cost_estimate=cost(4),
-    )(jnp.concatenate([table, jnp.stack(cols)]), *pieces)
+        cost_estimate=cost(5),
+    )(table, spans)
 
 
 def copy_to(src, dst, send_sem, recv_sem, target):
@@ -541,6 +533,16 @@
     ]
 
 
+PIECES = 5
+
+
+def fetch(pairs, sems):
+    copies = [pltpu.make_async_copy(src, dst, sems.at[k]) for k, (src, dst) in enumerate(pairs)]
+    for copy in copies:
+        copy.start()
+    return copies
+
+
 class Undeal:
     def __init__(self, nd, spans, table, own, cross, joined, sent, gath, sems):
         self.nd, self.spans, self.table, self.own, self.cross = nd, spans, table, own, cross
@@ -555,17 +557,17 @@
             self.mine = pl.multiple_of((2 * self.x + self.core) * self.quarter, 128)
             self.theirs = pl.multiple_of((2 * (1 - self.x) + self.core) * self.quarter, 128)
 
-    def swap(self):
+    def swap(self, i):
+        count = self.spans // PIECES
         return copy_to(
-            self.cross,
-            self.joined.at[pl.ds(self.x * self.spans, self.spans)],
-            self.x_send.at[0],
-            self.x_recv.at[0],
+            self.cross.at[pl.ds(i * count, count)],
+            self.joined.at[pl.ds(self.x * self.spans + i * count, count)],
+            self.x_send.at[i],
+            self.x_recv.at[i],
             {"x": 1 - self.x},
         )
 
     def begin(self):
-        self.swap().start()
 
         def body(i, _):
             self.joined[self.x * self.spans + i] = self.own[i]
@@ -586,7 +588,8 @@
         )
 
     def exchange(self):
-        self.swap().wait_recv()
+        for i in range(PIECES):
+            self.swap(i).wait_recv()
         cap = self.cap
         for k in range(1, self.nd):
             d = lax.rem(self.dp + k, self.nd)
@@ -626,7 +629,8 @@
                     self.widen(k, step).wait_send()
         for k in range(1, self.nd):
             self.a2a(k).wait_send()
-        self.swap().wait_send()
+        for i in range(PIECES):
+            self.swap(i).wait_send()
 
 
 def undeal_scratch(nd, per_dev, spans, quarter, cap, wide):
@@ -638,7 +642,7 @@
         pltpu.VMEM((nd, cap, SPAN, quarter), BF),
         pltpu.VMEM((nd * cap, SPAN, quarter * (4 if wide else 1)), BF),
     ]
-    sems = [dma((1,)), dma((1,)), dma((nd,)), dma((nd,))]
+    sems = [dma((PIECES,)), dma((PIECES,)), dma((nd,)), dma((nd,))]
     return buffers, sems + ([dma((3 * nd,)), dma((3 * nd,))] if wide else [])
 
 
@@ -1114,13 +1118,14 @@
         send_out[:, h * quarter : (h + 1) * quarter] = part[:, pl.ds(theirs, quarter)]
 
 
-def weight_grad_into(acc, lhs, rhs, chunk):
+def weight_grad_into(acc, lhs, rhs, first=0, count=None):
     def body(i, _):
-        at = pl.multiple_of(i * chunk, chunk)
-        acc[pl.ds(at, chunk), :] = dot(lhs[:, pl.ds(at, chunk)], rhs[...], 0, 0).astype(BF)
+        at = pl.multiple_of(i * 128, 128)
+        acc[pl.ds(at, 128), :] = dot(lhs[:, pl.ds(at, 128)], rhs[...], 0, 0).astype(BF)
         return 0
 
-    lax.fori_loop(0, acc.shape[0] // chunk, body, 0)
+    last = acc.shape[0] // 128 if count is None else first + count
+    lax.fori_loop(first, last, body, 0)
 
 
 def out_back_kernel(
@@ -1308,7 +1313,7 @@
             out[j] = dealt[j * SPAN : (j + 1) * SPAN, pl.ds(col, quarter)]
 
 
-def back_kernel(nd, spans, reach, direct, f, table, act, grad_gu, normed, cot, qkvg, log_decay, grad_mixed, packet_in,
+def back_kernel(nd, spans, reach, direct, f, table, act_in, grad_gu, normed, cot_in, qkvg_in, log_decay_in, mixed_in, packet_in,
                 factors, out_own, out_cross, ups, downs, level, level_t, *rest):
     n_sums = 5 if direct else 3
     (leaving, grad_qk_o, grad_v_o, grad_ld_o, gath_o, *sums), rest = rest[: 5 + n_sums], rest[5 + n_sums :]
@@ -1316,12 +1321,18 @@
     (carry_send, carry_recv, out_sems), rest = rest[:3], rest[3:]
     (joined, sent, gath), rest = rest[:3], rest[3:]
     undeal_sems, rest = rest[:4], rest[4:]
+    (act, cot, qkvg, log_decay, grad_mixed, late_sems), rest = rest[:6], rest[6:]
+    late = fetch(
+        ((act_in, act), (cot_in, cot), (qkvg_in, qkvg), (log_decay_in, log_decay), (mixed_in, grad_mixed)), late_sems
+    )
     pitch = act.shape[1] // 2
     tiles = spans * SPAN // TILE
     nz = nd // 2
     carry = Carry(nd, reach, -1, leaving, sent_packets, got_packets, carry_send, carry_recv)
     enter(nd, carry.shifts())
     undeal = Undeal(nd, spans, table, out_own, out_cross, joined, sent, gath, undeal_sems)
+    for i in range(PIECES):
+        undeal.swap(i).start()
     undeal.begin()
     leaving[: 2 * DV] = packet_in[...]
     leaving[2 * DV :] = factors[...]
@@ -1359,20 +1370,28 @@
                 ((accs[0], 0, 0, f), (accs[1], 1, 0, f), (accs[2], 0, 0, f // 2), (accs[2], 1, f // 2, f // 2))
             )
         ]
-        weight_grad_into(accs[0], grad_gu.at[:, pl.ds(0, 2 * pitch)], normed, 128)
+        at_x = lax.axis_index("x")
+        chunks = 2 * pitch // 128
+        part = -(-pitch // 128)
+        gate = grad_gu.at[:, pl.ds(0, 2 * pitch)]
+        weight_grad_into(accs[0], gate, normed, (chunks - part) * (1 - at_x), part)
         chains[0].begin()
+        weight_grad_into(accs[0], gate, normed, part * at_x, chunks - part)
         advance()
-        weight_grad_into(accs[1], grad_gu.at[:, pl.ds(2 * pitch, 2 * pitch)], normed, 128)
+        weight_grad_into(accs[1], grad_gu.at[:, pl.ds(2 * pitch, 2 * pitch)], normed)
         chains[1].begin()
         advance()
-        undeal.exchange()
-        for kz in [k % nz for k in range(1, nz + 1)]:
-            chains[0].second(kz)
-        weight_grad_into(accs[2], act, cot, 128)
-        for kz in [k % nz for k in range(1, nz + 1)]:
-            chains[1].second(kz)
+        for copy in late:
+            copy.wait()
+        third = -(-chunks // nz)
+        for i in range(nz):
+            chains[0].second((i + 1) % nz)
+            weight_grad_into(accs[2], act, cot, third * i, max(0, min(third, chunks - third * i)))
+        for i in range(nz):
+            chains[1].second((i + 1) % nz)
         chains[2].begin()
         chains[3].begin()
+        undeal.exchange()
         advance()
         for kz in [k % nz for k in range(1, nz + 1)]:
             chains[0].third(kz)
@@ -1385,9 +1404,11 @@
             chain.finish(out, squares)
     else:
         undeal.exchange()
-        weight_grad_into(sums[0], grad_gu.at[:, pl.ds(0, 2 * pitch)], normed, 128)
-        weight_grad_into(sums[1], grad_gu.at[:, pl.ds(2 * pitch, 2 * pitch)], normed, 128)
-        weight_grad_into(sums[2], act, cot, 128)
+        weight_grad_into(sums[0], grad_gu.at[:, pl.ds(0, 2 * pitch)], normed)
+        weight_grad_into(sums[1], grad_gu.at[:, pl.ds(2 * pitch, 2 * pitch)], normed)
+        for copy in late:
+            copy.wait()
+        weight_grad_into(sums[2], act, cot)
         some(0, tiles)()
         while stages:
             advance()
@@ -1403,7 +1424,7 @@
 
 
 def last_kernel(nd, spans, direct, table, keep, qkvg, log_decay, grad_mixed, before, leaving, grad_qk, grad_v, grad_ld,
-                grad_gate, rank, up, bias, ups, downs, weights, src, normed, grad_hidden, gain, po_in, gain_second, head_part, squares_in,
+                grad_gate, rank, up, bias, ups, downs, weights, src_in, normed_in, hidden_in, gain, po_in, gain_second, head_part, squares_in,
                 *rest):
     n_sums = 6 if direct else 1
     (gath_o, down_sum, gain_sum, up_sum, bias_sum, *sums), rest = rest[: 5 + n_sums], rest[5 + n_sums :]
@@ -1412,6 +1433,8 @@
     (gf_send, gf_recv, rk_send, rk_recv, out_sems), rest = rest[:5], rest[5:]
     (own, cross, joined, sent, gath), rest = rest[:5], rest[5:]
     undeal_sems, rest = rest[:6], rest[6:]
+    (src, normed, grad_hidden, late_sems), rest = rest[:4], rest[4:]
+    late = fetch(((src_in, src), (normed_in, normed), (hidden_in, grad_hidden)), late_sems)
     tiles = spans * SPAN // TILE
     per_tile = TILE // SPAN
     nz = nd // 2
@@ -1487,22 +1510,30 @@
             own.at[pl.ds(i * per_tile, per_tile)], cross.at[pl.ds(i * per_tile, per_tile)],
             dealt, down_sum, gain_sum,
         )
+        undeal.swap(i).start()
         return 0
 
+    for copy in late:
+        copy.wait()
     lax.fori_loop(0, tiles, finish_tile, 0)
     undeal.begin()
     if direct:
         small.fill(gain_sum, gain_second, down_sum, up_sum, bias_sum, head_part)
         small.begin(0)
-        weight_grad_into(pi_acc, grad_project, normed, 128)
+        at_x = lax.axis_index("x")
+        part = HEAD // 256
+        weight_grad_into(pi_acc, grad_project, normed, 2 * part * (1 - at_x), part)
         chains[0].begin()
+        weight_grad_into(pi_acc, grad_project, normed, part, part)
+        weight_grad_into(pi_acc, grad_project, normed, 3 * part, part)
         chains[1].begin()
+        weight_grad_into(pi_acc, grad_project, normed, 2 * part * at_x, part)
         advance_small()
         for kz in [k % nz for k in range(1, nz + 1)]:
             chains[2].third(kz)
             chains[3].third(kz)
     else:
-        weight_grad_into(sums[0], grad_project, normed, 128)
+        weight_grad_into(sums[0], grad_project, normed)
     undeal.exchange()
     arrivals = [functools.partial(undeal.arrive, k) for k in range(1, nd)]
     if direct:
@@ -1702,6 +1733,7 @@
     scratch = [pltpu.VMEM(shape_qk, F32), pltpu.VMEM(shape_v, BF), pltpu.VMEM(shape_ld, F32)]
     scratch += [pltpu.VMEM((steps - 1, 2 * DV + 16, DK), BF), pltpu.VMEM((steps, 2 * DV + 16, DK), BF)]
     scratch += [dma((steps,)), dma((steps,)), dma((4,))] + buffers[2:] + sems
+    scratch += [pltpu.VMEM(v.shape, v.dtype) for v in (act, cot, qkvg, log_decay, grad_mixed)] + [dma((5,))]
     if direct:
         sums = [sds(f, w), sds(f, w), sds(f // 2, w), sds(f // 2, w), sds(8, 128)]
         scratch += [pltpu.VMEM((2 * pitch, d), BF)] * 3
@@ -1713,7 +1745,7 @@
         functools.partial(back_kernel, nd, spans, reach, direct, f),
         (back_local, act, grad_gu, normed_second, cot, qkvg, log_decay, grad_mixed, packet_back, factors,
          out_own.reshape(spans, SPAN, quarter), out_cross.reshape(spans, SPAN, quarter), ups, downs, level, level_t),
-        [SMEM] + [VMEM] * 15,
+        [SMEM, ANY, VMEM, VMEM, ANY, ANY, ANY, ANY] + [VMEM] * 8,
         [sds(2 * DV + 16, DK), sds(*shape_qk), sds(*shape_v, dtype=BF), sds(*shape_ld),
          sds(nd * capacity, SPAN, quarter, dtype=BF)] + sums,
         [VMEM] + [ANY] * 4 + [VMEM] * len(sums),
@@ -1723,7 +1755,7 @@
         shard_gate, shard_up, shard_fo = sums_f[0], sums_f[1], fit(sums_f[2:4])
     else:
         shard_gate, shard_up, shard_fo = (plain_shard(v, pitch)[:f] for v in sums_f)
-    block_out = home([back_out.reshape(-1, quarter)], home_slot, [jnp.int32(0)], "block_out_home")
+    block_out = home(back_out, home_slot, "block_out_home")
 
     buffers, sems = undeal_scratch(nd, per_dev, spans, quarter, capacity, True)
     scratch = [
@@ -1732,6 +1764,7 @@
         pltpu.VMEM((TILE, 2 * DK), BF), pltpu.VMEM((TILE, 2 * DK), BF), pltpu.VMEM((TILE, 2 * DK), F32),
         pltpu.VMEM((TILE, d), BF), dma((tiles,)), dma((tiles,)), dma((tiles,)), dma((tiles,)), dma((1,)),
     ] + buffers + sems
+    scratch += [pltpu.VMEM(v.shape, v.dtype) for v in (src, normed_first, grad_hidden)] + [dma((3,))]
     if direct:
         sums = [sds(hh, w), sds(hh, w), sds(ho, w), sds(ho, w), sds(SMALL, 128), sds(8, 128)]
         scratch += [pltpu.VMEM((2 * DV, d), BF), pltpu.VMEM((2 * HEAD, d), BF)] + small_scratch(nd)
@@ -1744,7 +1777,7 @@
         (back_local, keep.astype(jnp.int32), qkvg, log_decay, grad_mixed, before, leaving, grad_qk, grad_v, grad_ld,
          grad_gate, rank, up, bias, ups_last, downs_last, weights, src, normed_first, grad_hidden, gain_one,
          acc_po, gain_second, head_part, sums_f[4] if direct else gain_second),
-        [SMEM, SMEM] + [VMEM] * 19 + [ANY] + [VMEM] * 3,
+        [SMEM, SMEM] + [VMEM] * 15 + [ANY] * 3 + [VMEM, ANY] + [VMEM] * 3,
         [sds(nd * capacity, SPAN, d, dtype=BF), sds(16, d), sds(8, d), sds(16, 2 * DK), sds(8, 2 * DK)] + sums,
         [ANY] + [VMEM] * (4 + len(sums)),
         scratch, "finish_all", 2, 100,
@@ -1753,7 +1786,7 @@
         shard_pi, shard_po = fit(sums_p[:2]), fit(sums_p[2:4])
     else:
         shard_pi, shard_po = plain_shard(sums_p[0], HEAD), plain_shard(acc_po, DV)
-    token_grad = home([back_grad.reshape(-1, d)], home_slot, [jnp.int32(0)], "token_grad_home")
+    token_grad = home(back_grad, home_slot, "token_grad_home")
 
     if direct:
         small, norm_block = sums_p[4], sums_p[5]

time: 580 us -> 573 us (0.988)
  Pallas kernels: 522 us -> 515 us
    pallas_call x2, Pallas kernels: 266 us -> 258 us  [remote(): pl.pallas_call(kernel, in_specs=specs, out_specs=out_specs, out_shape=out...]
where the time goes in v4:
time: 573 us; the launch traced here: 565 us
  Pallas kernels  515 us (90%)
  other arithmetic  22.7 us (4%)
  local copies, waits for them, and re-layouts  17 us (3%)
    pallas_call x2, Pallas kernels, remote(): pl.pallas_call(kernel, in_specs=specs, out_specs=out_specs, out_shape=out...  258 us
    pallas_call x1, Pallas kernels, forward(): pl.pallas_call(kernel, in_specs=[SMEM, SMEM, ANY, ANY, ANY, ANY] + [VMEM]...  191 us
    pallas_call x1, Pallas kernels, on_device(): run(ffn_kernel, (tiles,), [SMEM] + [rows_spec(d)] * 4 + [whole_spec(1, d)...  34.9 us
    pallas_call x1, Pallas kernels, on_device(): run(functools.partial(out_back_kernel, tiles), (tiles,), [SMEM] + [rows_s...  18.9 us
    pallas_call x2, Pallas kernels, home(): pl.pallas_call(functools.partial(home_kernel, count), grid=(total // coun...  12.2 us
  transfers between devices with their start and end apart: 3, of which 2 were waited for; matrix products, arithmetic and copies ran while one was open for 3% of the time, Pallas kernels for 0%

profile of v4, /device:TPU:0, one launch (start us, length us, event | category | flops | bytes accessed | tf_op | source)
XLA Modules:
  0.0 565.0 jit_solution(15168004874815698420)
XLA Ops:
  2.1 2.9 collective-permute-start
  9.7 1.1 copy.91
  10.8 1.1 fusion.24
  11.9 1.4 fusion.26
  13.3 1.6 pad_maximum_fusion.2.refs_4_
  14.9 1.8 pad_maximum_fusion.1.refs_5_
  19.0 191.5 %forward.1 = (bf16[1280,1024]{1,0:T(8,128)(2,1)}, bf16[1280,1024]{1,0:T(8,128)(2,1)}, bf16[2080,1024]{1,0:T(8,128)(2,1)}, bf16[4224,1024]{1,0:T(8,128)(2,1)}, bf...) custom-call(s32[80]{0:T(128)} %pad_add_fusion.refs_0_, ...), custom_call_target="tpu_custom_call" | custom-call | flops 149999992832 | bytes 150000000 | tf_op jit(solution)/shard_map/forward/pallas_call | solution.py:959
  210.6 34.9 %ffn.1 = (f32[1280,1024]{1,0:T(8,128)}, bf16[1280,1024]{1,0:T(8,128)(2,1)}, bf16[1280,1408]{1,0:T(8,128)(2,1)}, bf16[1280,2816]{1,0:T(8,128)(2,1)}, bf16[1280,51...) custom-call(s32[28]{0:T(128)} %concatenate.47.ints, ...), custom_call_target="tpu_custom_call" | custom-call | flops 33999998976 | bytes 34000000 | tf_op jit(solution)/shard_map/ffn/pallas_call | solution.py:1694
  247.0 1.1 copy.93
  248.0 1.1 copy.92
  249.8 2.7 collective-permute-done.2.recv_out
  253.6 18.9 %out_back.1 = (f32[1280,1024]{1,0:T(8,128)}, bf16[1280,512]{1,0:T(8,128)(2,1)}, bf16[1280,512]{1,0:T(8,128)(2,1)}, f32[8,1024]{1,0:T(8,128)}, f32[8,256]{1,0:T(8...) custom-call(s32[28]{0:T(128)} %concatenate.47.ints, ...), custom_call_target="tpu_custom_call" | custom-call | flops 19000000512 | bytes 19000000 | tf_op jit(solution)/shard_map/out_back/pallas_call | solution.py:1713
  272.5 139.1 %back_all.1 = (f32[528,128]{1,0:T(8,128)}, f32[1280,512]{1,0:T(8,128)}, bf16[1280,512]{1,0:T(8,128)(2,1)}, f32[1280,256]{1,0:T(8,128)}, bf16[40,64,256]{2,1,0:T(...) custom-call(s32[40]{0:T(128)} %reshape.333.table, ...), custom_call_target="tpu_custom_call" | custom-call | flops 109999996928 | bytes 110000000 | tf_op jit(solution)/shard_map/back_all/pallas_call | solution.py:1572
  411.6 4.5 block_out_home.1
  416.1 118.9 %finish_all.1 = (bf16[40,64,1024]{2,1,0:T(8,128)(2,1)}, f32[16,1024]{1,0:T(8,128)}, f32[8,1024]{1,0:T(8,128)}, f32[16,256]{1,0:T(8,128)}, f32[8,256]{1,0:T(8,128...) custom-call(s32[40]{0:T(128)} %reshape.333.table, ...), custom_call_target="tpu_custom_call" | custom-call | flops 99999997952 | bytes 100000000 | tf_op jit(solution)/shard_map/finish_all/pallas_call | solution.py:1572
  535.1 7.7 %token_grad_home.1 = f32[2560,1024]{1,0:T(8,128)} custom-call(s32[40]{0:T(128)} %multiply_reduce_fusion.table, bf16[40,64,1024]{2,1,0:T(8,128)(2,1)} %get-tuple-element.122.src), custom_call_target="tpu_custom_call" | custom-call | flops 5000000000 | bytes 5000000 | tf_op jit(solution)/shard_map/token_grad_home/pallas_call | solution.py:151
  550.4 1.3 add_multiply_fusion.6
  551.7 1.5 maximum_bitcast_fusion
  554.2 1.5 add_multiply_fusion.5
  555.7 1.4 fusion.7
  557.0 1.3 add_multiply_fusion.7
  558.3 1.2 add_multiply_fusion.2
  560.3 1.4 add_multiply_fusion.4
  561.7 1.8 add_multiply_fusion
  (128 shorter events, 20.2 us)
Async XLA Ops:
  0.7 17.2 %copy-start.30 = (f32[1,128]{1,0:T(1,128)S(1)}, f32[1,128]{1,0:T(1,128)}, u32[]{:S(2)}) copy-start(f32[1,128]{1,0:T(1,128)} %param.44) | copy-start | bytes 1540
  2.1 15.8 %collective-permute-start = (f32[24,128]{1,0:T(8,128)S(1)}, f32[24,128]{1,0:T(8,128)S(1)}, u32[]{:S(2)}, u32[]{:S(2)}) collective-permute-start(f32[24,128]{1,0:T(8,128)S(1)} %pad_maximum_fusion.3), channel_id=1, source_target_pairs={{0,2},{2,0},{1,3},{3,1},{4,6},{6,4},{5,7},{7,5},{8,10},{10,8},{9,1... | collective-permute-start | bytes 36872 | tf_op jit(solution)/shard_map/ppermute | solution.py:1611
  7.6 11.5 %copy-start.36 = (s32[20]{0:T(128)}, s32[20]{0:T(128)S(1)}, u32[]{:S(2)}) copy-start(s32[20]{0:T(128)S(1)} %convert_subtract_fusion.refs_1_.keep) | copy-start | bytes 244
  210.5 35.5 %copy-start.35 = (s32[40]{0:T(128)S(1)}, s32[40]{0:T(128)}, u32[]{:S(2)}) copy-start(s32[40]{0:T(128)} %copy-done.34) | copy-start | bytes 484
  210.6 35.5 %copy-start.33 = (s32[40]{0:T(128)S(1)}, s32[40]{0:T(128)}, u32[]{:S(2)}) copy-start(s32[40]{0:T(128)} %copy-done.32) | copy-start | bytes 484
  210.6 36.4 %copy-start.9 = (f32[128,1,768]{2,1,0:T(1,128)S(1)}, f32[128,1,768]{2,1,0:T(1,128)}, u32[]{:S(2)}) copy-start(f32[128,1,768]{2,1,0:T(1,128)} %param.51) | copy-start | bytes 1179652
  210.6 37.4 %copy-start.10 = (f32[128,1,768]{2,1,0:T(1,128)S(1)}, f32[128,1,768]{2,1,0:T(1,128)}, u32[]{:S(2)}) copy-start(f32[128,1,768]{2,1,0:T(1,128)} %param.50) | copy-start | bytes 1179652
  210.6 38.5 %copy-start.23 = (s32[8,40]{1,0:T(8,128)S(1)}, s32[8,40]{1,0:T(8,128)}, u32[]{:S(2)}) copy-start(s32[8,40]{1,0:T(8,128)} %copy-done.22) | copy-start | bytes 3844
  210.6 38.5 %copy-start.25 = (s32[8,40]{1,0:T(8,128)S(1)}, s32[8,40]{1,0:T(8,128)}, u32[]{:S(2)}) copy-start(s32[8,40]{1,0:T(8,128)} %copy-done.24) | copy-start | bytes 3844
  210.6 38.5 %copy-start.28 = (s32[8,40]{1,0:T(8,128)S(1)}, s32[8,40]{1,0:T(8,128)}, u32[]{:S(2)}) copy-start(s32[8,40]{1,0:T(8,128)} %get-tuple-element.261) | copy-start | bytes 3844
  245.5 7.2 %collective-permute-start.1 = (bf16[1280,1024]{1,0:T(8,128)(2,1)}, bf16[1280,1024]{1,0:T(8,128)(2,1)}, u32[]{:S(2)}, u32[]{:S(2)}) collective-permute-start(bf16[1280,1024]{1,0:T(8,128)(2,1)} %get-tuple-element.97.gs_a), channel_id=1, source_target_pairs={{0,1},{1,0},{2,3},{3,2},{4,5},{5,4},{6,7},{7,6},{8,9},{9,8},{10,11... | collective-permute-start | bytes 7864328 | tf_op jit(solution)/shard_map/ppermute | solution.py:1611
  245.9 6.6 %collective-permute-start.2 = (bf16[1280,512]{1,0:T(8,128)(2,1)}, bf16[1280,512]{1,0:T(8,128)(2,1)S(1)}, u32[]{:S(2)}, u32[]{:S(2)}) collective-permute-start(bf16[1280,512]{1,0:T(8,128)(2,1)} %get-tuple-element.102), channel_id=1, source_target_pairs={{0,1},{1,0},{2,3},{3,2},{4,5},{5,4},{6,7},{7,6},{8,9},{9,8},{10,11... | collective-permute-start | bytes 3932168 | tf_op jit(solution)/shard_map/ppermute | solution.py:1611
  545.3 13.0 %copy-start.8 = (bf16[704,128]{1,0:T(8,128)(2,1)S(1)}, bf16[704,128]{1,0:T(8,128)(2,1)}, u32[]{:S(2)}) copy-start(bf16[704,128]{1,0:T(8,128)(2,1)} %param.49) | copy-start | bytes 540676
  545.3 13.0 %copy-start.11 = (f32[704,128]{1,0:T(8,128)S(1)}, f32[704,128]{1,0:T(8,128)}, u32[]{:S(2)}) copy-start(f32[704,128]{1,0:T(8,128)} %param.67) | copy-start | bytes 1081348
  545.3 13.0 %copy-start.12 = (f32[704,128]{1,0:T(8,128)S(1)}, f32[704,128]{1,0:T(8,128)}, u32[]{:S(2)}) copy-start(f32[704,128]{1,0:T(8,128)} %param.66) | copy-start | bytes 1081348
  546.6 12.8 %copy-start.15 = (f32[128,128]{1,0:T(8,128)S(1)}, f32[128,128]{1,0:T(8,128)}, u32[]{:S(2)}) copy-start(f32[128,128]{1,0:T(8,128)} %get-tuple-element.127) | copy-start | bytes 196612
  547.6 12.7 %copy-start.26 = (f32[2,1024]{1,0:T(2,128)S(1)}, f32[2,1024]{1,0:T(2,128)}, u32[]{:S(2)}) copy-start(f32[2,1024]{1,0:T(2,128)} %param.47) | copy-start | bytes 24580
  547.6 14.0 %copy-start.4 = (bf16[128,2,704]{0,2,1:T(8,128)(2,1)S(1)}, bf16[128,2,704]{0,2,1:T(8,128)(2,1)}, u32[]{:S(2)}) copy-start(bf16[128,2,704]{0,2,1:T(8,128)(2,1)} %param.48) | copy-start | bytes 1081348
  547.6 14.0 %copy-start.6 = (f32[128,2,704]{0,2,1:T(8,128)S(1)}, f32[128,2,704]{0,2,1:T(8,128)}, u32[]{:S(2)}) copy-start(f32[128,2,704]{0,2,1:T(8,128)} %param.65) | copy-start | bytes 2162692
  547.6 14.0 %copy-start.7 = (f32[128,2,704]{0,2,1:T(8,128)S(1)}, f32[128,2,704]{0,2,1:T(8,128)}, u32[]{:S(2)}) copy-start(f32[128,2,704]{0,2,1:T(8,128)} %param.64) | copy-start | bytes 2162692
  547.6 14.0 %copy-start.13 = (f32[704,128]{1,0:T(8,128)S(1)}, f32[704,128]{1,0:T(8,128)}, u32[]{:S(2)}) copy-start(f32[704,128]{1,0:T(8,128)} %get-tuple-element.129) | copy-start | bytes 1081348
  548.6 10.8 %copy-start.20 = (f32[1,256,128]{2,1,0:T(8,128)S(1)}, f32[1,256,128]{2,1,0:T(8,128)}, u32[]{:S(2)}) copy-start(f32[1,256,128]{2,1,0:T(8,128)} %param.61) | copy-start | bytes 393220
  548.7 10.8 %copy-start.21 = (f32[1,256,128]{2,1,0:T(8,128)S(1)}, f32[1,256,128]{2,1,0:T(8,128)}, u32[]{:S(2)}) copy-start(f32[1,256,128]{2,1,0:T(8,128)} %param.60) | copy-start | bytes 393220
  548.7 13.0 %copy-start.14 = (f32[704,128]{1,0:T(8,128)S(1)}, f32[704,128]{1,0:T(8,128)}, u32[]{:S(2)}) copy-start(f32[704,128]{1,0:T(8,128)} %get-tuple-element.130) | copy-start | bytes 1081348
  (17 other events, 114.6 us)

commit v5 on v4

--- a/solution.py
+++ b/solution.py
@@ -1527,14 +1527,15 @@
         weight_grad_into(pi_acc, grad_project, normed, part, part)
         weight_grad_into(pi_acc, grad_project, normed, 3 * part, part)
         chains[1].begin()
+        undeal.exchange()
         weight_grad_into(pi_acc, grad_project, normed, 2 * part * at_x, part)
         advance_small()
         for kz in [k % nz for k in range(1, nz + 1)]:
             chains[2].third(kz)
             chains[3].third(kz)
     else:
+        undeal.exchange()
         weight_grad_into(sums[0], grad_project, normed)
-    undeal.exchange()
     arrivals = [functools.partial(undeal.arrive, k) for k in range(1, nd)]
     if direct:
         for kz in [k % nz for k in range(1, nz + 1)]:

time: 573 us -> 570 us (level)
  no operation moved by 1% of the time
where the time goes in v5:
time: 570 us; the launch traced here: 561 us
  Pallas kernels  511 us (90%)
  other arithmetic  22.7 us (4%)
  local copies, waits for them, and re-layouts  17 us (3%)
    pallas_call x2, Pallas kernels, remote(): pl.pallas_call(kernel, in_specs=specs, out_specs=out_specs, out_shape=out...  254 us
    pallas_call x1, Pallas kernels, forward(): pl.pallas_call(kernel, in_specs=[SMEM, SMEM, ANY, ANY, ANY, ANY] + [VMEM]...  191 us
    pallas_call x1, Pallas kernels, on_device(): run(ffn_kernel, (tiles,), [SMEM] + [rows_spec(d)] * 4 + [whole_spec(1, d)...  34.9 us
    pallas_call x1, Pallas kernels, on_device(): run(functools.partial(out_back_kernel, tiles), (tiles,), [SMEM] + [rows_s...  18.9 us
    pallas_call x2, Pallas kernels, home(): pl.pallas_call(functools.partial(home_kernel, count), grid=(total // coun...  12.2 us
  transfers between devices with their start and end apart: 3, of which 2 were waited for; matrix products, arithmetic and copies ran while one was open for 3% of the time, Pallas kernels for 0%

profile of v5, /device:TPU:0, one launch (start us, length us, event | category | flops | bytes accessed | tf_op | source)
XLA Modules:
  0.0 560.9 jit_solution(11849269058811799092)
XLA Ops:
  2.1 2.9 collective-permute-start
  9.7 1.1 copy.91
  10.8 1.1 fusion.24
  11.9 1.4 fusion.26
  13.3 1.6 pad_maximum_fusion.2.refs_4_
  14.9 1.8 pad_maximum_fusion.1.refs_5_
  19.0 191.5 %forward.1 = (bf16[1280,1024]{1,0:T(8,128)(2,1)}, bf16[1280,1024]{1,0:T(8,128)(2,1)}, bf16[2080,1024]{1,0:T(8,128)(2,1)}, bf16[4224,1024]{1,0:T(8,128)(2,1)}, bf...) custom-call(s32[80]{0:T(128)} %pad_add_fusion.refs_0_, ...), custom_call_target="tpu_custom_call" | custom-call | flops 149999992832 | bytes 150000000 | tf_op jit(solution)/shard_map/forward/pallas_call | solution.py:959
  210.6 34.9 %ffn.1 = (f32[1280,1024]{1,0:T(8,128)}, bf16[1280,1024]{1,0:T(8,128)(2,1)}, bf16[1280,1408]{1,0:T(8,128)(2,1)}, bf16[1280,2816]{1,0:T(8,128)(2,1)}, bf16[1280,51...) custom-call(s32[28]{0:T(128)} %concatenate.47.ints, ...), custom_call_target="tpu_custom_call" | custom-call | flops 33999998976 | bytes 34000000 | tf_op jit(solution)/shard_map/ffn/pallas_call | solution.py:1695
  247.0 1.1 copy.93
  248.0 1.1 copy.92
  249.8 2.7 collective-permute-done.2.recv_out
  253.6 18.9 %out_back.1 = (f32[1280,1024]{1,0:T(8,128)}, bf16[1280,512]{1,0:T(8,128)(2,1)}, bf16[1280,512]{1,0:T(8,128)(2,1)}, f32[8,1024]{1,0:T(8,128)}, f32[8,256]{1,0:T(8...) custom-call(s32[28]{0:T(128)} %concatenate.47.ints, ...), custom_call_target="tpu_custom_call" | custom-call | flops 19000000512 | bytes 19000000 | tf_op jit(solution)/shard_map/out_back/pallas_call | solution.py:1714
  272.5 139.1 %back_all.1 = (f32[528,128]{1,0:T(8,128)}, f32[1280,512]{1,0:T(8,128)}, bf16[1280,512]{1,0:T(8,128)(2,1)}, f32[1280,256]{1,0:T(8,128)}, bf16[40,64,256]{2,1,0:T(...) custom-call(s32[40]{0:T(128)} %reshape.333.table, ...), custom_call_target="tpu_custom_call" | custom-call | flops 109999996928 | bytes 110000000 | tf_op jit(solution)/shard_map/back_all/pallas_call | solution.py:1573
  411.6 4.5 block_out_home.1
  416.1 114.9 %finish_all.1 = (bf16[40,64,1024]{2,1,0:T(8,128)(2,1)}, f32[16,1024]{1,0:T(8,128)}, f32[8,1024]{1,0:T(8,128)}, f32[16,256]{1,0:T(8,128)}, f32[8,256]{1,0:T(8,128...) custom-call(s32[40]{0:T(128)} %reshape.333.table, ...), custom_call_target="tpu_custom_call" | custom-call | flops 99999997952 | bytes 100000000 | tf_op jit(solution)/shard_map/finish_all/pallas_call | solution.py:1573
  531.1 7.7 %token_grad_home.1 = f32[2560,1024]{1,0:T(8,128)} custom-call(s32[40]{0:T(128)} %multiply_reduce_fusion.table, bf16[40,64,1024]{2,1,0:T(8,128)(2,1)} %get-tuple-element.122.src), custom_call_target="tpu_custom_call" | custom-call | flops 5000000000 | bytes 5000000 | tf_op jit(solution)/shard_map/token_grad_home/pallas_call | solution.py:151
  546.3 1.3 add_multiply_fusion.6
  547.6 1.5 maximum_bitcast_fusion
  550.1 1.5 add_multiply_fusion.5
  551.6 1.4 fusion.7
  553.0 1.3 add_multiply_fusion.7
  554.2 1.2 add_multiply_fusion.2
  556.2 1.4 add_multiply_fusion.4
  557.6 1.8 add_multiply_fusion
  (128 shorter events, 20.2 us)
Async XLA Ops:
  0.7 17.2 %copy-start.30 = (f32[1,128]{1,0:T(1,128)S(1)}, f32[1,128]{1,0:T(1,128)}, u32[]{:S(2)}) copy-start(f32[1,128]{1,0:T(1,128)} %param.44) | copy-start | bytes 1540
  2.1 15.8 %collective-permute-start = (f32[24,128]{1,0:T(8,128)S(1)}, f32[24,128]{1,0:T(8,128)S(1)}, u32[]{:S(2)}, u32[]{:S(2)}) collective-permute-start(f32[24,128]{1,0:T(8,128)S(1)} %pad_maximum_fusion.3), channel_id=1, source_target_pairs={{0,2},{2,0},{1,3},{3,1},{4,6},{6,4},{5,7},{7,5},{8,10},{10,8},{9,1... | collective-permute-start | bytes 36872 | tf_op jit(solution)/shard_map/ppermute | solution.py:1612
  7.6 11.5 %copy-start.36 = (s32[20]{0:T(128)}, s32[20]{0:T(128)S(1)}, u32[]{:S(2)}) copy-start(s32[20]{0:T(128)S(1)} %convert_subtract_fusion.refs_1_.keep) | copy-start | bytes 244
  210.5 35.5 %copy-start.35 = (s32[40]{0:T(128)S(1)}, s32[40]{0:T(128)}, u32[]{:S(2)}) copy-start(s32[40]{0:T(128)} %copy-done.34) | copy-start | bytes 484
  210.6 35.5 %copy-start.33 = (s32[40]{0:T(128)S(1)}, s32[40]{0:T(128)}, u32[]{:S(2)}) copy-start(s32[40]{0:T(128)} %copy-done.32) | copy-start | bytes 484
  210.6 36.4 %copy-start.9 = (f32[128,1,768]{2,1,0:T(1,128)S(1)}, f32[128,1,768]{2,1,0:T(1,128)}, u32[]{:S(2)}) copy-start(f32[128,1,768]{2,1,0:T(1,128)} %param.51) | copy-start | bytes 1179652
  210.6 37.4 %copy-start.10 = (f32[128,1,768]{2,1,0:T(1,128)S(1)}, f32[128,1,768]{2,1,0:T(1,128)}, u32[]{:S(2)}) copy-start(f32[128,1,768]{2,1,0:T(1,128)} %param.50) | copy-start | bytes 1179652
  210.6 38.5 %copy-start.23 = (s32[8,40]{1,0:T(8,128)S(1)}, s32[8,40]{1,0:T(8,128)}, u32[]{:S(2)}) copy-start(s32[8,40]{1,0:T(8,128)} %copy-done.22) | copy-start | bytes 3844
  210.6 38.5 %copy-start.25 = (s32[8,40]{1,0:T(8,128)S(1)}, s32[8,40]{1,0:T(8,128)}, u32[]{:S(2)}) copy-start(s32[8,40]{1,0:T(8,128)} %copy-done.24) | copy-start | bytes 3844
  210.6 38.5 %copy-start.28 = (s32[8,40]{1,0:T(8,128)S(1)}, s32[8,40]{1,0:T(8,128)}, u32[]{:S(2)}) copy-start(s32[8,40]{1,0:T(8,128)} %get-tuple-element.261) | copy-start | bytes 3844
  245.5 7.2 %collective-permute-start.1 = (bf16[1280,1024]{1,0:T(8,128)(2,1)}, bf16[1280,1024]{1,0:T(8,128)(2,1)}, u32[]{:S(2)}, u32[]{:S(2)}) collective-permute-start(bf16[1280,1024]{1,0:T(8,128)(2,1)} %get-tuple-element.97.gs_a), channel_id=1, source_target_pairs={{0,1},{1,0},{2,3},{3,2},{4,5},{5,4},{6,7},{7,6},{8,9},{9,8},{10,11... | collective-permute-start | bytes 7864328 | tf_op jit(solution)/shard_map/ppermute | solution.py:1612
  245.9 6.6 %collective-permute-start.2 = (bf16[1280,512]{1,0:T(8,128)(2,1)}, bf16[1280,512]{1,0:T(8,128)(2,1)S(1)}, u32[]{:S(2)}, u32[]{:S(2)}) collective-permute-start(bf16[1280,512]{1,0:T(8,128)(2,1)} %get-tuple-element.102), channel_id=1, source_target_pairs={{0,1},{1,0},{2,3},{3,2},{4,5},{5,4},{6,7},{7,6},{8,9},{9,8},{10,11... | collective-permute-start | bytes 3932168 | tf_op jit(solution)/shard_map/ppermute | solution.py:1612
  541.2 13.0 %copy-start.8 = (bf16[704,128]{1,0:T(8,128)(2,1)S(1)}, bf16[704,128]{1,0:T(8,128)(2,1)}, u32[]{:S(2)}) copy-start(bf16[704,128]{1,0:T(8,128)(2,1)} %param.49) | copy-start | bytes 540676
  541.2 13.0 %copy-start.11 = (f32[704,128]{1,0:T(8,128)S(1)}, f32[704,128]{1,0:T(8,128)}, u32[]{:S(2)}) copy-start(f32[704,128]{1,0:T(8,128)} %param.67) | copy-start | bytes 1081348
  541.2 13.0 %copy-start.12 = (f32[704,128]{1,0:T(8,128)S(1)}, f32[704,128]{1,0:T(8,128)}, u32[]{:S(2)}) copy-start(f32[704,128]{1,0:T(8,128)} %param.66) | copy-start | bytes 1081348
  542.6 12.8 %copy-start.15 = (f32[128,128]{1,0:T(8,128)S(1)}, f32[128,128]{1,0:T(8,128)}, u32[]{:S(2)}) copy-start(f32[128,128]{1,0:T(8,128)} %get-tuple-element.127) | copy-start | bytes 196612
  543.6 12.7 %copy-start.26 = (f32[2,1024]{1,0:T(2,128)S(1)}, f32[2,1024]{1,0:T(2,128)}, u32[]{:S(2)}) copy-start(f32[2,1024]{1,0:T(2,128)} %param.47) | copy-start | bytes 24580
  543.6 14.0 %copy-start.4 = (bf16[128,2,704]{0,2,1:T(8,128)(2,1)S(1)}, bf16[128,2,704]{0,2,1:T(8,128)(2,1)}, u32[]{:S(2)}) copy-start(bf16[128,2,704]{0,2,1:T(8,128)(2,1)} %param.48) | copy-start | bytes 1081348
  543.6 14.0 %copy-start.6 = (f32[128,2,704]{0,2,1:T(8,128)S(1)}, f32[128,2,704]{0,2,1:T(8,128)}, u32[]{:S(2)}) copy-start(f32[128,2,704]{0,2,1:T(8,128)} %param.65) | copy-start | bytes 2162692
  543.6 14.0 %copy-start.7 = (f32[128,2,704]{0,2,1:T(8,128)S(1)}, f32[128,2,704]{0,2,1:T(8,128)}, u32[]{:S(2)}) copy-start(f32[128,2,704]{0,2,1:T(8,128)} %param.64) | copy-start | bytes 2162692
  543.6 14.0 %copy-start.13 = (f32[704,128]{1,0:T(8,128)S(1)}, f32[704,128]{1,0:T(8,128)}, u32[]{:S(2)}) copy-start(f32[704,128]{1,0:T(8,128)} %get-tuple-element.129) | copy-start | bytes 1081348
  544.6 10.8 %copy-start.20 = (f32[1,256,128]{2,1,0:T(8,128)S(1)}, f32[1,256,128]{2,1,0:T(8,128)}, u32[]{:S(2)}) copy-start(f32[1,256,128]{2,1,0:T(8,128)} %param.61) | copy-start | bytes 393220
  544.6 10.8 %copy-start.21 = (f32[1,256,128]{2,1,0:T(8,128)S(1)}, f32[1,256,128]{2,1,0:T(8,128)}, u32[]{:S(2)}) copy-start(f32[1,256,128]{2,1,0:T(8,128)} %param.60) | copy-start | bytes 393220
  544.6 13.0 %copy-start.14 = (f32[704,128]{1,0:T(8,128)S(1)}, f32[704,128]{1,0:T(8,128)}, u32[]{:S(2)}) copy-start(f32[704,128]{1,0:T(8,128)} %get-tuple-element.130) | copy-start | bytes 1081348
  (17 other events, 114.6 us)
